TPU v7x, 256 devices: a whole 4x4x8 slice. The times are simulated.
256 devices in a mesh: grp: 8 (over x, core), usr: 32 (over y, z).
Axes of the slice: x: 4, y: 4, z: 8, core: 2. Of those that a mesh axis runs over, the one named last changes fastest.
Arguments:
- candidates: bfloat16 [262144, 1024], P(('grp', 'usr')), may hold values from -6 to 6
- hist_kv: bfloat16 [256, 384, 2048], P(('grp', 'usr')), may hold values from -6 to 6
- hist_len: int32 [256], P(('grp', 'usr')), may hold values from 1 to 384, as said below
- block_mask: int32 [256, 3], P(('grp', 'usr')), may hold values 0 or 1
- tile_user: int32 [4096, 1], P(('grp', 'usr')), may hold values from 0 to 31; in each aligned block of 16 rows (0 to 15, 16 to 31, ...) no two rows name the same one
- tile_count: int32 [4096], P(('grp', 'usr')), may hold values from 1 to 64, as said below
- weight_in: bfloat16 [1024, 4096], P(None, ('grp', 'usr')), may hold values from -0.1875 to 0.1875
- weight_out: bfloat16 [1024, 1024], P(('grp', 'usr')), may hold values from -0.1875 to 0.1875
Outputs:
- scored: bfloat16 [262144, 1024], P(('grp', 'usr'))
Inputs may be any that keep to these rules, and one draw needn't show every extreme that they name: `hist_len`: some user's history has exactly 384 items. `tile_count`: the first tile of every device is full. A tile's live candidates take its first slots. `tile_user`: the tiles of one device belong to distinct users of its group.
All inputs are finite; a program needn't handle non-finite values. No bound on the sum of `block_mask` on one device may be relied on, other than what follows from the above.
Results may differ from a plain program's by a relative error of at most 0.0057.
Values may be sent and summed in bfloat16 or wider, within the bound.
No kernel may reach another device: no remote copies, remote signals or barrier semaphores. Data moves between devices by JAX's collectives and lax.ppermute only.
A program may use at most 128 MiB of HBM per device.

v0:
```python
import math

import jax
import jax.numpy as jnp
from jax import lax
from jax.sharding import PartitionSpec as P

HEADS = 8
BLK = 128


def norm_rows(values_in):
    centred = values_in - jnp.mean(values_in, axis=-1, keepdims=True)
    variance = jnp.mean(centred * centred, axis=-1, keepdims=True)
    return centred * lax.rsqrt(variance + 1e-05)


def attend_rows(query_rows, hist_keys, hist_values, live_items, score_scale):
    row_total = query_rows.shape[0]
    model_width = query_rows.shape[1]
    head_dim = model_width // HEADS
    query_heads = query_rows.reshape(row_total, HEADS, head_dim)
    key_heads = hist_keys.reshape(-1, HEADS, head_dim)
    value_heads = hist_values.reshape(-1, HEADS, head_dim)
    scores = (
        jnp.einsum("nhd,lhd->hnl", query_heads, key_heads, preferred_element_type=jnp.float32)
        * score_scale
    )
    weights = (jax.nn.silu(scores) * live_items).astype(jnp.bfloat16)
    attended = jnp.einsum("hnl,lhd->nhd", weights, value_heads, preferred_element_type=jnp.float32)
    return attended.reshape(row_total, model_width)


def own_term(queries, self_keys, self_values, score_scale):
    row_total = queries.shape[0]
    products = (queries.astype(jnp.float32) * self_keys.astype(jnp.float32)).reshape(
        row_total, HEADS, -1
    )
    strength = jax.nn.silu(jnp.sum(products, axis=2) * score_scale)
    value_heads = self_values.astype(jnp.float32).reshape(row_total, HEADS, -1)
    return (strength[:, :, None] * value_heads).reshape(row_total, -1)


def holder_attend(incoming, hist_keys, hist_values, live_items, score_scale):
    slot_total, item_count, model_width = incoming.shape
    per_group = math.gcd(slot_total, max(1, 512 // item_count))
    group_total = slot_total // per_group

    def answer_rows(row_block):
        return attend_rows(row_block, hist_keys, hist_values, live_items, score_scale).astype(
            jnp.bfloat16
        )

    row_blocks = incoming.reshape(group_total, per_group * item_count, model_width)
    answered = lax.map(answer_rows, row_blocks)
    return answered.reshape(slot_total, item_count, model_width)


def shards(candidates, hist_kv, hist_len, block_mask, tile_user, tile_count, weight_in, weight_out):
    row_total, model_width = candidates.shape
    tiles_here = tile_user.shape[0]
    tile_rows = row_total // tiles_here
    score_scale = (model_width // HEADS) ** (-0.5)
    holders = lax.axis_size("usr")
    normed = norm_rows(candidates.astype(jnp.float32)).astype(jnp.bfloat16)
    projected = jax.nn.silu(
        jnp.dot(
            normed,
            lax.all_gather(weight_in, ("grp", "usr"), axis=1, tiled=True),
            preferred_element_type=jnp.float32,
        )
    ).astype(jnp.bfloat16)
    queries = projected[:, :model_width]
    self_keys = projected[:, model_width : 2 * model_width]
    self_values = projected[:, 2 * model_width : 3 * model_width]
    gate_units = projected[:, 3 * model_width :]
    own_part = own_term(queries, self_keys, self_values, score_scale)
    tile_dest = tile_user[:, 0]
    outgoing = jnp.zeros((holders, tile_rows, model_width), jnp.bfloat16)
    outgoing = outgoing.at[tile_dest].set(queries.reshape(tiles_here, tile_rows, model_width))
    hist_keys = hist_kv[0, :, :model_width]
    hist_values = hist_kv[0, :, model_width:]
    positions = jnp.arange(hist_kv.shape[1], dtype=jnp.int32)
    live_items = ((positions < hist_len[0]) & (jnp.repeat(block_mask[0], BLK) > 0)).astype(
        jnp.float32
    )
    incoming = lax.all_to_all(outgoing, "usr", split_axis=0, concat_axis=0, tiled=True)
    returned = lax.all_to_all(
        holder_attend(incoming, hist_keys, hist_values, live_items, score_scale),
        "usr",
        split_axis=0,
        concat_axis=0,
        tiled=True,
    )
    history = returned[tile_dest].reshape(row_total, model_width)
    combined = history.astype(jnp.float32) + own_part
    gated_rows = (norm_rows(combined) * gate_units.astype(jnp.float32)).astype(jnp.bfloat16)
    mixed_rows = jnp.dot(
        gated_rows,
        lax.all_gather(weight_out, ("grp", "usr"), axis=0, tiled=True),
        preferred_element_type=jnp.float32,
    )
    mixed_rows = mixed_rows + candidates.astype(jnp.float32)
    live_rows = (jnp.arange(tile_rows, dtype=jnp.int32)[None, :] < tile_count[:, None]).reshape(-1)
    return jnp.where(live_rows[:, None], mixed_rows, 0.0).astype(jnp.bfloat16)


def solution(mesh):
    in_specs = (
        P(("grp", "usr"), None),
        P(("grp", "usr"), None, None),
        P(("grp", "usr")),
        P(("grp", "usr"), None),
        P(("grp", "usr"), None),
        P(("grp", "usr")),
        P(None, ("grp", "usr")),
        P(("grp", "usr"), None),
    )
    out_specs = P(("grp", "usr"), None)
    return jax.shard_map(shards, mesh=mesh, in_specs=in_specs, out_specs=out_specs, check_vma=False)
```

profile of v0, /device:TPU:1, one launch (start us, length us, event | category | flops | bytes accessed | tf_op | source)
XLA Modules:
  0.0 472.6 jit_solution(16405378057129019806)
XLA Ops:
  7.3 1.9 convert_reduce_fusion
  9.9 2.3 fusion.14
  12.1 121.5 %all-gather.4.cloned.1.call-done = bf16[1024,4096]{0,1:T(8,128)(2,1)} async-done(((bf16[1024,16]{0,1:T(8,128)(2,1)}), bf16[1024,4096]{0,1:T(8,128)(2,1)}) %all-gather.4.cloned.1.call-update) | async-done | bytes 8388624 | tf_op jit(solution)/shard_map/all_gather | solution.py:69
  133.6 15.8 %multiply_convert_fusion.4 = bf16[1024,4096]{1,0:T(8,128)(2,1)} fusion(bf16[1024,4096]{0,1:T(8,128)(2,1)} %all-gather.4.cloned.1.call-done, bf16[1024,1024]{1,0:T(8,128)(2,1)S(1)} %copy-done, f32[1024]{0:T(1024)S(1)} %add_rsqrt_fusion.1, f32[1024]{0:T(1024)S(1)} %broadcast_multiply_fusion.1), kind=kOutput, calls=%fused_computation.15 | convolution fusion | flops 8615100416 | bytes 18882560 | tf_op jit(solution)/shard_map/dot_general | solution.py:67
  149.4 1.8 slice.26
  151.2 2.5 broadcast_in_dim.19
  153.7 5.2 %scatter_fusion = bf16[32,64,1024]{2,1,0:T(8,128)(2,1)} fusion(bf16[32,64,1024]{2,1,0:T(8,128)(2,1)} %broadcast_in_dim.19, s32[16]{0:T(128)S(1)} %fusion.29, bf16[16,64,1024]{2,1,0:T(8,128)(2,1)S(1)} %bitcast.58), kind=kCustom, calls=%fused_computation.1 | custom fusion | bytes 6291520 | tf_op jit(solution)/shard_map/scatter | solution.py:80
  158.9 6.5 %all-to-all-start = ((bf16[32,64,1024]{2,1,0:T(8,128)(2,1)}), bf16[32,64,1024]{2,1,0:T(8,128)(2,1)}, u32[]{:S(2)}, u32[]{:S(2)}) async-start(bf16[32,64,1024]{2,1,0:T(8,128)(2,1)} %scatter_fusion), calls=%async_computation | async-start | bytes 8388608 | tf_op jit(solution)/shard_map/all_to_all | solution.py:87
  165.5 1.2 copy.42
  166.7 93.0 %all-to-all-done = bf16[32,64,1024]{2,1,0:T(8,128)(2,1)} async-done(((bf16[32,64,1024]{2,1,0:T(8,128)(2,1)}), bf16[32,64,1024]{2,1,0:T(8,128)(2,1)}, u32[]{:S(2)}, u32[]{:S(2)}) %all-to-all-start) | async-done | bytes 4194336 | tf_op jit(solution)/shard_map/all_to_all | solution.py:87
  259.7 38.3 %while.11 = (s32[]{:T(128)}, bf16[4,512,1024]{2,1,0:T(8,128)(2,1)}, bf16[4,512,1024]{2,1,0:T(8,128)(2,1)}, bf16[1,384,1024]{2,1,0:T(8,128)(2,1)S(1)}, bf16[1,384...) while((s32[]{:T(128)}, bf16[4,512,1024]{2,1,0:T(8,128)(2,1)}, ...), condition=%wide.region_4.5_spmd.clone, body=%wide.region_3.4_spmd.clone.sunk | while | flops 816841856 | bytes 13635168 | solution.py:55
  259.7 1.3 constant_dynamic-slice_fusion.2
  262.3 1.1 copy.57
  263.4 4.3 fusion.46
  268.2 1.1 constant_dynamic-update-slice_fusion.2
  269.3 1.3 constant_dynamic-slice_fusion.2
  273.0 4.3 fusion.46
  278.9 1.3 constant_dynamic-slice_fusion.2
  281.4 1.1 copy.57
  282.5 4.3 fusion.46
  288.4 1.3 constant_dynamic-slice_fusion.2
  292.1 4.3 fusion.46
  298.0 7.8 %all-to-all-start.1 = ((bf16[32,64,1024]{2,1,0:T(8,128)(2,1)}), bf16[32,64,1024]{2,1,0:T(8,128)(2,1)}, u32[]{:S(2)}, u32[]{:S(2)}) async-start(bf16[32,64,1024]{2,1,0:T(8,128)(2,1)} %bitcast.59), calls=%async_computation.1 | async-start | bytes 8388608 | tf_op jit(solution)/shard_map/all_to_all | solution.py:88
  306.7 131.0 %all-gather.6.cloned.1.call-done = bf16[256,4,1024]{2,1,0:T(4,128)(2,1)} async-done(((bf16[1,4,1024]{2,1,0:T(4,128)(2,1)}), bf16[256,4,1024]{2,1,0:T(4,128)(2,1)}) %all-gather.6.cloned.1.call-update) | async-done | bytes 2097168 | tf_op jit(solution)/shard_map/all_gather | solution.py:100
  437.8 3.9 reshape.109
  441.7 3.1 multiply_bitcast_fusion
  444.8 2.9 copy.44
  447.8 3.4 reduce_sum.47
  451.6 2.9 gather_fusion
  454.4 1.1 mul.84
  455.6 2.5 fusion.30
  460.3 5.5 %fusion.17 = bf16[1024,1024]{1,0:T(8,128)(2,1)} fusion(bf16[1024,1024]{1,0:T(8,128)(2,1)S(1)} %copy-done.1, pred[1024]{0:T(1024)(128)(4,1)S(1)} %lt.37, bf16[1024,1024]{1,0:T(8,128)(2,1)S(1)} %copy-done.2, f32[1024,1024]{1,0:T(8,128)S(1)} %get-tuple-element.99, bf16[1024,4096]{1,0:T(8,128)(2,1)} %multiply_convert_fusion.4, f32[1024]{0:T(1024)S(1)} %add_rsqrt_fusion, ...), kind=kOutput, calls=%fused_computation.24 | convolution fusion | flops 2156920832 | bytes 12592128 | tf_op jit(solution)/shard_map/dot_general | solution.py:98
  (49 shorter events, 17.6 us)
Async XLA Ops:
  6.5 127.1 %copy-start = (bf16[1024,1024]{1,0:T(8,128)(2,1)S(1)}, bf16[1024,1024]{1,0:T(8,128)(2,1)}, u32[]{:S(2)}) copy-start(bf16[1024,1024]{1,0:T(8,128)(2,1)} %param.10) | copy-start | bytes 6291460
  6.5 127.1 %all-gather.4.cloned.1.call-start = ((), (), s32[]{:S(2)}) async-start(), calls=%async_computation.2 | async-start | bytes 8421376 | tf_op jit(solution)/shard_map/all_gather | solution.py:69
  158.9 6.5 %copy-start.3 = (bf16[1,384,2048]{2,1,0:T(8,128)(2,1)S(1)}, bf16[1,384,2048]{2,1,0:T(8,128)(2,1)}, u32[]{:S(2)}) copy-start(bf16[1,384,2048]{2,1,0:T(8,128)(2,1)} %param.11) | copy-start | bytes 4718596
  158.9 100.9 %all-to-all-start = ((bf16[32,64,1024]{2,1,0:T(8,128)(2,1)}), bf16[32,64,1024]{2,1,0:T(8,128)(2,1)}, u32[]{:S(2)}, u32[]{:S(2)}) async-start(bf16[32,64,1024]{2,1,0:T(8,128)(2,1)} %scatter_fusion), calls=%async_computation | async-start | bytes 8388608 | tf_op jit(solution)/shard_map/all_to_all | solution.py:87
  165.4 1.3 copy-start.5
  298.0 8.6 %copy-start.4 = (s32[16]{0:T(128)S(1)}, s32[16]{0:T(128)}, u32[]{:S(2)}) copy-start(s32[16]{0:T(128)} %param.15) | copy-start | bytes 196
  298.0 153.6 %all-to-all-start.1 = ((bf16[32,64,1024]{2,1,0:T(8,128)(2,1)}), bf16[32,64,1024]{2,1,0:T(8,128)(2,1)}, u32[]{:S(2)}, u32[]{:S(2)}) async-start(bf16[32,64,1024]{2,1,0:T(8,128)(2,1)} %bitcast.59), calls=%async_computation.1 | async-start | bytes 8388608 | tf_op jit(solution)/shard_map/all_to_all | solution.py:88
  305.8 132.0 %all-gather.6.cloned.1.call-start = ((), (), s32[]{:S(2)}) async-start(), calls=%async_computation.3 | async-start | bytes 2105344 | tf_op jit(solution)/shard_map/all_gather | solution.py:100
  458.1 1.6 copy-start.1
  458.1 2.2 copy-start.2
Sparse Core Ops, SparseCore 0:
  11.1 122.4 all-gather.3
  310.4 127.3 all-gather.5
where the time goes:
time: 474 us; the launch traced here: 473 us
  waiting for transfers between devices  347 us (73%)
  local copies, waits for them, and re-layouts  41.8 us (9%)
  matrix products  38.4 us (8%)
  other arithmetic  17.4 us (4%)
  starting transfers between devices  14.5 us (3%)
  between operations  13.6 us (3%)
    all_gather x1, waiting for transfers between devices, shards(): lax.all_gather(weight_out, ('grp', 'usr'), axis=0, tiled=True)  131 us
    all_gather x1, waiting for transfers between devices, shards(): lax.all_gather(weight_in, ('grp', 'usr'), axis=1, tiled=True)  121 us
    all_to_all x1, waiting for transfers between devices, shards(): lax.all_to_all(outgoing, 'usr', split_axis=0, concat_axis=0, tiled=True)  93 us
    dot_general x4, matrix products, attend_rows(): jnp.einsum('hnl,lhd->nhd', weights, value_heads, preferred_element_type=j...  17.1 us
    dot_general x1, matrix products, shards(): jnp.dot(normed, lax.all_gather(weight_in, ('grp', 'usr'), axis=1, tiled=T...  15.8 us
    unnamed x15, local copies, waits for them, and re-layouts  9.68 us
  transfers between devices with their start and end apart: 4, of which 3 were waited for; matrix products, arithmetic and copies ran while one was open for 4% of the time, Pallas kernels for 0%

commit v1 on v0

v1 whole, which is shorter than its diff:
```python
import functools

import jax
import jax.numpy as jnp
from jax import lax
from jax.experimental import pallas as pl
from jax.experimental.pallas import tpu as pltpu
from jax.sharding import Mesh
from jax.sharding import PartitionSpec as P

HEADS = 8
HEAD = 128
BLK = 128
HIST = 384
TILE = 64
ROWS = 256
CHUNKS = 2
META = 4
NX, NC, NY, NZ = 4, 2, 4, 8
BF = jnp.bfloat16
F32 = jnp.float32
VMEM_LIMIT = 56 * 1024 * 1024
NT = (((1,), (1,)), ((), ()))


def half_silu(a):
    return a + a * jnp.tanh(a)


def params():
    return pltpu.CompilerParams(vmem_limit_bytes=VMEM_LIMIT)


def ring(size, step):
    return [(i, (i + step) % size) for i in range(size)]


def prep_kernel(len_ref, mask_ref, key_in, value_in, key_out, value_out):
    place = lax.broadcasted_iota(jnp.int32, (HIST, HEAD), 0)
    kept = jnp.where(
        place < BLK, mask_ref[0, 0], jnp.where(place < 2 * BLK, mask_ref[0, 1], mask_ref[0, 2])
    )
    live = (place < len_ref[0]) & (kept > 0)
    key_out[0] = key_in[...]
    value_out[0] = jnp.where(live, value_in[...].astype(F32), 0.0).astype(BF)


def prep(hist, hist_len, block_mask):
    shape = jax.ShapeDtypeStruct((HEADS, HIST, HEAD), BF)
    smem = pl.BlockSpec(memory_space=pltpu.SMEM)
    return pl.pallas_call(
        prep_kernel,
        grid=(HEADS,),
        in_specs=[
            smem,
            smem,
            pl.BlockSpec((HIST, HEAD), lambda h: (0, h)),
            pl.BlockSpec((HIST, HEAD), lambda h: (0, HEADS + h)),
        ],
        out_specs=[pl.BlockSpec((1, HIST, HEAD), lambda h: (h, 0, 0))] * 2,
        out_shape=[shape, shape],
        compiler_params=params(),
        name="prep",
    )(hist_len, block_mask, hist, hist)


def norm_kernel(rows_ref, out_ref):
    values = rows_ref[...].astype(F32)
    centred = values - jnp.mean(values, axis=-1, keepdims=True)
    variance = jnp.mean(centred * centred, axis=-1, keepdims=True)
    out_ref[...] = (centred * lax.rsqrt(variance + 1e-05)).astype(BF)


def norm(rows):
    total, width = rows.shape
    return pl.pallas_call(
        norm_kernel,
        grid=(total // ROWS,),
        in_specs=[pl.BlockSpec((ROWS, width), lambda i: (i, 0))],
        out_specs=pl.BlockSpec((ROWS, width), lambda i: (i, 0)),
        out_shape=jax.ShapeDtypeStruct((total, width), BF),
        compiler_params=params(),
        name="norm",
    )(rows)


def query_kernel(slot_ref, rows_ref, mine_ref, other_ref, out_ref):
    rows = rows_ref[...]
    for part, weights in enumerate((mine_ref, other_ref)):
        for pair in range(2):
            block = weights[pl.ds(pair * 2 * HEAD, 2 * HEAD), :]
            made = lax.dot_general(rows, block, NT, preferred_element_type=F32)
            made = half_silu(made * 0.5).astype(BF)
            for lane in range(2):
                slot = slot_ref[part * 4 + pair * 2 + lane]
                out_ref[slot] = made[:, lane * HEAD : (lane + 1) * HEAD]


def query(slots, normed, mine, other, chunk):
    width = normed.shape[1]
    rows = normed.shape[0] // CHUNKS
    steps = rows // ROWS
    half = pl.BlockSpec((4 * HEAD, width), lambda i: (0, 0))
    return pl.pallas_call(
        query_kernel,
        grid=(steps,),
        in_specs=[
            pl.BlockSpec(memory_space=pltpu.SMEM),
            pl.BlockSpec((ROWS, width), lambda i: (chunk * steps + i, 0)),
            half,
            half,
        ],
        out_specs=pl.BlockSpec((HEADS, ROWS, HEAD), lambda i: (0, i, 0)),
        out_shape=jax.ShapeDtypeStruct((HEADS, rows, HEAD), BF),
        compiler_params=params(),
        name="query",
    )(slots, normed, mine, other)


def attend_kernel(scale, user_ref, query_ref, key_ref, value_ref, out_ref):
    source = pl.program_id(0)
    tiles = query_ref.shape[1] // TILE
    for t in range(tiles):
        user = user_ref[source, t]
        scores = lax.dot_general(
            query_ref[0, pl.ds(t * TILE, TILE), :], key_ref[user], NT, preferred_element_type=F32
        )
        weights = half_silu(scores * (0.5 * scale)).astype(BF)
        out_ref[0, pl.ds(t * TILE, TILE), :] = jnp.dot(
            weights, value_ref[user], preferred_element_type=F32
        ).astype(BF)


def attend(users, queries, keys, values, scale):
    count, rows, _ = queries.shape
    whole = pl.BlockSpec(keys.shape, lambda i: (0, 0, 0))
    return pl.pallas_call(
        functools.partial(attend_kernel, scale),
        grid=(count,),
        in_specs=[
            pl.BlockSpec(memory_space=pltpu.SMEM),
            pl.BlockSpec((1, rows, HEAD), lambda i: (i, 0, 0)),
            whole,
            whole,
        ],
        out_specs=pl.BlockSpec((1, rows, HEAD), lambda i: (i, 0, 0)),
        out_shape=jax.ShapeDtypeStruct(queries.shape, BF),
        compiler_params=params(),
        name="attend",
    )(users, queries, keys, values)


def own_kernel(scale, rows_ref, query_ref, key_w, value_w, gate_w, own_ref, gate_ref):
    rows = rows_ref[...]
    width = rows.shape[1]

    def project(weights, start):
        block = weights[pl.ds(start // HEAD, 2)].reshape(2 * HEAD, width)
        made = lax.dot_general(rows, block, NT, preferred_element_type=F32)
        return half_silu(made * 0.5).astype(BF)

    for start in range(0, width, 2 * HEAD):
        self_keys = project(key_w, start).astype(F32)
        self_values = project(value_w, start).astype(F32)
        gate_ref[:, start : start + 2 * HEAD] = project(gate_w, start)
        for lane in range(2):
            cut = slice(lane * HEAD, (lane + 1) * HEAD)
            head = start // HEAD + lane
            products = query_ref[head].astype(F32) * self_keys[:, cut]
            strength = half_silu(jnp.sum(products, axis=1, keepdims=True) * (0.5 * scale))
            own_ref[:, head * HEAD : (head + 1) * HEAD] = strength * self_values[:, cut]


def own(normed, queries, gathered, chunk, scale):
    width = normed.shape[1]
    rows = queries.shape[1]
    steps = rows // ROWS

    def weights(place):
        return pl.BlockSpec((HEADS, HEAD, width), lambda i: (place, 0, 0))

    return pl.pallas_call(
        functools.partial(own_kernel, scale),
        grid=(steps,),
        in_specs=[
            pl.BlockSpec((ROWS, width), lambda i: (chunk * steps + i, 0)),
            pl.BlockSpec((HEADS, ROWS, HEAD), lambda i: (0, i, 0)),
            weights(1),
            weights(2),
            weights(3),
        ],
        out_specs=[pl.BlockSpec((ROWS, width), lambda i: (i, 0))] * 2,
        out_shape=[
            jax.ShapeDtypeStruct((rows, width), F32),
            jax.ShapeDtypeStruct((rows, width), BF),
        ],
        compiler_params=params(),
        name="own",
    )(normed, queries, gathered, gathered, gathered)


def finish_kernel(chunk, count_ref, hist_ref, own_ref, gate_ref, out_w, rows_ref, *rest):
    out_ref = rest[-1]
    width = rows_ref.shape[1]
    history = jnp.concatenate([hist_ref[h].astype(F32) for h in range(HEADS)], axis=1)
    combined = history + own_ref[...]
    centred = combined - jnp.mean(combined, axis=-1, keepdims=True)
    variance = jnp.mean(centred * centred, axis=-1, keepdims=True)
    gated = (centred * lax.rsqrt(variance + 1e-05) * gate_ref[...].astype(F32)).astype(BF)
    weights = out_w[...].reshape(width, width)
    mixed = jnp.dot(gated, weights, preferred_element_type=F32) + rows_ref[...].astype(F32)
    first = (chunk * pl.num_programs(0) + pl.program_id(0)) * (ROWS // TILE)
    slot = lax.broadcasted_iota(jnp.int32, (TILE, width), 0)
    for t in range(ROWS // TILE):
        cut = slice(t * TILE, (t + 1) * TILE)
        out_ref[cut, :] = jnp.where(slot < count_ref[first + t], mixed[cut, :], 0.0).astype(BF)


def finish(counts, history, own_part, gate, gathered, rows, chunk, before):
    total, width = rows.shape
    steps = total // CHUNKS // ROWS
    place = pl.BlockSpec((ROWS, width), lambda i: (chunk * steps + i, 0))
    local = pl.BlockSpec((ROWS, width), lambda i: (i, 0))
    shares = gathered.shape[0]
    out_rows = width // shares
    specs = [
        pl.BlockSpec(memory_space=pltpu.SMEM),
        pl.BlockSpec((HEADS, ROWS, HEAD), lambda i: (0, i, 0)),
        local,
        local,
        pl.BlockSpec((shares, out_rows, width), lambda i: (0, HEAD // out_rows, 0)),
        place,
    ]
    given = [counts, history, own_part, gate, gathered, rows]
    aliases = {}
    if before is not None:
        specs.append(pl.BlockSpec(memory_space=pl.ANY))
        given.append(before)
        aliases = {len(given) - 1: 0}
    return pl.pallas_call(
        functools.partial(finish_kernel, chunk),
        grid=(steps,),
        in_specs=specs,
        out_specs=place,
        out_shape=jax.ShapeDtypeStruct((total, width), BF),
        input_output_aliases=aliases,
        compiler_params=params(),
        name="finish",
    )(*given)


def swap_z(values):
    return lax.all_to_all(values, "z", split_axis=0, concat_axis=0, tiled=True)


def shards(candidates, hist_kv, hist_len, block_mask, tile_user, tile_count, weight_in, weight_out):
    width = candidates.shape[1]
    tiles = tile_user.shape[0]
    scale = HEAD ** (-0.5)
    at_x, at_core, at_y = lax.axis_index("x"), lax.axis_index("core"), lax.axis_index("y")

    columns = weight_in.T
    share = columns.shape[0]
    sent = [lax.ppermute(columns, "x", [(0, k)]) for k in range(1, NX)]
    query_part = jnp.where(at_x == 0, columns, sent[0] + sent[1] + sent[2])
    query_z = swap_z(jnp.broadcast_to(query_part, (NZ, share, width)))

    meta = jnp.zeros((META, width), BF).at[0, :tiles].set(tile_user[:, 0].astype(BF))
    packed = jnp.concatenate([columns, weight_out, meta], axis=0)
    packed, query_part = lax.optimization_barrier((packed, query_part))
    rest_z = swap_z(jnp.broadcast_to(packed, (NZ,) + packed.shape))
    users = rest_z[:, share + weight_out.shape[0], :tiles].astype(jnp.int32)

    keys, values = prep(hist_kv[0], hist_len, block_mask)
    keys = swap_z(keys)
    values = swap_z(values)

    query_z = query_z.reshape(NZ * share, width)
    query_y = [query_z]
    for step in range(1, NY):
        query_y.append(lax.ppermute(query_z, "y", ring(NY, step)))
    mine = jnp.concatenate(query_y, axis=0)
    other = lax.ppermute(mine, "core", ring(NC, 1))
    at = (at_y - jnp.arange(NY, dtype=jnp.int32)) % NY
    slots = jnp.concatenate([at_core * NY + at, (1 - at_core) * NY + at]).astype(jnp.int32)

    in_rows = rest_z[:, :share].reshape(NZ * share, width)
    out_rows = rest_z[:, share : share + weight_out.shape[0]].reshape(-1, width)
    gathered = lax.all_gather(jnp.concatenate([in_rows, out_rows], axis=0), ("x", "core", "y"))

    key_up = lax.ppermute(keys, "y", ring(NY, 1))
    key_down = lax.ppermute(keys, "y", ring(NY, NY - 1))
    value_up = lax.ppermute(values, "y", ring(NY, 1))
    value_down = lax.ppermute(values, "y", ring(NY, NY - 1))
    key_far = lax.ppermute(key_up, "y", ring(NY, 1))
    value_far = lax.ppermute(value_down, "y", ring(NY, NY - 1))
    all_keys = jnp.concatenate([keys, key_up, key_far, key_down], axis=0)
    all_values = jnp.concatenate([values, value_up, value_far, value_down], axis=0)
    users = ((at_y - users // NZ) % NY) * NZ + users % NZ

    normed = norm(candidates)
    queries = [query(slots, normed, mine, other, c) for c in range(CHUNKS)]
    arrived = [swap_z(q) for q in queries]
    per = tiles // CHUNKS
    history = []
    for c in range(CHUNKS):
        part = users[:, c * per : (c + 1) * per]
        history.append(swap_z(attend(part, arrived[c], all_keys, all_values, scale)))
    out = None
    for c in range(CHUNKS):
        own_part, gate = own(normed, queries[c], gathered, c, scale)
        out = finish(tile_count, history[c], own_part, gate, gathered, candidates, c, out)
    return out


def solution(mesh):
    fine = Mesh(mesh.devices.reshape(NX, NC, NY, NZ), ("x", "core", "y", "z"))
    every = ("x", "core", "y", "z")
    in_specs = (
        P(every, None),
        P(every, None, None),
        P(every),
        P(every, None),
        P(every, None),
        P(every),
        P(None, every),
        P(every, None),
    )
    return jax.shard_map(
        shards, mesh=fine, in_specs=in_specs, out_specs=P(every, None), check_vma=False
    )
```

time: 474 us -> 262 us (0.55)
  waiting for transfers between devices: 347 us -> 78.5 us
  Pallas kernels: 0 us -> 79.1 us
  matrix products: 38.4 us -> 0 us
  starting transfers between devices: 14.5 us -> 51.8 us
  local copies, waits for them, and re-layouts: 41.8 us -> 9.96 us
  blocking collectives: 0 us -> 20.6 us
  other arithmetic: 17.4 us -> 3.66 us
    all_gather x2 -> x1, waiting for transfers between devices: 252 us -> 0.02 us  [shards(): lax.all_gather(jnp.concatenate([in_rows, out_rows], axis=0), ('x', 'core'...]
    pallas_call x0 -> x10, Pallas kernels: none -> 79.1 us  [the longest x2 31.8 us: attend(): pl.pallas_call(functools.partial(attend_kernel, scale), grid=(count,), in...]
    all_to_all x2 -> x7, waiting for transfers between devices: 93 us -> 54.1 us  [swap_z(): return lax.all_to_all(values, 'z', split_axis=0, concat_axis=0, tiled=True)]
    dot_general x6 -> x0, matrix products: 38.4 us -> none  [the longest x4 17.1 us: attend_rows(): jnp.einsum('hnl,lhd->nhd', weights, value_heads, preferred_element_type=j...]
    ppermute x0 -> x13, waiting for transfers between devices: none -> 24.4 us  [the longest x1 15.3 us: shards(): key_far = lax.ppermute(key_up, 'y', ring(NY, 1))]
    ppermute x0 -> x13, starting transfers between devices: none -> 22.9 us  [the longest x3 7.79 us: shards(): sent = [lax.ppermute(columns, 'x', [(0, k)]) for k in range(1, NX)]]
    all_to_all x0 -> x1, blocking collectives: none -> 20.6 us  [swap_z(): return lax.all_to_all(values, 'z', split_axis=0, concat_axis=0, tiled=True)]
    all_to_all x2 -> x7, starting transfers between devices: 14.3 us -> 28.8 us  [swap_z(): return lax.all_to_all(values, 'z', split_axis=0, concat_axis=0, tiled=True)]
  transfers between devices with their start and end apart: 4 -> 21, of which waited for: 3 -> 8; matrix products, arithmetic and copies ran while one was open for 4% -> 3% of each run, Pallas kernels for 0% -> 29%
where the time goes in v1:
time: 262 us; the launch traced here: 258 us
  Pallas kernels  79.1 us (30%)
  waiting for transfers between devices  78.5 us (30%)
  starting transfers between devices  51.8 us (20%)
  blocking collectives  20.6 us (8%)
  between operations  14.3 us (5%)
  local copies, waits for them, and re-layouts  9.96 us (4%)
  other arithmetic  3.66 us (1%)
    all_to_all x7, waiting for transfers between devices, swap_z(): return lax.all_to_all(values, 'z', split_axis=0, concat_axis=0, tiled=True)  54.1 us
    pallas_call x2, Pallas kernels, attend(): pl.pallas_call(functools.partial(attend_kernel, scale), grid=(count,), in...  31.8 us
    all_to_all x7, starting transfers between devices, swap_z(): return lax.all_to_all(values, 'z', split_axis=0, concat_axis=0, tiled=True)  28.8 us
    all_to_all x1, blocking collectives, swap_z(): return lax.all_to_all(values, 'z', split_axis=0, concat_axis=0, tiled=True)  20.6 us
    pallas_call x2, Pallas kernels, own(): pl.pallas_call(functools.partial(own_kernel, scale), grid=(steps,), in_sp...  18.2 us
    ppermute x1, waiting for transfers between devices, shards(): key_far = lax.ppermute(key_up, 'y', ring(NY, 1))  15.3 us
    pallas_call x2, Pallas kernels, finish(): pl.pallas_call(functools.partial(finish_kernel, chunk), grid=(steps,), in...  10.5 us
    ppermute x1, waiting for transfers between devices, shards(): value_up = lax.ppermute(values, 'y', ring(NY, 1))  9.13 us
  transfers between devices with their start and end apart: 21, of which 8 were waited for; matrix products, arithmetic and copies ran while one was open for 3% of the time, Pallas kernels for 29%

profile of v1, /device:TPU:1, one launch (start us, length us, event | category | flops | bytes accessed | tf_op | source)
XLA Modules:
  0.0 257.9 jit_solution(15748658944592481247)
XLA Ops:
  6.5 5.2 %collective-permute-start.2 = (bf16[16,1024]{1,0:T(8,128)(2,1)}, bf16[16,1024]{1,0:T(8,128)(2,1)S(1)}, u32[]{:S(2)}, u32[]{:S(2)}) collective-permute-start(bf16[16,1024]{1,0:T(8,128)(2,1)} %bitcast.28), channel_id=1, source_target_pairs={{0,192},{1,193},{2,194},{3,195},{4,196},{5,197},{6,198},{7,199},{8... | collective-permute-start | bytes 98312 | tf_op jit(solution)/shard_map/ppermute | solution.py:264
  16.6 20.6 %all_to_all.40 = bf16[8,24,1024]{2,1,0:T(8,128)(2,1)S(1)} all-to-all(bf16[8,24,1024]{2,1,0:T(8,128)(2,1)S(1)} %broadcast_in_dim.7), channel_id=1, replica_groups=mesh['x'=4,'core'=2,'y'=4,'z'=8] {'z'}, dimensions={0} | all-to-all | bytes 786432 | tf_op jit(solution)/shard_map/all_to_all | solution.py:253
  38.9 3.4 %all-to-all-start.1 = ((bf16[8,16,1024]{2,1,0:T(8,128)(2,1)}), bf16[8,16,1024]{2,1,0:T(8,128)(2,1)S(1)}, u32[]{:S(2)}, u32[]{:S(2)}) async-start(bf16[8,16,1024]{2,1,0:T(8,128)(2,1)} %broadcast_in_dim.8), calls=%async_computation.1 | async-start | bytes 524288 | tf_op jit(solution)/shard_map/all_to_all | solution.py:253
  42.9 5.5 %prep.1 = (bf16[8,384,128]{2,1,0:T(8,128)(2,1)}, bf16[8,384,128]{2,1,0:T(8,128)(2,1)}) custom-call(s32[1]{0:T(128)S(6)} %copy.24.len_ref, s32[1,3]{1,0:T(1,128)} %mask_ref.1, bf16[384,2048]{1,0:T(8,128)(2,1)} %bitcast.21, bf16[384,2048]{1,0:T(8,128)(2,1)} %bitcast.22), custom_call_target="tpu_custom_call" | custom-call | tf_op jit(solution)/shard_map/prep/pallas_call | solution.py:51
  48.5 3.2 %all-to-all-done.1 = bf16[8,16,1024]{2,1,0:T(8,128)(2,1)S(1)} async-done(((bf16[8,16,1024]{2,1,0:T(8,128)(2,1)}), bf16[8,16,1024]{2,1,0:T(8,128)(2,1)S(1)}, u32[]{:S(2)}, u32[]{:S(2)}) %all-to-all-start.1) | async-done | bytes 262176 | tf_op jit(solution)/shard_map/all_to_all | solution.py:253
  51.6 3.5 %all-to-all-start.3 = ((bf16[8,384,128]{2,1,0:T(8,128)(2,1)}), bf16[8,384,128]{2,1,0:T(8,128)(2,1)S(1)}, u32[]{:S(2)}, u32[]{:S(2)}) async-start(bf16[8,384,128]{2,1,0:T(8,128)(2,1)} %get-tuple-element.25), calls=%async_computation.3 | async-start | bytes 1572864 | tf_op jit(solution)/shard_map/all_to_all | solution.py:253
  55.2 2.8 %collective-permute-start.5 = (bf16[128,1024]{1,0:T(8,128)(2,1)S(1)}, bf16[128,1024]{1,0:T(8,128)(2,1)S(1)}, u32[]{:S(2)}, u32[]{:S(2)}) collective-permute-start(bf16[128,1024]{1,0:T(8,128)(2,1)S(1)} %bitcast.24), channel_id=1, source_target_pairs={{0,24},{8,0},{16,8},{24,16},{1,25},{9,1},{17,9},{25,17},{2,26},{10... | collective-permute-start | bytes 786440 | tf_op jit(solution)/shard_map/ppermute | solution.py:281
  59.0 16.1 %all-to-all-done.3 = bf16[8,384,128]{2,1,0:T(8,128)(2,1)S(1)} async-done(((bf16[8,384,128]{2,1,0:T(8,128)(2,1)}), bf16[8,384,128]{2,1,0:T(8,128)(2,1)S(1)}, u32[]{:S(2)}, u32[]{:S(2)}) %all-to-all-start.3) | async-done | bytes 786464 | tf_op jit(solution)/shard_map/all_to_all | solution.py:253
  75.1 4.2 %all-to-all-start.4 = ((bf16[8,384,128]{2,1,0:T(8,128)(2,1)}), bf16[8,384,128]{2,1,0:T(8,128)(2,1)}, u32[]{:S(2)}, u32[]{:S(2)}) async-start(bf16[8,384,128]{2,1,0:T(8,128)(2,1)} %get-tuple-element.26), calls=%async_computation.4 | async-start | bytes 1572864 | tf_op jit(solution)/shard_map/all_to_all | solution.py:253
  79.5 4.2 %collective-permute-start.6 = (bf16[512,1024]{1,0:T(8,128)(2,1)S(1)}, bf16[512,1024]{1,0:T(8,128)(2,1)S(1)}, u32[]{:S(2)}, u32[]{:S(2)}) collective-permute-start(bf16[512,1024]{1,0:T(8,128)(2,1)S(1)} %pad_maximum_fusion.mine_ref), channel_id=1, source_target_pairs={{0,32},{32,0},{1,33},{33,1},{2,34},{34,2},{3,35},{35,3},{4,36},{36... | collective-permute-start | bytes 3145736 | tf_op jit(solution)/shard_map/ppermute | solution.py:283
  83.7 4.4 %norm.1.rows_ref = bf16[1024,1024]{1,0:T(8,128)(2,1)} custom-call(bf16[1024,1024]{1,0:T(8,128)(2,1)} %rows_ref.5), custom_call_target="tpu_custom_call" | custom-call | tf_op jit(solution)/shard_map/norm/pallas_call | solution.py:76
  89.6 4.4 %query.3.query_ref = bf16[8,512,128]{2,1,0:T(8,128)(2,1)} custom-call(s32[8]{0:T(128)} %pad_add_fusion.slot_ref, bf16[1024,1024]{1,0:T(8,128)(2,1)} %norm.1.rows_ref, bf16[512,1024]{1,0:T(8,128)(2,1)} %copy-done.2, bf16[512,1024]{1,0:T(8,128)(2,1)} %copy-done.4), custom_call_target="tpu_custom_call" | custom-call | tf_op jit(solution)/shard_map/query/pallas_call | solution.py:104
  94.1 5.3 %all-to-all-done.4 = bf16[8,384,128]{2,1,0:T(8,128)(2,1)} async-done(((bf16[8,384,128]{2,1,0:T(8,128)(2,1)}), bf16[8,384,128]{2,1,0:T(8,128)(2,1)}, u32[]{:S(2)}, u32[]{:S(2)}) %all-to-all-start.4) | async-done | bytes 786464 | tf_op jit(solution)/shard_map/all_to_all | solution.py:253
  99.4 3.6 %all-to-all-start.6 = ((bf16[8,512,128]{2,1,0:T(8,128)(2,1)}), bf16[8,512,128]{2,1,0:T(8,128)(2,1)S(1)}, u32[]{:S(2)}, u32[]{:S(2)}) async-start(bf16[8,512,128]{2,1,0:T(8,128)(2,1)} %query.3.query_ref), calls=%async_computation.6 | async-start | bytes 2097152 | tf_op jit(solution)/shard_map/all_to_all | solution.py:253
  102.9 2.8 %collective-permute-start.11 = (bf16[8,384,128]{2,1,0:T(8,128)(2,1)}, bf16[8,384,128]{2,1,0:T(8,128)(2,1)}, u32[]{:S(2)}, u32[]{:S(2)}) collective-permute-start(bf16[8,384,128]{2,1,0:T(8,128)(2,1)} %all-to-all-done.4), channel_id=1, source_target_pairs={{0,24},{8,0},{16,8},{24,16},{1,25},{9,1},{17,9},{25,17},{2,26},{10... | collective-permute-start | bytes 2359304 | tf_op jit(solution)/shard_map/ppermute | solution.py:294
  105.7 4.3 %query.2.query_ref = bf16[8,512,128]{2,1,0:T(8,128)(2,1)} custom-call(s32[8]{0:T(128)} %pad_add_fusion.slot_ref, bf16[1024,1024]{1,0:T(8,128)(2,1)} %norm.1.rows_ref, bf16[512,1024]{1,0:T(8,128)(2,1)} %copy-done.2, bf16[512,1024]{1,0:T(8,128)(2,1)} %copy-done.4), custom_call_target="tpu_custom_call" | custom-call | tf_op jit(solution)/shard_map/query/pallas_call | solution.py:104
  110.0 18.5 %all-to-all-done.6.query_ref = bf16[8,512,128]{2,1,0:T(8,128)(2,1)S(1)} async-done(((bf16[8,512,128]{2,1,0:T(8,128)(2,1)}), bf16[8,512,128]{2,1,0:T(8,128)(2,1)S(1)}, u32[]{:S(2)}, u32[]{:S(2)}) %all-to-all-start.6) | async-done | bytes 1048608 | tf_op jit(solution)/shard_map/all_to_all | solution.py:253
  128.5 4.2 %all-to-all-start.2 = ((bf16[8,512,128]{2,1,0:T(8,128)(2,1)}), bf16[8,512,128]{2,1,0:T(8,128)(2,1)}, u32[]{:S(2)}, u32[]{:S(2)}) async-start(bf16[8,512,128]{2,1,0:T(8,128)(2,1)} %query.2.query_ref), calls=%async_computation.2 | async-start | bytes 2097152 | tf_op jit(solution)/shard_map/all_to_all | solution.py:253
  134.8 1.5 collective-permute-start.12
  141.0 9.1 %collective-permute-done.10 = bf16[8,384,128]{2,1,0:T(8,128)(2,1)S(1)} collective-permute-done((bf16[8,384,128]{2,1,0:T(8,128)(2,1)}, bf16[8,384,128]{2,1,0:T(8,128)(2,1)S(1)}, u32[]{:S(2)}, u32[]{:S(2)}) %collective-permute-start.10) | collective-permute-done | bytes 786464 | tf_op jit(solution)/shard_map/ppermute | solution.py:293
  151.6 15.3 %collective-permute-done.8 = bf16[8,384,128]{2,1,0:T(8,128)(2,1)S(1)} collective-permute-done((bf16[8,384,128]{2,1,0:T(8,128)(2,1)}, bf16[8,384,128]{2,1,0:T(8,128)(2,1)S(1)}, u32[]{:S(2)}, u32[]{:S(2)}) %collective-permute-start.8) | collective-permute-done | bytes 786464 | tf_op jit(solution)/shard_map/ppermute | solution.py:295
  167.1 1.6 copy-done.1
  168.7 15.9 %attend.3 = bf16[8,512,128]{2,1,0:T(8,128)(2,1)} custom-call(s32[8,8]{1,0:T(8,128)} %get-tuple-element.31.user_ref, bf16[8,512,128]{2,1,0:T(8,128)(2,1)} %copy-done.5, bf16[32,384,128]{2,1,0:T(8,128)(2,1)} %copy-done.1, bf16[32,384,128]{2,1,0:T(8,128)(2,1)} %copy-done), custom_call_target="tpu_custom_call" | custom-call | tf_op jit(solution)/shard_map/attend/pallas_call | solution.py:137
  184.6 6.3 %all-to-all-start.7 = ((bf16[8,512,128]{2,1,0:T(8,128)(2,1)}), bf16[8,512,128]{2,1,0:T(8,128)(2,1)S(1)}, u32[]{:S(2)}, u32[]{:S(2)}) async-start(bf16[8,512,128]{2,1,0:T(8,128)(2,1)} %attend.3), calls=%async_computation.7 | async-start | bytes 2097152 | tf_op jit(solution)/shard_map/all_to_all | solution.py:253
  190.8 15.9 %attend.2 = bf16[8,512,128]{2,1,0:T(8,128)(2,1)} custom-call(s32[8,8]{1,0:T(8,128)} %get-tuple-element.32.user_ref, bf16[8,512,128]{2,1,0:T(8,128)(2,1)} %all-to-all-done.2.query_ref, bf16[32,384,128]{2,1,0:T(8,128)(2,1)} %copy-done.1, bf16[32,384,128]{2,1,0:T(8,128)(2,1)} %copy-done), custom_call_target="tpu_custom_call" | custom-call | tf_op jit(solution)/shard_map/attend/pallas_call | solution.py:137
  206.7 9.2 %all-to-all-done.7.hist_ref = bf16[8,512,128]{2,1,0:T(8,128)(2,1)S(1)} async-done(((bf16[8,512,128]{2,1,0:T(8,128)(2,1)}), bf16[8,512,128]{2,1,0:T(8,128)(2,1)S(1)}, u32[]{:S(2)}, u32[]{:S(2)}) %all-to-all-start.7) | async-done | bytes 1048608 | tf_op jit(solution)/shard_map/all_to_all | solution.py:253
  216.0 3.6 %all-to-all-start.5 = ((bf16[8,512,128]{2,1,0:T(8,128)(2,1)}), bf16[8,512,128]{2,1,0:T(8,128)(2,1)S(1)}, u32[]{:S(2)}, u32[]{:S(2)}) async-start(bf16[8,512,128]{2,1,0:T(8,128)(2,1)} %attend.2), calls=%async_computation.5 | async-start | bytes 2097152 | tf_op jit(solution)/shard_map/all_to_all | solution.py:253
  219.6 9.1 %own.2 = (f32[512,1024]{1,0:T(8,128)}, bf16[512,1024]{1,0:T(8,128)(2,1)}) custom-call(bf16[1024,1024]{1,0:T(8,128)(2,1)} %norm.1.rows_ref, bf16[8,512,128]{2,1,0:T(8,128)(2,1)} %query.2.query_ref, bf16[32,160,1024]{2,1,0:T(8,128)(2,1)} %bitcast.13, bf16[32,160,1024]{2,1,0:T(8,128)(2,1)} %bitcast.14, bf16[32,160,1024]{2,1,0:T(8,128)(2,1)} %bitcast.15), custom_call_target="tpu_custom_call" | custom-call | tf_op jit(solution)/shard_map/own/pallas_call | solution.py:182
  228.6 9.1 %own.3 = (f32[512,1024]{1,0:T(8,128)}, bf16[512,1024]{1,0:T(8,128)(2,1)}) custom-call(bf16[1024,1024]{1,0:T(8,128)(2,1)} %norm.1.rows_ref, bf16[8,512,128]{2,1,0:T(8,128)(2,1)} %query.3.query_ref, bf16[32,160,1024]{2,1,0:T(8,128)(2,1)} %bitcast.16, bf16[32,160,1024]{2,1,0:T(8,128)(2,1)} %bitcast.17, bf16[32,160,1024]{2,1,0:T(8,128)(2,1)} %bitcast.18), custom_call_target="tpu_custom_call" | custom-call | tf_op jit(solution)/shard_map/own/pallas_call | solution.py:182
  237.7 5.3 %finish.2.rest_0_ = bf16[1024,1024]{1,0:T(8,128)(2,1)} custom-call(s32[16]{0:T(128)} %count_ref.3, bf16[8,512,128]{2,1,0:T(8,128)(2,1)} %copy-done.6, f32[512,1024]{1,0:T(8,128)} %get-tuple-element.29.own_ref, bf16[512,1024]{1,0:T(8,128)(2,1)} %get-tuple-element.30.gate_ref, bf16[32,160,1024]{2,1,0:T(8,128)(2,1)} %bitcast.19, bf16[1024,1024]{1,0:T(8,128)(2,1)} %rows_ref.5), custom_call_target="tpu_custom_call" | custom-call | tf_op jit(solution)/shard_map/finish/pallas_call | solution.py:240
  243.0 1.8 all-to-all-done.5.hist_ref
  245.8 5.3 %finish.3 = bf16[1024,1024]{1,0:T(8,128)(2,1)} custom-call(s32[16]{0:T(128)} %count_ref.3, bf16[8,512,128]{2,1,0:T(8,128)(2,1)} %copy-done.3, f32[512,1024]{1,0:T(8,128)} %get-tuple-element.27.own_ref, bf16[512,1024]{1,0:T(8,128)(2,1)} %get-tuple-element.28.gate_ref, bf16[32,160,1024]{2,1,0:T(8,128)(2,1)} %bitcast.20, ...), custom_call_target="tpu_custom_call", output_to_operand_aliasing={{}: (6, {})} | custom-call | tf_op jit(solution)/shard_map/finish/pallas_call | solution.py:240
  (61 shorter events, 18.5 us)
Async XLA Ops:
  6.5 213.0 %all-gather.3.cloned.1.call-start = ((), (), s32[]{:S(2)}) async-start(), calls=%async_computation.8 | async-start | bytes 10813440 | tf_op jit(solution)/shard_map/all_gather | solution.py:289
  6.5 9.3 %collective-permute-start.2 = (bf16[16,1024]{1,0:T(8,128)(2,1)}, bf16[16,1024]{1,0:T(8,128)(2,1)S(1)}, u32[]{:S(2)}, u32[]{:S(2)}) collective-permute-start(bf16[16,1024]{1,0:T(8,128)(2,1)} %bitcast.28), channel_id=1, source_target_pairs={{0,192},{1,193},{2,194},{3,195},{4,196},{5,197},{6,198},{7,199},{8... | collective-permute-start | bytes 98312 | tf_op jit(solution)/shard_map/ppermute | solution.py:264
  11.7 4.1 %collective-permute-start = (bf16[16,1024]{1,0:T(8,128)(2,1)}, bf16[16,1024]{1,0:T(8,128)(2,1)S(1)}, u32[]{:S(2)}, u32[]{:S(2)}) collective-permute-start(bf16[16,1024]{1,0:T(8,128)(2,1)} %bitcast.29), channel_id=1, source_target_pairs={{0,64},{1,65},{2,66},{3,67},{4,68},{5,69},{6,70},{7,71},{8,72},{9,... | collective-permute-start | bytes 98312 | tf_op jit(solution)/shard_map/ppermute | solution.py:264
  13.1 2.8 %collective-permute-start.1 = (bf16[16,1024]{1,0:T(8,128)(2,1)}, bf16[16,1024]{1,0:T(8,128)(2,1)S(1)}, u32[]{:S(2)}, u32[]{:S(2)}) collective-permute-start(bf16[16,1024]{1,0:T(8,128)(2,1)} %bitcast.30), channel_id=1, source_target_pairs={{0,128},{1,129},{2,130},{3,131},{4,132},{5,133},{6,134},{7,135},{8... | collective-permute-start | bytes 98312 | tf_op jit(solution)/shard_map/ppermute | solution.py:264
  37.2 14.4 %copy-start.7 = (bf16[8,24,1024]{2,1,0:T(8,128)(2,1)}, bf16[8,24,1024]{2,1,0:T(8,128)(2,1)S(1)}, u32[]{:S(2)}) copy-start(bf16[8,24,1024]{2,1,0:T(8,128)(2,1)S(1)} %all_to_all.40) | copy-start | bytes 1179652
  38.9 12.8 %all-to-all-start.1 = ((bf16[8,16,1024]{2,1,0:T(8,128)(2,1)}), bf16[8,16,1024]{2,1,0:T(8,128)(2,1)S(1)}, u32[]{:S(2)}, u32[]{:S(2)}) async-start(bf16[8,16,1024]{2,1,0:T(8,128)(2,1)} %broadcast_in_dim.8), calls=%async_computation.1 | async-start | bytes 524288 | tf_op jit(solution)/shard_map/all_to_all | solution.py:253
  51.6 23.5 %all-to-all-start.3 = ((bf16[8,384,128]{2,1,0:T(8,128)(2,1)}), bf16[8,384,128]{2,1,0:T(8,128)(2,1)S(1)}, u32[]{:S(2)}, u32[]{:S(2)}) async-start(bf16[8,384,128]{2,1,0:T(8,128)(2,1)} %get-tuple-element.25), calls=%async_computation.3 | async-start | bytes 1572864 | tf_op jit(solution)/shard_map/all_to_all | solution.py:253
  55.2 24.2 %collective-permute-start.5 = (bf16[128,1024]{1,0:T(8,128)(2,1)S(1)}, bf16[128,1024]{1,0:T(8,128)(2,1)S(1)}, u32[]{:S(2)}, u32[]{:S(2)}) collective-permute-start(bf16[128,1024]{1,0:T(8,128)(2,1)S(1)} %bitcast.24), channel_id=1, source_target_pairs={{0,24},{8,0},{16,8},{24,16},{1,25},{9,1},{17,9},{25,17},{2,26},{10... | collective-permute-start | bytes 786440 | tf_op jit(solution)/shard_map/ppermute | solution.py:281
  58.0 21.4 %collective-permute-start.4 = (bf16[128,1024]{1,0:T(8,128)(2,1)S(1)}, bf16[128,1024]{1,0:T(8,128)(2,1)S(1)}, u32[]{:S(2)}, u32[]{:S(2)}) collective-permute-start(bf16[128,1024]{1,0:T(8,128)(2,1)S(1)} %bitcast.25), channel_id=1, source_target_pairs={{0,16},{8,24},{16,0},{24,8},{1,17},{9,25},{17,1},{25,9},{2,18},{10... | collective-permute-start | bytes 786440 | tf_op jit(solution)/shard_map/ppermute | solution.py:281
  58.4 21.0 %collective-permute-start.3 = (bf16[128,1024]{1,0:T(8,128)(2,1)S(1)}, bf16[128,1024]{1,0:T(8,128)(2,1)S(1)}, u32[]{:S(2)}, u32[]{:S(2)}) collective-permute-start(bf16[128,1024]{1,0:T(8,128)(2,1)S(1)} %bitcast.26), channel_id=1, source_target_pairs={{0,8},{8,16},{16,24},{24,0},{1,9},{9,17},{17,25},{25,1},{2,10},{10... | collective-permute-start | bytes 786440 | tf_op jit(solution)/shard_map/ppermute | solution.py:281
  75.1 24.2 %all-to-all-start.4 = ((bf16[8,384,128]{2,1,0:T(8,128)(2,1)}), bf16[8,384,128]{2,1,0:T(8,128)(2,1)}, u32[]{:S(2)}, u32[]{:S(2)}) async-start(bf16[8,384,128]{2,1,0:T(8,128)(2,1)} %get-tuple-element.26), calls=%async_computation.4 | async-start | bytes 1572864 | tf_op jit(solution)/shard_map/all_to_all | solution.py:253
  79.5 9.2 %copy-start.2 = (bf16[512,1024]{1,0:T(8,128)(2,1)}, bf16[512,1024]{1,0:T(8,128)(2,1)S(1)}, u32[]{:S(2)}) copy-start(bf16[512,1024]{1,0:T(8,128)(2,1)S(1)} %pad_maximum_fusion.mine_ref) | copy-start | bytes 3145732
  79.5 9.2 %collective-permute-start.6 = (bf16[512,1024]{1,0:T(8,128)(2,1)S(1)}, bf16[512,1024]{1,0:T(8,128)(2,1)S(1)}, u32[]{:S(2)}, u32[]{:S(2)}) collective-permute-start(bf16[512,1024]{1,0:T(8,128)(2,1)S(1)} %pad_maximum_fusion.mine_ref), channel_id=1, source_target_pairs={{0,32},{32,0},{1,33},{33,1},{2,34},{34,2},{3,35},{35,3},{4,36},{36... | collective-permute-start | bytes 3145736 | tf_op jit(solution)/shard_map/ppermute | solution.py:283
  88.6 1.0 copy-start.4
  99.4 29.1 %all-to-all-start.6 = ((bf16[8,512,128]{2,1,0:T(8,128)(2,1)}), bf16[8,512,128]{2,1,0:T(8,128)(2,1)S(1)}, u32[]{:S(2)}, u32[]{:S(2)}) async-start(bf16[8,512,128]{2,1,0:T(8,128)(2,1)} %query.3.query_ref), calls=%async_computation.6 | async-start | bytes 2097152 | tf_op jit(solution)/shard_map/all_to_all | solution.py:253
  102.9 31.9 %collective-permute-start.11 = (bf16[8,384,128]{2,1,0:T(8,128)(2,1)}, bf16[8,384,128]{2,1,0:T(8,128)(2,1)}, u32[]{:S(2)}, u32[]{:S(2)}) collective-permute-start(bf16[8,384,128]{2,1,0:T(8,128)(2,1)} %all-to-all-done.4), channel_id=1, source_target_pairs={{0,24},{8,0},{16,8},{24,16},{1,25},{9,1},{17,9},{25,17},{2,26},{10... | collective-permute-start | bytes 2359304 | tf_op jit(solution)/shard_map/ppermute | solution.py:294
  105.7 32.7 %collective-permute-start.7 = (bf16[8,384,128]{2,1,0:T(8,128)(2,1)S(1)}, bf16[8,384,128]{2,1,0:T(8,128)(2,1)}, u32[]{:S(2)}, u32[]{:S(2)}) collective-permute-start(bf16[8,384,128]{2,1,0:T(8,128)(2,1)S(1)} %all-to-all-done.3), channel_id=1, source_target_pairs={{0,8},{8,16},{16,24},{24,0},{1,9},{9,17},{17,25},{25,1},{2,10},{10... | collective-permute-start | bytes 2359304 | tf_op jit(solution)/shard_map/ppermute | solution.py:291
  128.5 12.5 %copy-start.5 = (bf16[8,512,128]{2,1,0:T(8,128)(2,1)}, bf16[8,512,128]{2,1,0:T(8,128)(2,1)S(1)}, u32[]{:S(2)}) copy-start(bf16[8,512,128]{2,1,0:T(8,128)(2,1)S(1)} %all-to-all-done.6.query_ref) | copy-start | bytes 3145732
  128.5 56.1 %all-to-all-start.2 = ((bf16[8,512,128]{2,1,0:T(8,128)(2,1)}), bf16[8,512,128]{2,1,0:T(8,128)(2,1)}, u32[]{:S(2)}, u32[]{:S(2)}) async-start(bf16[8,512,128]{2,1,0:T(8,128)(2,1)} %query.2.query_ref), calls=%async_computation.2 | async-start | bytes 2097152 | tf_op jit(solution)/shard_map/all_to_all | solution.py:253
  133.5 16.6 %collective-permute-start.10 = (bf16[8,384,128]{2,1,0:T(8,128)(2,1)}, bf16[8,384,128]{2,1,0:T(8,128)(2,1)S(1)}, u32[]{:S(2)}, u32[]{:S(2)}) collective-permute-start(bf16[8,384,128]{2,1,0:T(8,128)(2,1)} %all-to-all-done.4), channel_id=1, source_target_pairs={{0,8},{8,16},{16,24},{24,0},{1,9},{9,17},{17,25},{25,1},{2,10},{10... | collective-permute-start | bytes 2359304 | tf_op jit(solution)/shard_map/ppermute | solution.py:293
  134.8 15.4 %collective-permute-start.12 = (bf16[8,384,128]{2,1,0:T(8,128)(2,1)}, bf16[8,384,128]{2,1,0:T(8,128)(2,1)S(1)}, u32[]{:S(2)}, u32[]{:S(2)}) collective-permute-start(bf16[8,384,128]{2,1,0:T(8,128)(2,1)} %collective-permute-done.11), channel_id=1, source_target_pairs={{0,24},{8,0},{16,8},{24,16},{1,25},{9,1},{17,9},{25,17},{2,26},{10... | collective-permute-start | bytes 2359304 | tf_op jit(solution)/shard_map/ppermute | solution.py:296
  137.0 30.0 %collective-permute-start.9 = (bf16[8,384,128]{2,1,0:T(8,128)(2,1)S(1)}, bf16[8,384,128]{2,1,0:T(8,128)(2,1)S(1)}, u32[]{:S(2)}, u32[]{:S(2)}) collective-permute-start(bf16[8,384,128]{2,1,0:T(8,128)(2,1)S(1)} %all-to-all-done.3), channel_id=1, source_target_pairs={{0,24},{8,0},{16,8},{24,16},{1,25},{9,1},{17,9},{25,17},{2,26},{10... | collective-permute-start | bytes 2359304 | tf_op jit(solution)/shard_map/ppermute | solution.py:292
  138.4 28.5 %collective-permute-start.8 = (bf16[8,384,128]{2,1,0:T(8,128)(2,1)}, bf16[8,384,128]{2,1,0:T(8,128)(2,1)S(1)}, u32[]{:S(2)}, u32[]{:S(2)}) collective-permute-start(bf16[8,384,128]{2,1,0:T(8,128)(2,1)} %collective-permute-done.7), channel_id=1, source_target_pairs={{0,8},{8,16},{16,24},{24,0},{1,9},{9,17},{17,25},{25,1},{2,10},{10... | collective-permute-start | bytes 2359304 | tf_op jit(solution)/shard_map/ppermute | solution.py:295
  151.6 15.5 %copy-start = (bf16[32,384,128]{2,1,0:T(8,128)(2,1)}, bf16[32,384,128]{2,1,0:T(8,128)(2,1)S(1)}, u32[]{:S(2)}) copy-start(bf16[32,384,128]{2,1,0:T(8,128)(2,1)S(1)} %constant_dynamic-update-slice_fusion.4.value_ref) | copy-start | bytes 9437188
  167.1 1.6 copy-start.1
  184.6 31.4 %all-to-all-start.7 = ((bf16[8,512,128]{2,1,0:T(8,128)(2,1)}), bf16[8,512,128]{2,1,0:T(8,128)(2,1)S(1)}, u32[]{:S(2)}, u32[]{:S(2)}) async-start(bf16[8,512,128]{2,1,0:T(8,128)(2,1)} %attend.3), calls=%async_computation.7 | async-start | bytes 2097152 | tf_op jit(solution)/shard_map/all_to_all | solution.py:253
  216.0 12.7 %copy-start.6 = (bf16[8,512,128]{2,1,0:T(8,128)(2,1)}, bf16[8,512,128]{2,1,0:T(8,128)(2,1)S(1)}, u32[]{:S(2)}) copy-start(bf16[8,512,128]{2,1,0:T(8,128)(2,1)S(1)} %all-to-all-done.7.hist_ref) | copy-start | bytes 3145732
  216.0 28.8 %all-to-all-start.5 = ((bf16[8,512,128]{2,1,0:T(8,128)(2,1)}), bf16[8,512,128]{2,1,0:T(8,128)(2,1)S(1)}, u32[]{:S(2)}, u32[]{:S(2)}) async-start(bf16[8,512,128]{2,1,0:T(8,128)(2,1)} %attend.2), calls=%async_computation.5 | async-start | bytes 2097152 | tf_op jit(solution)/shard_map/all_to_all | solution.py:253
  244.8 1.0 copy-start.3
Sparse Core Ops, SparseCore 0:
  38.2 65.9 all-gather.2

commit v2 on v1

v2 whole, which is shorter than its diff:
```python
import functools

import jax
import jax.numpy as jnp
from jax import lax
from jax.experimental import pallas as pl
from jax.experimental.pallas import tpu as pltpu
from jax.sharding import Mesh
from jax.sharding import PartitionSpec as P

HEADS = 8
HEAD = 128
BLK = 128
HIST = 384
TILE = 64
CHUNKS = 2
META = 8
PIECE = 128
NX, NC, NY, NZ = 4, 2, 4, 8
BF = jnp.bfloat16
F32 = jnp.float32
MIB = 1024 * 1024
NT = (((1,), (1,)), ((), ()))


def half_silu(a):
    return a + a * jnp.tanh(a)


def params(limit=16):
    return pltpu.CompilerParams(vmem_limit_bytes=limit * MIB)


def ring(size, step):
    return [(i, (i + step) % size) for i in range(size)]


def prep_kernel(len_ref, mask_ref, hist_ref, out_ref):
    place = lax.broadcasted_iota(jnp.int32, (HIST, HEAD), 0)
    kept = jnp.where(
        place < BLK, mask_ref[0, 0], jnp.where(place < 2 * BLK, mask_ref[0, 1], mask_ref[0, 2])
    )
    live = (place < len_ref[0]) & (kept > 0)
    width = HEADS * HEAD
    for h in range(HEADS):
        cut = slice(h * HEAD, (h + 1) * HEAD)
        for b in range(0, HIST, BLK):
            turned = hist_ref[b : b + BLK, cut].astype(F32).T
            out_ref[h, b : b + BLK, :] = turned.astype(BF)
        values = hist_ref[:, width + h * HEAD : width + (h + 1) * HEAD].astype(F32)
        out_ref[h, HIST:, :] = jnp.where(live, values, 0.0).astype(BF)


def prep(hist, hist_len, block_mask):
    smem = pl.BlockSpec(memory_space=pltpu.SMEM)
    vmem = pl.BlockSpec(memory_space=pltpu.VMEM)
    return pl.pallas_call(
        prep_kernel,
        in_specs=[smem, smem, vmem],
        out_specs=vmem,
        out_shape=jax.ShapeDtypeStruct((HEADS, 2 * HIST, HEAD), BF),
        compiler_params=params(),
        name="prep",
    )(hist_len, block_mask, hist)


def norm_kernel(rows_ref, out_ref):
    total = rows_ref.shape[0]
    for start in range(0, total, PIECE):
        values = rows_ref[start : start + PIECE, :].astype(F32)
        centred = values - jnp.mean(values, axis=-1, keepdims=True)
        variance = jnp.mean(centred * centred, axis=-1, keepdims=True)
        out_ref[start : start + PIECE, :] = (centred * lax.rsqrt(variance + 1e-05)).astype(BF)


def norm(rows):
    vmem = pl.BlockSpec(memory_space=pltpu.VMEM)
    return pl.pallas_call(
        norm_kernel,
        in_specs=[vmem],
        out_specs=vmem,
        out_shape=jax.ShapeDtypeStruct(rows.shape, BF),
        compiler_params=params(),
        name="norm",
    )(rows)


def query_kernel(slot_ref, rows_ref, mine_ref, other_ref, out_ref):
    rows = rows_ref[...]
    share = mine_ref.shape[0] // NY
    for part, weights in enumerate((mine_ref, other_ref)):
        for pair in range(2):
            block = jnp.concatenate(
                [weights[(2 * pair + k) * share : (2 * pair + k) * share + HEAD, :] for k in range(2)]
            )
            made = lax.dot_general(rows, block, NT, preferred_element_type=F32)
            made = half_silu(made * 0.5).astype(BF)
            for lane in range(2):
                slot = slot_ref[part * 4 + pair * 2 + lane]
                out_ref[slot] = made[:, lane * HEAD : (lane + 1) * HEAD]


def query(slots, normed, mine, other):
    vmem = pl.BlockSpec(memory_space=pltpu.VMEM)
    return pl.pallas_call(
        query_kernel,
        in_specs=[pl.BlockSpec(memory_space=pltpu.SMEM), vmem, vmem, vmem],
        out_specs=vmem,
        out_shape=jax.ShapeDtypeStruct((HEADS, normed.shape[0], HEAD), BF),
        compiler_params=params(),
        name="query",
    )(slots, normed, mine, other)


def attend_kernel(scale, first, user_ref, query_ref, cache_ref, out_ref):
    sources, rows, _ = out_ref.shape

    def step(t, carry):
        users = [user_ref[s, first + t] for s in range(sources)]
        here = pl.ds(pl.multiple_of((first + t) * TILE, TILE), TILE)
        there = pl.ds(pl.multiple_of(t * TILE, TILE), TILE)
        weights = []
        for s, u in enumerate(users):
            turned = jnp.concatenate(
                [cache_ref[u, b : b + BLK, :] for b in range(0, HIST, BLK)], axis=1
            )
            score = jnp.dot(query_ref[s, here, :], turned, preferred_element_type=F32)
            weights.append(half_silu(score * (0.5 * scale)).astype(BF))
        for s, u in enumerate(users):
            out_ref[s, there, :] = jnp.dot(
                weights[s], cache_ref[u, HIST:, :], preferred_element_type=F32
            ).astype(BF)
        return carry

    lax.fori_loop(0, rows // TILE, step, 0, unroll=2)


def attend(users, queries, caches, chunk, scale):
    sources, rows, _ = queries.shape
    rows = rows // CHUNKS
    vmem = pl.BlockSpec(memory_space=pltpu.VMEM)
    smem = pl.BlockSpec(memory_space=pltpu.SMEM)
    return pl.pallas_call(
        functools.partial(attend_kernel, scale, chunk * rows // TILE),
        in_specs=[smem, vmem, vmem],
        out_specs=vmem,
        out_shape=jax.ShapeDtypeStruct((sources, rows, HEAD), BF),
        compiler_params=params(),
        name="attend",
    )(users, queries, caches)


def own_kernel(scale, rows_ref, query_ref, key_w, value_w, gate_w, own_ref, gate_ref):
    rows = rows_ref[...]
    width = rows.shape[1]

    def project(weights):
        block = weights[...].reshape(2 * HEAD, width)
        made = lax.dot_general(rows, block, NT, preferred_element_type=F32)
        return half_silu(made * 0.5).astype(BF)

    self_keys = project(key_w).astype(F32)
    self_values = project(value_w).astype(F32)
    gate_ref[...] = project(gate_w)
    for lane in range(2):
        cut = slice(lane * HEAD, (lane + 1) * HEAD)
        products = query_ref[lane].astype(F32) * self_keys[:, cut]
        strength = half_silu(jnp.sum(products, axis=1, keepdims=True) * (0.5 * scale))
        own_ref[:, cut] = strength * self_values[:, cut]


def own(normed, queries, gathered, scale):
    total, width = normed.shape
    steps = width // (2 * HEAD)

    def weights(place):
        return pl.BlockSpec((2, HEAD, width), lambda i: (place * steps + i, 0, 0))

    return pl.pallas_call(
        functools.partial(own_kernel, scale),
        grid=(steps,),
        in_specs=[
            pl.BlockSpec((total, width), lambda i: (0, 0)),
            pl.BlockSpec((2, total, HEAD), lambda i: (i, 0, 0)),
            weights(1),
            weights(2),
            weights(3),
        ],
        out_specs=[pl.BlockSpec((total, 2 * HEAD), lambda i: (0, i))] * 2,
        out_shape=[
            jax.ShapeDtypeStruct((total, width), F32),
            jax.ShapeDtypeStruct((total, width), BF),
        ],
        compiler_params=params(56),
        name="own",
    )(normed, queries, gathered, gathered, gathered)


def finish_kernel(first, count_ref, hist_ref, own_ref, gate_ref, out_w, rows_ref, *rest):
    out_ref = rest[-1]
    rows, width = rows_ref.shape
    history = jnp.concatenate([hist_ref[h].astype(F32) for h in range(HEADS)], axis=1)
    combined = history + own_ref[...]
    centred = combined - jnp.mean(combined, axis=-1, keepdims=True)
    variance = jnp.mean(centred * centred, axis=-1, keepdims=True)
    gated = centred * lax.rsqrt(variance + 1e-05) * gate_ref[...].astype(F32)
    mixed = jnp.dot(gated.astype(BF), out_w[...], preferred_element_type=F32)
    mixed = mixed + rows_ref[...].astype(F32)
    slot = lax.broadcasted_iota(jnp.int32, (TILE, width), 0)
    tile = (first + pl.program_id(0)) * (rows // TILE)
    for t in range(rows // TILE):
        cut = slice(t * TILE, (t + 1) * TILE)
        scored = jnp.where(slot < count_ref[tile + t], mixed[cut, :], 0.0)
        out_ref[cut, :] = scored.astype(BF)


def finish(counts, history, own_part, gate, out_w, candidates, chunk, before):
    total, width = candidates.shape
    steps = total // CHUNKS // PIECE
    place = pl.BlockSpec((PIECE, width), lambda i: (chunk * steps + i, 0))
    specs = [
        pl.BlockSpec(memory_space=pltpu.SMEM),
        pl.BlockSpec((HEADS, PIECE, HEAD), lambda i: (0, i, 0)),
        place,
        place,
        pl.BlockSpec((width, width), lambda i: (0, 0)),
        place,
    ]
    given = [counts, history, own_part, gate, out_w, candidates]
    aliases = {}
    if before is not None:
        specs.append(pl.BlockSpec(memory_space=pl.ANY))
        given.append(before)
        aliases = {len(given) - 1: 0}
    return pl.pallas_call(
        functools.partial(finish_kernel, chunk * steps),
        grid=(steps,),
        in_specs=specs,
        out_specs=place,
        out_shape=jax.ShapeDtypeStruct((total, width), BF),
        input_output_aliases=aliases,
        compiler_params=params(56),
        name="finish",
    )(*given)


def swap_z(values):
    return lax.all_to_all(values, "z", split_axis=0, concat_axis=0, tiled=True)


def spread_y(part):
    up = lax.ppermute(part, "y", ring(NY, 1))
    down = lax.ppermute(part, "y", ring(NY, NY - 1))
    half = part.shape[0] // 2
    far = [
        lax.ppermute(up[:half], "y", ring(NY, 1)),
        lax.ppermute(down[half:], "y", ring(NY, NY - 1)),
    ]
    return jnp.concatenate([part, up] + far + [down], axis=0)


def shards(candidates, hist_kv, hist_len, block_mask, tile_user, tile_count, weight_in, weight_out):
    width = candidates.shape[1]
    tiles = tile_user.shape[0]
    scale = HEAD ** (-0.5)
    at_x, at_core, at_y, at_z = [lax.axis_index(name) for name in ("x", "core", "y", "z")]

    columns = weight_in.T
    share, out_share = columns.shape[0], weight_out.shape[0]
    normed = norm(candidates)
    caches = swap_z(prep(hist_kv[0], hist_len, block_mask))
    both = jnp.concatenate([columns, weight_out], axis=0)
    sent = [lax.ppermute(both, "x", [(0, k), (k, 0)]) for k in range(1, NX)]
    query_part = jnp.where(at_x == 0, columns, sent[0][:share] + sent[1][:share] + sent[2][:share])
    out_part = jnp.concatenate([weight_out] + [piece[share:] for piece in sent], axis=0)
    rest_part = jnp.where(at_x == 0, out_part, columns)
    meta = jnp.zeros((META, width), BF).at[0, :tiles].set(tile_user[:, 0].astype(BF))
    packed = jnp.concatenate([query_part, rest_part, meta], axis=0)
    spread = [packed] + [lax.ppermute(packed, "z", ring(NZ, k)) for k in range(1, NZ)]
    spread, caches, normed = lax.optimization_barrier((spread, caches, normed))
    caches = lax.all_gather(caches, "y", axis=0, tiled=True)
    spread = jnp.stack(spread)[(at_z - jnp.arange(NZ, dtype=jnp.int32)) % NZ]
    query_z = spread[:, :share].reshape(NZ * share, width)
    users = spread[:, 2 * share, :tiles].astype(jnp.int32)
    rest = spread[:, share : 2 * share].reshape(NZ * share, width)

    parts = [query_z] + [lax.ppermute(query_z, "y", ring(NY, k)) for k in range(1, NY)]
    mine = jnp.concatenate(parts, axis=0)
    other = lax.ppermute(mine, "core", ring(NC, 1))
    at = (at_y - jnp.arange(NY, dtype=jnp.int32)) % NY
    slots = jnp.concatenate([at_core * NY + at, (1 - at_core) * NY + at]).astype(jnp.int32)

    queries = query(slots, normed, mine, other)
    arrived = swap_z(queries)
    rest = [rest] + [lax.ppermute(rest, "y", ring(NY, k)) for k in range(1, NY)]
    rest = jnp.stack(rest)[at]
    rest, arrived = lax.optimization_barrier((rest, arrived))
    gathered = lax.all_gather(rest, ("x", "core"), axis=0, tiled=True)

    history = [swap_z(attend(users, arrived, caches, c, scale)) for c in range(CHUNKS)]
    out_w = gathered[:HEADS].reshape(NC * NY * NZ, NX, -1, width)
    out_w = jnp.swapaxes(out_w, 0, 1).reshape(width, width)
    own_part, gate = own(normed, queries, gathered, scale)
    out = None
    for c in range(CHUNKS):
        out = finish(tile_count, history[c], own_part, gate, out_w, candidates, c, out)
    return out


def solution(mesh):
    fine = Mesh(mesh.devices.reshape(NX, NC, NY, NZ), ("x", "core", "y", "z"))
    every = ("x", "core", "y", "z")
    in_specs = (
        P(every, None),
        P(every, None, None),
        P(every),
        P(every, None),
        P(every, None),
        P(every),
        P(None, every),
        P(every, None),
    )
    return jax.shard_map(
        shards, mesh=fine, in_specs=in_specs, out_specs=P(every, None), check_vma=False
    )
```

time: 262 us -> 248 us (0.947); the launches traced: 258 us -> 247 us
  waiting for transfers between devices: 78.5 us -> 118 us
  Pallas kernels: 79.1 us -> 41.3 us
  blocking collectives: 20.6 us -> 0 us
  local copies, waits for them, and re-layouts: 9.96 us -> 23.6 us
  starting transfers between devices: 51.8 us -> 48.4 us
    ppermute x12 -> x16, waiting for transfers between devices: 24.4 us -> 64.1 us  [the longest x7 25.3 us: shards(): lax.ppermute(packed, 'z', ring(NZ, k))]
    pallas_call x8 -> x7, Pallas kernels: 60.9 us -> 28.8 us  [the longest x2 12.4 us: finish(): pl.pallas_call(functools.partial(finish_kernel, chunk * steps), grid=(ste...]
    all_to_all x1 -> x0, blocking collectives: 20.6 us -> none  [swap_z(): return lax.all_to_all(values, 'z', split_axis=0, concat_axis=0, tiled=True)]
    all_to_all x7 -> x4, waiting for transfers between devices: 54.1 us -> 44.3 us  [swap_z(): return lax.all_to_all(values, 'z', split_axis=0, concat_axis=0, tiled=True)]
    all_gather x1 -> x2, waiting for transfers between devices: 0.02 us -> 7.52 us  [the longest x1 7.52 us: shards(): gathered = lax.all_gather(rest, ('x', 'core'), axis=0, tiled=True)]
    all_to_all x7 -> x4, starting transfers between devices: 28.8 us -> 21.3 us  [swap_z(): return lax.all_to_all(values, 'z', split_axis=0, concat_axis=0, tiled=True)]
    unnamed x22 -> x33, local copies, waits for them, and re-layouts: 6.39 us -> 13.2 us
    reshape x1 -> x3, local copies, waits for them, and re-layouts: 0.02 us -> 6.64 us  [the longest x2 4.6 us: shards(): out_w = gathered[:HEADS].reshape(NC * NY * NZ, NX, -1, width)]
  transfers between devices with their start and end apart: 21 -> 23, of which waited for: 8 -> 18; matrix products, arithmetic and copies ran while one was open for 3% -> 4% of each run, Pallas kernels for 29% -> 13%
where the time goes in v2:
time: 248 us; the launch traced here: 247 us
  waiting for transfers between devices  118 us (48%)
  starting transfers between devices  48.4 us (20%)
  Pallas kernels  41.3 us (17%)
  local copies, waits for them, and re-layouts  23.6 us (10%)
  between operations  14.4 us (6%)
    all_to_all x4, waiting for transfers between devices, swap_z(): return lax.all_to_all(values, 'z', split_axis=0, concat_axis=0, tiled=True)  44.3 us
    ppermute x7, waiting for transfers between devices, shards(): lax.ppermute(packed, 'z', ring(NZ, k))  25.3 us
    ppermute x3, waiting for transfers between devices, shards(): rest = [rest] + [lax.ppermute(rest, 'y', ring(NY, k)) for k in range(1, NY)]  21.9 us
    all_to_all x4, starting transfers between devices, swap_z(): return lax.all_to_all(values, 'z', split_axis=0, concat_axis=0, tiled=True)  21.3 us
    ppermute x3, waiting for transfers between devices, shards(): lax.ppermute(query_z, 'y', ring(NY, k))  13.7 us
    unnamed x33, local copies, waits for them, and re-layouts  13.2 us
    pallas_call x1, Pallas kernels, own(): pl.pallas_call(functools.partial(own_kernel, scale), grid=(steps,), in_sp...  12.5 us
    pallas_call x2, Pallas kernels, finish(): pl.pallas_call(functools.partial(finish_kernel, chunk * steps), grid=(ste...  12.4 us
  transfers between devices with their start and end apart: 23, of which 18 were waited for; matrix products, arithmetic and copies ran while one was open for 4% of the time, Pallas kernels for 13%

profile of v2, /device:TPU:1, one launch (start us, length us, event | category | flops | bytes accessed | tf_op | source)
XLA Modules:
  0.0 247.2 jit_solution(13118145776044709533)
XLA Ops:
  9.3 2.2 prep.1
  11.5 9.1 %all-to-all-start = ((bf16[8,768,128]{2,1,0:T(8,128)(2,1)}), bf16[8,768,128]{2,1,0:T(8,128)(2,1)}, u32[]{:S(2)}, u32[]{:S(2)}) async-start(bf16[8,768,128]{2,1,0:T(8,128)(2,1)} %prep.1), calls=%async_computation | async-start | bytes 3145728 | tf_op jit(solution)/shard_map/all_to_all | solution.py:248
  20.7 4.4 %collective-permute-start.2 = (bf16[20,1024]{1,0:T(8,128)(2,1)S(1)}, bf16[20,1024]{1,0:T(8,128)(2,1)S(1)}, u32[]{:S(2)}, u32[]{:S(2)}) collective-permute-start(bf16[20,1024]{1,0:T(8,128)(2,1)S(1)} %pad_maximum_fusion.2), channel_id=1, source_target_pairs={{0,192},{192,0},{1,193},{193,1},{2,194},{194,2},{3,195},{195,3},{4... | collective-permute-start | bytes 122888 | tf_op jit(solution)/shard_map/ppermute | solution.py:273
  29.0 2.8 %collective-permute-done.1 = bf16[20,1024]{1,0:T(8,128)(2,1)S(1)} collective-permute-done((bf16[20,1024]{1,0:T(8,128)(2,1)S(1)}, bf16[20,1024]{1,0:T(8,128)(2,1)S(1)}, u32[]{:S(2)}, u32[]{:S(2)}) %collective-permute-start.1) | collective-permute-done | bytes 40992 | tf_op jit(solution)/shard_map/ppermute | solution.py:273
  32.3 2.7 %collective-permute-start.9 = (bf16[40,1024]{1,0:T(8,128)(2,1)S(1)}, bf16[40,1024]{1,0:T(8,128)(2,1)S(1)}, u32[]{:S(2)}, u32[]{:S(2)}) collective-permute-start(bf16[40,1024]{1,0:T(8,128)(2,1)S(1)} %fusion.1), channel_id=1, source_target_pairs={{0,7},{1,0},{2,1},{3,2},{4,3},{5,4},{6,5},{7,6},{8,15},{9,8},{10,9... | collective-permute-start | bytes 245768 | tf_op jit(solution)/shard_map/ppermute | solution.py:279
  38.3 3.3 %collective-permute-start.6 = (bf16[40,1024]{1,0:T(8,128)(2,1)S(1)}, bf16[40,1024]{1,0:T(8,128)(2,1)S(1)}, u32[]{:S(2)}, u32[]{:S(2)}) collective-permute-start(bf16[40,1024]{1,0:T(8,128)(2,1)S(1)} %fusion.1), channel_id=1, source_target_pairs={{0,4},{1,5},{2,6},{3,7},{4,0},{5,1},{6,2},{7,3},{8,12},{9,13},{10,... | collective-permute-start | bytes 245768 | tf_op jit(solution)/shard_map/ppermute | solution.py:279
  41.6 16.6 %collective-permute-done.9 = bf16[40,1024]{1,0:T(8,128)(2,1)S(1)} collective-permute-done((bf16[40,1024]{1,0:T(8,128)(2,1)S(1)}, bf16[40,1024]{1,0:T(8,128)(2,1)S(1)}, u32[]{:S(2)}, u32[]{:S(2)}) %collective-permute-start.9) | collective-permute-done | bytes 81952 | tf_op jit(solution)/shard_map/ppermute | solution.py:279
  63.5 2.2 collective-permute-done.6
  65.7 4.0 %collective-permute-done.4 = bf16[40,1024]{1,0:T(8,128)(2,1)S(1)} collective-permute-done((bf16[40,1024]{1,0:T(8,128)(2,1)S(1)}, bf16[40,1024]{1,0:T(8,128)(2,1)S(1)}, u32[]{:S(2)}, u32[]{:S(2)}) %collective-permute-start.4) | collective-permute-done | bytes 81952 | tf_op jit(solution)/shard_map/ppermute | solution.py:279
  71.8 2.8 %collective-permute-start.15 = (bf16[128,1024]{1,0:T(8,128)(2,1)S(1)}, bf16[128,1024]{1,0:T(8,128)(2,1)S(1)}, u32[]{:S(2)}, u32[]{:S(2)}) collective-permute-start(bf16[128,1024]{1,0:T(8,128)(2,1)S(1)} %bitcast.44), channel_id=1, source_target_pairs={{0,24},{8,0},{16,8},{24,16},{1,25},{9,1},{17,9},{25,17},{2,26},{10... | collective-permute-start | bytes 786440 | tf_op jit(solution)/shard_map/ppermute | solution.py:287
  75.6 5.1 %collective-permute-done.15 = bf16[128,1024]{1,0:T(8,128)(2,1)S(1)} collective-permute-done((bf16[128,1024]{1,0:T(8,128)(2,1)S(1)}, bf16[128,1024]{1,0:T(8,128)(2,1)S(1)}, u32[]{:S(2)}, u32[]{:S(2)}) %collective-permute-start.15) | collective-permute-done | bytes 262176 | tf_op jit(solution)/shard_map/ppermute | solution.py:287
  81.4 7.9 %collective-permute-done.13 = bf16[128,1024]{1,0:T(8,128)(2,1)S(1)} collective-permute-done((bf16[128,1024]{1,0:T(8,128)(2,1)S(1)}, bf16[128,1024]{1,0:T(8,128)(2,1)S(1)}, u32[]{:S(2)}, u32[]{:S(2)}) %collective-permute-start.13) | collective-permute-done | bytes 262176 | tf_op jit(solution)/shard_map/ppermute | solution.py:287
  89.4 2.9 %collective-permute-start.16 = (bf16[512,1024]{1,0:T(8,128)(2,1)S(1)}, bf16[512,1024]{1,0:T(8,128)(2,1)}, u32[]{:S(2)}, u32[]{:S(2)}) collective-permute-start(bf16[512,1024]{1,0:T(8,128)(2,1)S(1)} %pad_maximum_fusion.1.mine_ref), channel_id=1, source_target_pairs={{0,32},{32,0},{1,33},{33,1},{2,34},{34,2},{3,35},{35,3},{4,36},{36... | collective-permute-start | bytes 3145736 | tf_op jit(solution)/shard_map/ppermute | solution.py:289
  92.5 2.3 collective-permute-done.16.other_ref
  94.8 4.1 %query.1.query_ref = bf16[8,1024,128]{2,1,0:T(8,128)(2,1)S(1)} custom-call(s32[8]{0:T(128)S(1)} %pad_add_fusion.slot_ref, bf16[1024,1024]{1,0:T(8,128)(2,1)S(1)} %norm.1.rows_ref, bf16[512,1024]{1,0:T(8,128)(2,1)S(1)} %pad_maximum_fusion.1.mine_ref, bf16[512,1024]{1,0:T(8,128)(2,1)} %collective-permute-done.16.other_ref), custom_call_target="tpu_custom_call" | custom-call | tf_op jit(solution)/shard_map/query/pallas_call | solution.py:105
  100.2 3.6 %all-to-all-start.1 = ((bf16[8,1024,128]{2,1,0:T(8,128)(2,1)}), bf16[8,1024,128]{2,1,0:T(8,128)(2,1)S(1)}, u32[]{:S(2)}, u32[]{:S(2)}) async-start(bf16[8,1024,128]{2,1,0:T(8,128)(2,1)} %copy-done.3), calls=%async_computation.1 | async-start | bytes 4194304 | tf_op jit(solution)/shard_map/all_to_all | solution.py:248
  105.5 12.2 %collective-permute-done.12 = bf16[128,1024]{1,0:T(8,128)(2,1)S(1)} collective-permute-done((bf16[128,1024]{1,0:T(8,128)(2,1)S(1)}, bf16[128,1024]{1,0:T(8,128)(2,1)S(1)}, u32[]{:S(2)}, u32[]{:S(2)}) %collective-permute-start.12) | collective-permute-done | bytes 262176 | tf_op jit(solution)/shard_map/ppermute | solution.py:295
  119.0 8.3 %collective-permute-done.10 = bf16[128,1024]{1,0:T(8,128)(2,1)S(1)} collective-permute-done((bf16[128,1024]{1,0:T(8,128)(2,1)S(1)}, bf16[128,1024]{1,0:T(8,128)(2,1)S(1)}, u32[]{:S(2)}, u32[]{:S(2)}) %collective-permute-start.10) | collective-permute-done | bytes 262176 | tf_op jit(solution)/shard_map/ppermute | solution.py:295
  129.0 22.8 %all-to-all-done.1.query_ref = bf16[8,1024,128]{2,1,0:T(8,128)(2,1)S(1)} async-done(((bf16[8,1024,128]{2,1,0:T(8,128)(2,1)}), bf16[8,1024,128]{2,1,0:T(8,128)(2,1)S(1)}, u32[]{:S(2)}, u32[]{:S(2)}) %all-to-all-start.1) | async-done | bytes 2097184 | tf_op jit(solution)/shard_map/all_to_all | solution.py:248
  152.6 2.8 %copy-done = bf16[32,768,128]{2,1,0:T(8,128)(2,1)S(1)} copy-done((bf16[32,768,128]{2,1,0:T(8,128)(2,1)S(1)}, bf16[32,768,128]{2,1,0:T(8,128)(2,1)}, u32[]{:S(2)}) %copy-start) | copy-done | bytes 6291480
  155.4 4.4 %attend.3 = bf16[8,512,128]{2,1,0:T(8,128)(2,1)} custom-call(s32[8,16]{1,0:T(8,128)S(1)} %bitcast.37, bf16[8,1024,128]{2,1,0:T(8,128)(2,1)S(1)} %all-to-all-done.1.query_ref, bf16[32,768,128]{2,1,0:T(8,128)(2,1)S(1)} %copy-done), custom_call_target="tpu_custom_call" | custom-call | tf_op jit(solution)/shard_map/attend/pallas_call | solution.py:143
  159.8 5.0 %all-to-all-start.3 = ((bf16[8,512,128]{2,1,0:T(8,128)(2,1)}), bf16[8,512,128]{2,1,0:T(8,128)(2,1)S(1)}, u32[]{:S(2)}, u32[]{:S(2)}) async-start(bf16[8,512,128]{2,1,0:T(8,128)(2,1)} %attend.3), calls=%async_computation.3 | async-start | bytes 2097152 | tf_op jit(solution)/shard_map/all_to_all | solution.py:248
  164.9 3.3 %copy-done.1 = bf16[32,768,128]{2,1,0:T(8,128)(2,1)S(1)} copy-done((bf16[32,768,128]{2,1,0:T(8,128)(2,1)S(1)}, bf16[32,768,128]{2,1,0:T(8,128)(2,1)}, u32[]{:S(2)}) %copy-start.1) | copy-done | bytes 6291480
  168.2 4.4 %attend.2 = bf16[8,512,128]{2,1,0:T(8,128)(2,1)} custom-call(s32[8,16]{1,0:T(8,128)S(1)} %bitcast.38, bf16[8,1024,128]{2,1,0:T(8,128)(2,1)S(1)} %all-to-all-done.1.query_ref, bf16[32,768,128]{2,1,0:T(8,128)(2,1)S(1)} %copy-done.1), custom_call_target="tpu_custom_call" | custom-call | tf_op jit(solution)/shard_map/attend/pallas_call | solution.py:143
  172.6 21.4 %all-to-all-done.3.hist_ref = bf16[8,512,128]{2,1,0:T(8,128)(2,1)S(1)} async-done(((bf16[8,512,128]{2,1,0:T(8,128)(2,1)}), bf16[8,512,128]{2,1,0:T(8,128)(2,1)S(1)}, u32[]{:S(2)}, u32[]{:S(2)}) %all-to-all-start.3) | async-done | bytes 1048608 | tf_op jit(solution)/shard_map/all_to_all | solution.py:248
  195.1 3.6 %all-to-all-start.2 = ((bf16[8,512,128]{2,1,0:T(8,128)(2,1)}), bf16[8,512,128]{2,1,0:T(8,128)(2,1)S(1)}, u32[]{:S(2)}, u32[]{:S(2)}) async-start(bf16[8,512,128]{2,1,0:T(8,128)(2,1)} %attend.2), calls=%async_computation.2 | async-start | bytes 2097152 | tf_op jit(solution)/shard_map/all_to_all | solution.py:248
  198.6 7.5 %all-gather.5.cloned.1.call-done.key_w.value_w.gate_w = bf16[32,128,1024]{2,1,0:T(8,128)(2,1)} async-done(((bf16[4,128,1024]{2,1,0:T(8,128)(2,1)}), bf16[32,128,1024]{2,1,0:T(8,128)(2,1)}) %all-gather.5.cloned.1.call-update) | async-done | bytes 8388624 | tf_op jit(solution)/shard_map/all_gather | solution.py:298
  207.8 2.2 reshape.150
  210.0 2.4 copy.15
  214.4 12.5 %own.1 = (f32[1024,1024]{1,0:T(8,128)}, bf16[1024,1024]{1,0:T(8,128)(2,1)}) custom-call(bf16[1024,1024]{1,0:T(8,128)(2,1)} %copy-done.2, bf16[8,1024,128]{2,1,0:T(8,128)(2,1)} %copy-done.3, bf16[32,128,1024]{2,1,0:T(8,128)(2,1)} %all-gather.5.cloned.1.call-done.key_w.value_w.gate_w, bf16[32,128,1024]{2,1,0:T(8,128)(2,1)} %all-gather.5.cloned.1.call-done.key_w.value_w.gate_w, ...), custom_call_target="tpu_custom_call" | custom-call | tf_op jit(solution)/shard_map/own/pallas_call | solution.py:179
  226.9 6.2 %finish.2.rest_0_ = bf16[1024,1024]{1,0:T(8,128)(2,1)} custom-call(s32[16]{0:T(128)} %count_ref.3, bf16[8,512,128]{2,1,0:T(8,128)(2,1)} %copy-done.8, f32[1024,1024]{1,0:T(8,128)} %get-tuple-element.43.own_ref, bf16[1024,1024]{1,0:T(8,128)(2,1)} %get-tuple-element.44.gate_ref, bf16[1024,1024]{1,0:T(8,128)(2,1)} %reshape.151.out_w, bf16[1024,1024]{1,0:T(8,128)(2,1)} %rows_ref.5), custom_call_target="tpu_custom_call" | custom-call | tf_op jit(solution)/shard_map/finish/pallas_call | solution.py:235
  234.1 6.2 %finish.3 = bf16[1024,1024]{1,0:T(8,128)(2,1)} custom-call(s32[16]{0:T(128)} %count_ref.3, bf16[8,512,128]{2,1,0:T(8,128)(2,1)} %copy-done.7, f32[1024,1024]{1,0:T(8,128)} %get-tuple-element.43.own_ref, bf16[1024,1024]{1,0:T(8,128)(2,1)} %get-tuple-element.44.gate_ref, bf16[1024,1024]{1,0:T(8,128)(2,1)} %reshape.151.out_w, ...), custom_call_target="tpu_custom_call", output_to_operand_aliasing={{}: (6, {})} | custom-call | tf_op jit(solution)/shard_map/finish/pallas_call | solution.py:235
  (82 shorter events, 31.3 us)
Async XLA Ops:
  11.4 9.2 %copy-start.10 = (bf16[1024,16]{0,1:T(8,128)(2,1)S(1)}, bf16[1024,16]{0,1:T(8,128)(2,1)}, u32[]{:S(2)}) copy-start(bf16[1024,16]{0,1:T(8,128)(2,1)} %param.16) | copy-start | bytes 98308
  11.5 9.2 %copy-start.11 = (bf16[4,1024]{1,0:T(4,128)(2,1)S(1)}, bf16[4,1024]{1,0:T(4,128)(2,1)}, u32[]{:S(2)}) copy-start(bf16[4,1024]{1,0:T(4,128)(2,1)} %param.17) | copy-start | bytes 24580
  11.5 17.5 %copy-start.12 = (s32[16,1]{0,1:T(1,128)S(1)}, s32[16,1]{0,1:T(1,128)}, u32[]{:S(2)}) copy-start(s32[16,1]{0,1:T(1,128)} %param.14) | copy-start | bytes 196
  11.5 59.5 %all-to-all-start = ((bf16[8,768,128]{2,1,0:T(8,128)(2,1)}), bf16[8,768,128]{2,1,0:T(8,128)(2,1)}, u32[]{:S(2)}, u32[]{:S(2)}) async-start(bf16[8,768,128]{2,1,0:T(8,128)(2,1)} %prep.1), calls=%async_computation | async-start | bytes 3145728 | tf_op jit(solution)/shard_map/all_to_all | solution.py:248
  20.6 132.0 %all-gather.3.cloned.1.call-start = ((), (), s32[]{:S(2)}) async-start(), calls=%async_computation.4 | async-start | bytes 7864320 | tf_op jit(solution)/shard_map/all_gather | solution.py:281
  20.7 8.3 %collective-permute-start.2 = (bf16[20,1024]{1,0:T(8,128)(2,1)S(1)}, bf16[20,1024]{1,0:T(8,128)(2,1)S(1)}, u32[]{:S(2)}, u32[]{:S(2)}) collective-permute-start(bf16[20,1024]{1,0:T(8,128)(2,1)S(1)} %pad_maximum_fusion.2), channel_id=1, source_target_pairs={{0,192},{192,0},{1,193},{193,1},{2,194},{194,2},{3,195},{195,3},{4... | collective-permute-start | bytes 122888 | tf_op jit(solution)/shard_map/ppermute | solution.py:273
  25.1 6.7 %collective-permute-start.1 = (bf16[20,1024]{1,0:T(8,128)(2,1)S(1)}, bf16[20,1024]{1,0:T(8,128)(2,1)S(1)}, u32[]{:S(2)}, u32[]{:S(2)}) collective-permute-start(bf16[20,1024]{1,0:T(8,128)(2,1)S(1)} %pad_maximum_fusion.2), channel_id=1, source_target_pairs={{0,128},{128,0},{1,129},{129,1},{2,130},{130,2},{3,131},{131,3},{4... | collective-permute-start | bytes 122888 | tf_op jit(solution)/shard_map/ppermute | solution.py:273
  27.0 5.2 %collective-permute-start = (bf16[20,1024]{1,0:T(8,128)(2,1)S(1)}, bf16[20,1024]{1,0:T(8,128)(2,1)S(1)}, u32[]{:S(2)}, u32[]{:S(2)}) collective-permute-start(bf16[20,1024]{1,0:T(8,128)(2,1)S(1)} %pad_maximum_fusion.2), channel_id=1, source_target_pairs={{0,64},{64,0},{1,65},{65,1},{2,66},{66,2},{3,67},{67,3},{4,68},{68... | collective-permute-start | bytes 122888 | tf_op jit(solution)/shard_map/ppermute | solution.py:273
  32.3 25.8 %collective-permute-start.9 = (bf16[40,1024]{1,0:T(8,128)(2,1)S(1)}, bf16[40,1024]{1,0:T(8,128)(2,1)S(1)}, u32[]{:S(2)}, u32[]{:S(2)}) collective-permute-start(bf16[40,1024]{1,0:T(8,128)(2,1)S(1)} %fusion.1), channel_id=1, source_target_pairs={{0,7},{1,0},{2,1},{3,2},{4,3},{5,4},{6,5},{7,6},{8,15},{9,8},{10,9... | collective-permute-start | bytes 245768 | tf_op jit(solution)/shard_map/ppermute | solution.py:279
  35.0 24.4 %collective-permute-start.8 = (bf16[40,1024]{1,0:T(8,128)(2,1)S(1)}, bf16[40,1024]{1,0:T(8,128)(2,1)S(1)}, u32[]{:S(2)}, u32[]{:S(2)}) collective-permute-start(bf16[40,1024]{1,0:T(8,128)(2,1)S(1)} %fusion.1), channel_id=1, source_target_pairs={{0,6},{1,7},{2,0},{3,1},{4,2},{5,3},{6,4},{7,5},{8,14},{9,15},{10,... | collective-permute-start | bytes 245768 | tf_op jit(solution)/shard_map/ppermute | solution.py:279
  37.1 26.4 %collective-permute-start.7 = (bf16[40,1024]{1,0:T(8,128)(2,1)S(1)}, bf16[40,1024]{1,0:T(8,128)(2,1)S(1)}, u32[]{:S(2)}, u32[]{:S(2)}) collective-permute-start(bf16[40,1024]{1,0:T(8,128)(2,1)S(1)} %fusion.1), channel_id=1, source_target_pairs={{0,5},{1,6},{2,7},{3,0},{4,1},{5,2},{6,3},{7,4},{8,13},{9,14},{10,... | collective-permute-start | bytes 245768 | tf_op jit(solution)/shard_map/ppermute | solution.py:279
  38.3 27.5 %collective-permute-start.6 = (bf16[40,1024]{1,0:T(8,128)(2,1)S(1)}, bf16[40,1024]{1,0:T(8,128)(2,1)S(1)}, u32[]{:S(2)}, u32[]{:S(2)}) collective-permute-start(bf16[40,1024]{1,0:T(8,128)(2,1)S(1)} %fusion.1), channel_id=1, source_target_pairs={{0,4},{1,5},{2,6},{3,7},{4,0},{5,1},{6,2},{7,3},{8,12},{9,13},{10,... | collective-permute-start | bytes 245768 | tf_op jit(solution)/shard_map/ppermute | solution.py:279
  41.6 24.2 %collective-permute-start.5 = (bf16[40,1024]{1,0:T(8,128)(2,1)S(1)}, bf16[40,1024]{1,0:T(8,128)(2,1)S(1)}, u32[]{:S(2)}, u32[]{:S(2)}) collective-permute-start(bf16[40,1024]{1,0:T(8,128)(2,1)S(1)} %fusion.1), channel_id=1, source_target_pairs={{0,3},{1,4},{2,5},{3,6},{4,7},{5,0},{6,1},{7,2},{8,11},{9,12},{10,... | collective-permute-start | bytes 245768 | tf_op jit(solution)/shard_map/ppermute | solution.py:279
  58.1 11.6 %collective-permute-start.4 = (bf16[40,1024]{1,0:T(8,128)(2,1)S(1)}, bf16[40,1024]{1,0:T(8,128)(2,1)S(1)}, u32[]{:S(2)}, u32[]{:S(2)}) collective-permute-start(bf16[40,1024]{1,0:T(8,128)(2,1)S(1)} %fusion.1), channel_id=1, source_target_pairs={{0,2},{1,3},{2,4},{3,5},{4,6},{5,7},{6,0},{7,1},{8,10},{9,11},{10,... | collective-permute-start | bytes 245768 | tf_op jit(solution)/shard_map/ppermute | solution.py:279
  59.4 11.5 %collective-permute-start.3 = (bf16[40,1024]{1,0:T(8,128)(2,1)S(1)}, bf16[40,1024]{1,0:T(8,128)(2,1)S(1)}, u32[]{:S(2)}, u32[]{:S(2)}) collective-permute-start(bf16[40,1024]{1,0:T(8,128)(2,1)S(1)} %fusion.1), channel_id=1, source_target_pairs={{0,1},{1,2},{2,3},{3,4},{4,5},{5,6},{6,7},{7,0},{8,9},{9,10},{10,1... | collective-permute-start | bytes 245768 | tf_op jit(solution)/shard_map/ppermute | solution.py:279
  60.6 1.6 copy-start.4
  63.4 31.4 %copy-start.2 = (bf16[1024,1024]{1,0:T(8,128)(2,1)}, bf16[1024,1024]{1,0:T(8,128)(2,1)S(1)}, u32[]{:S(2)}) copy-start(bf16[1024,1024]{1,0:T(8,128)(2,1)S(1)} %norm.1.rows_ref) | copy-start | bytes 6291460
  71.7 9.7 %copy-start.9 = (bf16[8,40,1024]{2,1,0:T(8,128)(2,1)}, bf16[8,40,1024]{2,1,0:T(8,128)(2,1)S(1)}, u32[]{:S(2)}) copy-start(bf16[8,40,1024]{2,1,0:T(8,128)(2,1)S(1)} %gather_fusion) | copy-start | bytes 1966084
  71.8 8.9 %collective-permute-start.15 = (bf16[128,1024]{1,0:T(8,128)(2,1)S(1)}, bf16[128,1024]{1,0:T(8,128)(2,1)S(1)}, u32[]{:S(2)}, u32[]{:S(2)}) collective-permute-start(bf16[128,1024]{1,0:T(8,128)(2,1)S(1)} %bitcast.44), channel_id=1, source_target_pairs={{0,24},{8,0},{16,8},{24,16},{1,25},{9,1},{17,9},{25,17},{2,26},{10... | collective-permute-start | bytes 786440 | tf_op jit(solution)/shard_map/ppermute | solution.py:287
  74.6 6.8 %collective-permute-start.14 = (bf16[128,1024]{1,0:T(8,128)(2,1)S(1)}, bf16[128,1024]{1,0:T(8,128)(2,1)S(1)}, u32[]{:S(2)}, u32[]{:S(2)}) collective-permute-start(bf16[128,1024]{1,0:T(8,128)(2,1)S(1)} %bitcast.45), channel_id=1, source_target_pairs={{0,16},{8,24},{16,0},{24,8},{1,17},{9,25},{17,1},{25,9},{2,18},{10... | collective-permute-start | bytes 786440 | tf_op jit(solution)/shard_map/ppermute | solution.py:287
  74.9 14.4 %collective-permute-start.13 = (bf16[128,1024]{1,0:T(8,128)(2,1)S(1)}, bf16[128,1024]{1,0:T(8,128)(2,1)S(1)}, u32[]{:S(2)}, u32[]{:S(2)}) collective-permute-start(bf16[128,1024]{1,0:T(8,128)(2,1)S(1)} %bitcast.46), channel_id=1, source_target_pairs={{0,8},{8,16},{16,24},{24,0},{1,9},{9,17},{17,25},{25,1},{2,10},{10... | collective-permute-start | bytes 786440 | tf_op jit(solution)/shard_map/ppermute | solution.py:287
  89.4 5.4 %collective-permute-start.16 = (bf16[512,1024]{1,0:T(8,128)(2,1)S(1)}, bf16[512,1024]{1,0:T(8,128)(2,1)}, u32[]{:S(2)}, u32[]{:S(2)}) collective-permute-start(bf16[512,1024]{1,0:T(8,128)(2,1)S(1)} %pad_maximum_fusion.1.mine_ref), channel_id=1, source_target_pairs={{0,32},{32,0},{1,33},{33,1},{2,34},{34,2},{3,35},{35,3},{4,36},{36... | collective-permute-start | bytes 3145736 | tf_op jit(solution)/shard_map/ppermute | solution.py:289
  100.2 51.6 %all-to-all-start.1 = ((bf16[8,1024,128]{2,1,0:T(8,128)(2,1)}), bf16[8,1024,128]{2,1,0:T(8,128)(2,1)S(1)}, u32[]{:S(2)}, u32[]{:S(2)}) async-start(bf16[8,1024,128]{2,1,0:T(8,128)(2,1)} %copy-done.3), calls=%async_computation.1 | async-start | bytes 4194304 | tf_op jit(solution)/shard_map/all_to_all | solution.py:248
  103.8 102.3 %all-gather.5.cloned.1.call-start = ((), (), s32[]{:S(2)}) async-start(), calls=%async_computation.5 | async-start | bytes 9437184 | tf_op jit(solution)/shard_map/all_gather | solution.py:298
  103.9 13.8 %collective-permute-start.12 = (bf16[128,1024]{1,0:T(8,128)(2,1)S(1)}, bf16[128,1024]{1,0:T(8,128)(2,1)S(1)}, u32[]{:S(2)}, u32[]{:S(2)}) collective-permute-start(bf16[128,1024]{1,0:T(8,128)(2,1)S(1)} %bitcast.40), channel_id=1, source_target_pairs={{0,24},{8,0},{16,8},{24,16},{1,25},{9,1},{17,9},{25,17},{2,26},{10... | collective-permute-start | bytes 786440 | tf_op jit(solution)/shard_map/ppermute | solution.py:295
  104.1 14.9 %collective-permute-start.11 = (bf16[128,1024]{1,0:T(8,128)(2,1)S(1)}, bf16[128,1024]{1,0:T(8,128)(2,1)S(1)}, u32[]{:S(2)}, u32[]{:S(2)}) collective-permute-start(bf16[128,1024]{1,0:T(8,128)(2,1)S(1)} %bitcast.41), channel_id=1, source_target_pairs={{0,16},{8,24},{16,0},{24,8},{1,17},{9,25},{17,1},{25,9},{2,18},{10... | collective-permute-start | bytes 786440 | tf_op jit(solution)/shard_map/ppermute | solution.py:295
  104.8 22.6 %collective-permute-start.10 = (bf16[128,1024]{1,0:T(8,128)(2,1)S(1)}, bf16[128,1024]{1,0:T(8,128)(2,1)S(1)}, u32[]{:S(2)}, u32[]{:S(2)}) collective-permute-start(bf16[128,1024]{1,0:T(8,128)(2,1)S(1)} %bitcast.42), channel_id=1, source_target_pairs={{0,8},{8,16},{16,24},{24,0},{1,9},{9,17},{17,25},{25,1},{2,10},{10... | collective-permute-start | bytes 786440 | tf_op jit(solution)/shard_map/ppermute | solution.py:295
  152.6 2.8 %copy-start = (bf16[32,768,128]{2,1,0:T(8,128)(2,1)S(1)}, bf16[32,768,128]{2,1,0:T(8,128)(2,1)}, u32[]{:S(2)}) copy-start(bf16[32,768,128]{2,1,0:T(8,128)(2,1)} %all-gather.3.cloned.1.call-done.cache_ref) | copy-start | bytes 18874372
  159.8 34.2 %all-to-all-start.3 = ((bf16[8,512,128]{2,1,0:T(8,128)(2,1)}), bf16[8,512,128]{2,1,0:T(8,128)(2,1)S(1)}, u32[]{:S(2)}, u32[]{:S(2)}) async-start(bf16[8,512,128]{2,1,0:T(8,128)(2,1)} %attend.3), calls=%async_computation.3 | async-start | bytes 2097152 | tf_op jit(solution)/shard_map/all_to_all | solution.py:248
  164.9 3.3 %copy-start.1 = (bf16[32,768,128]{2,1,0:T(8,128)(2,1)S(1)}, bf16[32,768,128]{2,1,0:T(8,128)(2,1)}, u32[]{:S(2)}) copy-start(bf16[32,768,128]{2,1,0:T(8,128)(2,1)} %all-gather.3.cloned.1.call-done.cache_ref) | copy-start | bytes 18874372
  195.1 38.1 %all-to-all-start.2 = ((bf16[8,512,128]{2,1,0:T(8,128)(2,1)}), bf16[8,512,128]{2,1,0:T(8,128)(2,1)S(1)}, u32[]{:S(2)}, u32[]{:S(2)}) async-start(bf16[8,512,128]{2,1,0:T(8,128)(2,1)} %attend.2), calls=%async_computation.2 | async-start | bytes 2097152 | tf_op jit(solution)/shard_map/all_to_all | solution.py:248
  206.2 1.6 slice-start
  (5 other events, 5.4 us)
Sparse Core Ops, SparseCore 0:
  71.1 80.9 all-gather.2
  154.0 52.1 all-gather.4

commit v3 on v2

--- a/solution.py
+++ b/solution.py
@@ -13,9 +13,8 @@
 BLK = 128
 HIST = 384
 TILE = 64
-CHUNKS = 2
 META = 8
-PIECE = 128
+PIECE = 512
 NX, NC, NY, NZ = 4, 2, 4, 8
 BF = jnp.bfloat16
 F32 = jnp.float32
@@ -112,13 +111,12 @@
     )(slots, normed, mine, other)
 
 
-def attend_kernel(scale, first, user_ref, query_ref, cache_ref, out_ref):
+def attend_kernel(scale, user_ref, query_ref, cache_ref, out_ref):
     sources, rows, _ = out_ref.shape
 
     def step(t, carry):
-        users = [user_ref[s, first + t] for s in range(sources)]
-        here = pl.ds(pl.multiple_of((first + t) * TILE, TILE), TILE)
-        there = pl.ds(pl.multiple_of(t * TILE, TILE), TILE)
+        users = [user_ref[s, t] for s in range(sources)]
+        here = pl.ds(pl.multiple_of(t * TILE, TILE), TILE)
         weights = []
         for s, u in enumerate(users):
             turned = jnp.concatenate(
@@ -127,7 +125,7 @@
             score = jnp.dot(query_ref[s, here, :], turned, preferred_element_type=F32)
             weights.append(half_silu(score * (0.5 * scale)).astype(BF))
         for s, u in enumerate(users):
-            out_ref[s, there, :] = jnp.dot(
+            out_ref[s, here, :] = jnp.dot(
                 weights[s], cache_ref[u, HIST:, :], preferred_element_type=F32
             ).astype(BF)
         return carry
@@ -135,16 +133,14 @@
     lax.fori_loop(0, rows // TILE, step, 0, unroll=2)
 
 
-def attend(users, queries, caches, chunk, scale):
-    sources, rows, _ = queries.shape
-    rows = rows // CHUNKS
+def attend(users, queries, caches, scale):
     vmem = pl.BlockSpec(memory_space=pltpu.VMEM)
     smem = pl.BlockSpec(memory_space=pltpu.SMEM)
     return pl.pallas_call(
-        functools.partial(attend_kernel, scale, chunk * rows // TILE),
+        functools.partial(attend_kernel, scale),
         in_specs=[smem, vmem, vmem],
         out_specs=vmem,
-        out_shape=jax.ShapeDtypeStruct((sources, rows, HEAD), BF),
+        out_shape=jax.ShapeDtypeStruct(queries.shape, BF),
         compiler_params=params(),
         name="attend",
     )(users, queries, caches)
@@ -196,8 +192,35 @@
     )(normed, queries, gathered, gathered, gathered)
 
 
-def finish_kernel(first, count_ref, hist_ref, own_ref, gate_ref, out_w, rows_ref, *rest):
-    out_ref = rest[-1]
+def turn_kernel(gathered, out_ref):
+    shares, rows, _ = gathered.shape
+    piece = rows // (NX * NZ)
+    to = lax.broadcasted_iota(jnp.int32, (rows, rows), 0)
+    at = lax.broadcasted_iota(jnp.int32, (rows, rows), 1)
+    plane, place, line = to // (NZ * piece), to // piece % NZ, to % piece
+    picked = (at == (place * NX + plane) * piece + line).astype(F32).astype(BF)
+    span = rows // NX
+    for i in range(shares):
+        turned = jnp.dot(picked, gathered[i], preferred_element_type=F32).astype(BF)
+        for k in range(NX):
+            first = (k * shares + i) * span
+            out_ref[first : first + span, :] = turned[k * span : (k + 1) * span, :]
+
+
+def turn(gathered):
+    rows, width = gathered.shape[1:]
+    return pl.pallas_call(
+        turn_kernel,
+        grid=(1,),
+        in_specs=[pl.BlockSpec((HEADS, rows, width), lambda i: (0, 0, 0))],
+        out_specs=pl.BlockSpec((width, width), lambda i: (0, 0)),
+        out_shape=jax.ShapeDtypeStruct((width, width), BF),
+        compiler_params=params(56),
+        name="turn",
+    )(gathered)
+
+
+def finish_kernel(count_ref, hist_ref, own_ref, gate_ref, out_w, rows_ref, out_ref):
     rows, width = rows_ref.shape
     history = jnp.concatenate([hist_ref[h].astype(F32) for h in range(HEADS)], axis=1)
     combined = history + own_ref[...]
@@ -207,41 +230,32 @@
     mixed = jnp.dot(gated.astype(BF), out_w[...], preferred_element_type=F32)
     mixed = mixed + rows_ref[...].astype(F32)
     slot = lax.broadcasted_iota(jnp.int32, (TILE, width), 0)
-    tile = (first + pl.program_id(0)) * (rows // TILE)
+    tile = pl.program_id(0) * (rows // TILE)
     for t in range(rows // TILE):
         cut = slice(t * TILE, (t + 1) * TILE)
         scored = jnp.where(slot < count_ref[tile + t], mixed[cut, :], 0.0)
         out_ref[cut, :] = scored.astype(BF)
 
 
-def finish(counts, history, own_part, gate, out_w, candidates, chunk, before):
+def finish(counts, history, own_part, gate, out_w, candidates):
     total, width = candidates.shape
-    steps = total // CHUNKS // PIECE
-    place = pl.BlockSpec((PIECE, width), lambda i: (chunk * steps + i, 0))
-    specs = [
-        pl.BlockSpec(memory_space=pltpu.SMEM),
-        pl.BlockSpec((HEADS, PIECE, HEAD), lambda i: (0, i, 0)),
-        place,
-        place,
-        pl.BlockSpec((width, width), lambda i: (0, 0)),
-        place,
-    ]
-    given = [counts, history, own_part, gate, out_w, candidates]
-    aliases = {}
-    if before is not None:
-        specs.append(pl.BlockSpec(memory_space=pl.ANY))
-        given.append(before)
-        aliases = {len(given) - 1: 0}
-    return pl.pallas_call(
-        functools.partial(finish_kernel, chunk * steps),
-        grid=(steps,),
-        in_specs=specs,
+    place = pl.BlockSpec((PIECE, width), lambda i: (i, 0))
+    return pl.pallas_call(
+        finish_kernel,
+        grid=(total // PIECE,),
+        in_specs=[
+            pl.BlockSpec(memory_space=pltpu.SMEM),
+            pl.BlockSpec((HEADS, PIECE, HEAD), lambda i: (0, i, 0)),
+            place,
+            place,
+            pl.BlockSpec((width, width), lambda i: (0, 0)),
+            place,
+        ],
         out_specs=place,
         out_shape=jax.ShapeDtypeStruct((total, width), BF),
-        input_output_aliases=aliases,
         compiler_params=params(56),
         name="finish",
-    )(*given)
+    )(counts, history, own_part, gate, out_w, candidates)
 
 
 def swap_z(values):
@@ -291,20 +305,14 @@
     slots = jnp.concatenate([at_core * NY + at, (1 - at_core) * NY + at]).astype(jnp.int32)
 
     queries = query(slots, normed, mine, other)
+    rest, queries = lax.optimization_barrier((rest, queries))
     arrived = swap_z(queries)
-    rest = [rest] + [lax.ppermute(rest, "y", ring(NY, k)) for k in range(1, NY)]
-    rest = jnp.stack(rest)[at]
-    rest, arrived = lax.optimization_barrier((rest, arrived))
-    gathered = lax.all_gather(rest, ("x", "core"), axis=0, tiled=True)
-
-    history = [swap_z(attend(users, arrived, caches, c, scale)) for c in range(CHUNKS)]
-    out_w = gathered[:HEADS].reshape(NC * NY * NZ, NX, -1, width)
-    out_w = jnp.swapaxes(out_w, 0, 1).reshape(width, width)
+    gathered = lax.all_gather(rest, ("x", "core", "y"))
+
+    history = swap_z(attend(users, arrived, caches, scale))
+    out_w = turn(gathered)
     own_part, gate = own(normed, queries, gathered, scale)
-    out = None
-    for c in range(CHUNKS):
-        out = finish(tile_count, history[c], own_part, gate, out_w, candidates, c, out)
-    return out
+    return finish(tile_count, history, own_part, gate, out_w, candidates)
 
 
 def solution(mesh):

time: 248 us -> 241 us (0.972)
  local copies, waits for them, and re-layouts: 23.6 us -> 10.6 us
  waiting for transfers between devices: 118 us -> 128 us
    ppermute x3 -> x0, waiting for transfers between devices: 21.9 us -> none  [shards(): rest = [rest] + [lax.ppermute(rest, 'y', ring(NY, k)) for k in range(1, NY)]]
    all_gather x1, waiting for transfers between devices: 7.52 us -> 28.6 us  [shards(): gathered = lax.all_gather(rest, ('x', 'core', 'y'))]
    all_to_all x4 -> x3, waiting for transfers between devices: 44.3 us -> 54.5 us  [swap_z(): return lax.all_to_all(values, 'z', split_axis=0, concat_axis=0, tiled=True)]
    ppermute x7, starting transfers between devices: 10.5 us -> 17.2 us  [shards(): lax.ppermute(packed, 'z', ring(NZ, k))]
    reshape x3 -> x0, local copies, waits for them, and re-layouts: 6.64 us -> none  [the longest x2 4.6 us: shards(): out_w = gathered[:HEADS].reshape(NC * NY * NZ, NX, -1, width)]
    ppermute x7, waiting for transfers between devices: 25.3 us -> 21.2 us  [shards(): lax.ppermute(packed, 'z', ring(NZ, k))]
    unnamed x33 -> x29, local copies, waits for them, and re-layouts: 13.2 us -> 9.14 us
    ppermute x3, waiting for transfers between devices: 13.7 us -> 17.6 us  [shards(): lax.ppermute(query_z, 'y', ring(NY, k))]
  transfers between devices with their start and end apart: 23 -> 19, of which waited for: 18 -> 12; matrix products, arithmetic and copies ran while one was open for 4% -> 1% of each run, Pallas kernels for 13% -> 12%
where the time goes in v3:
time: 241 us; the launch traced here: 240 us
  waiting for transfers between devices  128 us (53%)
  starting transfers between devices  48 us (20%)
  Pallas kernels  38.9 us (16%)
  between operations  14.3 us (6%)
  local copies, waits for them, and re-layouts  10.6 us (4%)
    all_to_all x3, waiting for transfers between devices, swap_z(): return lax.all_to_all(values, 'z', split_axis=0, concat_axis=0, tiled=True)  54.5 us
    all_gather x1, waiting for transfers between devices, shards(): gathered = lax.all_gather(rest, ('x', 'core', 'y'))  28.6 us
    ppermute x7, waiting for transfers between devices, shards(): lax.ppermute(packed, 'z', ring(NZ, k))  21.2 us
    ppermute x3, waiting for transfers between devices, shards(): lax.ppermute(query_z, 'y', ring(NY, k))  17.6 us
    all_to_all x3, starting transfers between devices, swap_z(): return lax.all_to_all(values, 'z', split_axis=0, concat_axis=0, tiled=True)  17.6 us
    ppermute x7, starting transfers between devices, shards(): lax.ppermute(packed, 'z', ring(NZ, k))  17.2 us
    pallas_call x1, Pallas kernels, own(): pl.pallas_call(functools.partial(own_kernel, scale), grid=(steps,), in_sp...  12.5 us
    unnamed x29, local copies, waits for them, and re-layouts  9.14 us
  transfers between devices with their start and end apart: 19, of which 12 were waited for; matrix products, arithmetic and copies ran while one was open for 1% of the time, Pallas kernels for 12%

profile of v3, /device:TPU:1, one launch (start us, length us, event | category | flops | bytes accessed | tf_op | source)
XLA Modules:
  0.0 240.3 jit_solution(9461477319356551614)
XLA Ops:
  9.3 2.2 prep.1
  11.5 9.1 %all-to-all-start = ((bf16[8,768,128]{2,1,0:T(8,128)(2,1)}), bf16[8,768,128]{2,1,0:T(8,128)(2,1)}, u32[]{:S(2)}, u32[]{:S(2)}) async-start(bf16[8,768,128]{2,1,0:T(8,128)(2,1)} %prep.1), calls=%async_computation | async-start | bytes 3145728 | tf_op jit(solution)/shard_map/all_to_all | solution.py:262
  20.7 4.4 %collective-permute-start.2 = (bf16[20,1024]{1,0:T(8,128)(2,1)S(1)}, bf16[20,1024]{1,0:T(8,128)(2,1)S(1)}, u32[]{:S(2)}, u32[]{:S(2)}) collective-permute-start(bf16[20,1024]{1,0:T(8,128)(2,1)S(1)} %pad_maximum_fusion.1), channel_id=1, source_target_pairs={{0,192},{192,0},{1,193},{193,1},{2,194},{194,2},{3,195},{195,3},{4... | collective-permute-start | bytes 122888 | tf_op jit(solution)/shard_map/ppermute | solution.py:287
  25.1 1.9 collective-permute-start.1
  27.0 1.9 collective-permute-start
  29.0 2.8 %collective-permute-done.1 = bf16[20,1024]{1,0:T(8,128)(2,1)S(1)} collective-permute-done((bf16[20,1024]{1,0:T(8,128)(2,1)S(1)}, bf16[20,1024]{1,0:T(8,128)(2,1)S(1)}, u32[]{:S(2)}, u32[]{:S(2)}) %collective-permute-start.1) | collective-permute-done | bytes 40992 | tf_op jit(solution)/shard_map/ppermute | solution.py:287
  33.8 2.1 collective-permute-start.4
  35.9 2.4 collective-permute-start.5
  38.3 2.1 collective-permute-start.6
  40.4 2.4 collective-permute-start.7
  42.8 10.8 %collective-permute-done.3 = bf16[40,1024]{1,0:T(8,128)(2,1)S(1)} collective-permute-done((bf16[40,1024]{1,0:T(8,128)(2,1)S(1)}, bf16[40,1024]{1,0:T(8,128)(2,1)S(1)}, u32[]{:S(2)}, u32[]{:S(2)}) %collective-permute-start.3) | collective-permute-done | bytes 81952 | tf_op jit(solution)/shard_map/ppermute | solution.py:293
  53.5 5.2 %collective-permute-start.8 = (bf16[40,1024]{1,0:T(8,128)(2,1)S(1)}, bf16[40,1024]{1,0:T(8,128)(2,1)S(1)}, u32[]{:S(2)}, u32[]{:S(2)}) collective-permute-start(bf16[40,1024]{1,0:T(8,128)(2,1)S(1)} %fusion.1), channel_id=1, source_target_pairs={{0,6},{1,7},{2,0},{3,1},{4,2},{5,3},{6,4},{7,5},{8,14},{9,15},{10,... | collective-permute-start | bytes 245768 | tf_op jit(solution)/shard_map/ppermute | solution.py:293
  58.7 3.9 %collective-permute-done.4 = bf16[40,1024]{1,0:T(8,128)(2,1)S(1)} collective-permute-done((bf16[40,1024]{1,0:T(8,128)(2,1)S(1)}, bf16[40,1024]{1,0:T(8,128)(2,1)S(1)}, u32[]{:S(2)}, u32[]{:S(2)}) %collective-permute-start.4) | collective-permute-done | bytes 81952 | tf_op jit(solution)/shard_map/ppermute | solution.py:293
  62.6 1.5 collective-permute-start.9
  64.2 1.6 copy-done.2
  67.0 6.5 %collective-permute-done.6 = bf16[40,1024]{1,0:T(8,128)(2,1)S(1)} collective-permute-done((bf16[40,1024]{1,0:T(8,128)(2,1)S(1)}, bf16[40,1024]{1,0:T(8,128)(2,1)S(1)}, u32[]{:S(2)}, u32[]{:S(2)}) %collective-permute-start.6) | collective-permute-done | bytes 81952 | tf_op jit(solution)/shard_map/ppermute | solution.py:293
  75.2 2.7 %collective-permute-start.12 = (bf16[128,1024]{1,0:T(8,128)(2,1)S(1)}, bf16[128,1024]{1,0:T(8,128)(2,1)S(1)}, u32[]{:S(2)}, u32[]{:S(2)}) collective-permute-start(bf16[128,1024]{1,0:T(8,128)(2,1)S(1)} %bitcast.35), channel_id=1, source_target_pairs={{0,24},{8,0},{16,8},{24,16},{1,25},{9,1},{17,9},{25,17},{2,26},{10... | collective-permute-start | bytes 786440 | tf_op jit(solution)/shard_map/ppermute | solution.py:301
  79.0 4.5 %collective-permute-done.12 = bf16[128,1024]{1,0:T(8,128)(2,1)S(1)} collective-permute-done((bf16[128,1024]{1,0:T(8,128)(2,1)S(1)}, bf16[128,1024]{1,0:T(8,128)(2,1)S(1)}, u32[]{:S(2)}, u32[]{:S(2)}) %collective-permute-start.12) | collective-permute-done | bytes 262176 | tf_op jit(solution)/shard_map/ppermute | solution.py:301
  83.6 1.5 collective-permute-done.11
  85.1 11.6 %collective-permute-done.10 = bf16[128,1024]{1,0:T(8,128)(2,1)S(1)} collective-permute-done((bf16[128,1024]{1,0:T(8,128)(2,1)S(1)}, bf16[128,1024]{1,0:T(8,128)(2,1)S(1)}, u32[]{:S(2)}, u32[]{:S(2)}) %collective-permute-start.10) | collective-permute-done | bytes 262176 | tf_op jit(solution)/shard_map/ppermute | solution.py:301
  97.9 2.3 collective-permute-done.13.other_ref
  100.3 4.1 %query.1.query_ref = bf16[8,1024,128]{2,1,0:T(8,128)(2,1)S(1)} custom-call(s32[8]{0:T(128)S(1)} %pad_add_fusion.slot_ref, bf16[1024,1024]{1,0:T(8,128)(2,1)S(1)} %norm.1.rows_ref, bf16[512,1024]{1,0:T(8,128)(2,1)S(1)} %pad_maximum_fusion.mine_ref, bf16[512,1024]{1,0:T(8,128)(2,1)} %collective-permute-done.13.other_ref), custom_call_target="tpu_custom_call" | custom-call | tf_op jit(solution)/shard_map/query/pallas_call | solution.py:104
  105.7 3.6 %all-to-all-start.1 = ((bf16[8,1024,128]{2,1,0:T(8,128)(2,1)}), bf16[8,1024,128]{2,1,0:T(8,128)(2,1)S(1)}, u32[]{:S(2)}, u32[]{:S(2)}) async-start(bf16[8,1024,128]{2,1,0:T(8,128)(2,1)} %copy-done.1), calls=%async_computation.1 | async-start | bytes 4194304 | tf_op jit(solution)/shard_map/all_to_all | solution.py:262
  110.1 47.5 %all-to-all-done.1.query_ref = bf16[8,1024,128]{2,1,0:T(8,128)(2,1)S(1)} async-done(((bf16[8,1024,128]{2,1,0:T(8,128)(2,1)}), bf16[8,1024,128]{2,1,0:T(8,128)(2,1)S(1)}, u32[]{:S(2)}, u32[]{:S(2)}) %all-to-all-start.1) | async-done | bytes 2097184 | tf_op jit(solution)/shard_map/all_to_all | solution.py:262
  157.6 2.8 %copy-done.3 = bf16[32,768,128]{2,1,0:T(8,128)(2,1)S(1)} copy-done((bf16[32,768,128]{2,1,0:T(8,128)(2,1)S(1)}, bf16[32,768,128]{2,1,0:T(8,128)(2,1)}, u32[]{:S(2)}) %copy-start.3) | copy-done | bytes 6291480
  160.3 7.6 %attend.1 = bf16[8,1024,128]{2,1,0:T(8,128)(2,1)} custom-call(s32[8,16]{1,0:T(8,128)S(1)} %bitcast.29, bf16[8,1024,128]{2,1,0:T(8,128)(2,1)S(1)} %all-to-all-done.1.query_ref, bf16[32,768,128]{2,1,0:T(8,128)(2,1)S(1)} %copy-done.3), custom_call_target="tpu_custom_call" | custom-call | tf_op jit(solution)/shard_map/attend/pallas_call | solution.py:139
  167.9 4.8 %all-to-all-start.2 = ((bf16[8,1024,128]{2,1,0:T(8,128)(2,1)}), bf16[8,1024,128]{2,1,0:T(8,128)(2,1)S(1)}, u32[]{:S(2)}, u32[]{:S(2)}) async-start(bf16[8,1024,128]{2,1,0:T(8,128)(2,1)} %attend.1), calls=%async_computation.2 | async-start | bytes 4194304 | tf_op jit(solution)/shard_map/all_to_all | solution.py:262
  172.8 28.6 %all-gather.6.cloned.1.call-done = bf16[4096,1024]{1,0:T(8,128)(2,1)} async-done(((bf16[128,1024]{1,0:T(8,128)(2,1)}), bf16[4096,1024]{1,0:T(8,128)(2,1)}) %all-gather.6.cloned.1.call-update) | async-done | bytes 8388624 | tf_op jit(solution)/shard_map/all_gather | solution.py:310
  201.3 12.5 %own.1 = (f32[1024,1024]{1,0:T(8,128)}, bf16[1024,1024]{1,0:T(8,128)(2,1)}) custom-call(bf16[1024,1024]{1,0:T(8,128)(2,1)} %copy-done, bf16[8,1024,128]{2,1,0:T(8,128)(2,1)} %copy-done.1, bf16[32,128,1024]{2,1,0:T(8,128)(2,1)} %bitcast.30, bf16[32,128,1024]{2,1,0:T(8,128)(2,1)} %bitcast.31, bf16[32,128,1024]{2,1,0:T(8,128)(2,1)} %bitcast.32), custom_call_target="tpu_custom_call" | custom-call | tf_op jit(solution)/shard_map/own/pallas_call | solution.py:175
  213.8 3.6 %turn.1.out_w = bf16[1024,1024]{1,0:T(8,128)(2,1)} custom-call(bf16[32,128,1024]{2,1,0:T(8,128)(2,1)} %bitcast.33), custom_call_target="tpu_custom_call" | custom-call | tf_op jit(solution)/shard_map/turn/pallas_call | solution.py:212
  217.4 7.0 %all-to-all-done.2.hist_ref = bf16[8,1024,128]{2,1,0:T(8,128)(2,1)S(1)} async-done(((bf16[8,1024,128]{2,1,0:T(8,128)(2,1)}), bf16[8,1024,128]{2,1,0:T(8,128)(2,1)S(1)}, u32[]{:S(2)}, u32[]{:S(2)}) %all-to-all-start.2) | async-done | bytes 2097184 | tf_op jit(solution)/shard_map/all_to_all | solution.py:262
  225.7 7.7 %finish.1 = bf16[1024,1024]{1,0:T(8,128)(2,1)} custom-call(s32[16]{0:T(128)} %count_ref.1, bf16[8,1024,128]{2,1,0:T(8,128)(2,1)} %copy-done.6, f32[1024,1024]{1,0:T(8,128)} %get-tuple-element.43.own_ref, bf16[1024,1024]{1,0:T(8,128)(2,1)} %get-tuple-element.44.gate_ref, bf16[1024,1024]{1,0:T(8,128)(2,1)} %turn.1.out_w, bf16[1024,1024]{1,0:T(8,128)(2,1)} %rows_ref.3), custom_call_target="tpu_custom_call" | custom-call | tf_op jit(solution)/shard_map/finish/pallas_call | solution.py:243
  (60 shorter events, 12.6 us)
Async XLA Ops:
  7.2 1.4 copy-start.4
  8.6 0.7 copy-start.5
  11.4 9.2 %copy-start.8 = (bf16[1024,16]{0,1:T(8,128)(2,1)S(1)}, bf16[1024,16]{0,1:T(8,128)(2,1)}, u32[]{:S(2)}) copy-start(bf16[1024,16]{0,1:T(8,128)(2,1)} %param.16) | copy-start | bytes 98308
  11.5 9.2 %copy-start.9 = (bf16[4,1024]{1,0:T(4,128)(2,1)S(1)}, bf16[4,1024]{1,0:T(4,128)(2,1)}, u32[]{:S(2)}) copy-start(bf16[4,1024]{1,0:T(4,128)(2,1)} %param.17) | copy-start | bytes 24580
  11.5 17.5 %copy-start.10 = (s32[16,1]{0,1:T(1,128)S(1)}, s32[16,1]{0,1:T(1,128)}, u32[]{:S(2)}) copy-start(s32[16,1]{0,1:T(1,128)} %param.14) | copy-start | bytes 196
  11.5 62.1 %all-to-all-start = ((bf16[8,768,128]{2,1,0:T(8,128)(2,1)}), bf16[8,768,128]{2,1,0:T(8,128)(2,1)}, u32[]{:S(2)}, u32[]{:S(2)}) async-start(bf16[8,768,128]{2,1,0:T(8,128)(2,1)} %prep.1), calls=%async_computation | async-start | bytes 3145728 | tf_op jit(solution)/shard_map/all_to_all | solution.py:262
  20.6 137.0 %all-gather.4.cloned.1.call-start = ((), (), s32[]{:S(2)}) async-start(), calls=%async_computation.3 | async-start | bytes 7864320 | tf_op jit(solution)/shard_map/all_gather | solution.py:295
  20.7 8.3 %collective-permute-start.2 = (bf16[20,1024]{1,0:T(8,128)(2,1)S(1)}, bf16[20,1024]{1,0:T(8,128)(2,1)S(1)}, u32[]{:S(2)}, u32[]{:S(2)}) collective-permute-start(bf16[20,1024]{1,0:T(8,128)(2,1)S(1)} %pad_maximum_fusion.1), channel_id=1, source_target_pairs={{0,192},{192,0},{1,193},{193,1},{2,194},{194,2},{3,195},{195,3},{4... | collective-permute-start | bytes 122888 | tf_op jit(solution)/shard_map/ppermute | solution.py:287
  25.1 6.7 %collective-permute-start.1 = (bf16[20,1024]{1,0:T(8,128)(2,1)S(1)}, bf16[20,1024]{1,0:T(8,128)(2,1)S(1)}, u32[]{:S(2)}, u32[]{:S(2)}) collective-permute-start(bf16[20,1024]{1,0:T(8,128)(2,1)S(1)} %pad_maximum_fusion.1), channel_id=1, source_target_pairs={{0,128},{128,0},{1,129},{129,1},{2,130},{130,2},{3,131},{131,3},{4... | collective-permute-start | bytes 122888 | tf_op jit(solution)/shard_map/ppermute | solution.py:287
  27.0 5.2 %collective-permute-start = (bf16[20,1024]{1,0:T(8,128)(2,1)S(1)}, bf16[20,1024]{1,0:T(8,128)(2,1)S(1)}, u32[]{:S(2)}, u32[]{:S(2)}) collective-permute-start(bf16[20,1024]{1,0:T(8,128)(2,1)S(1)} %pad_maximum_fusion.1), channel_id=1, source_target_pairs={{0,64},{64,0},{1,65},{65,1},{2,66},{66,2},{3,67},{67,3},{4,68},{68... | collective-permute-start | bytes 122888 | tf_op jit(solution)/shard_map/ppermute | solution.py:287
  32.3 21.2 %collective-permute-start.3 = (bf16[40,1024]{1,0:T(8,128)(2,1)S(1)}, bf16[40,1024]{1,0:T(8,128)(2,1)S(1)}, u32[]{:S(2)}, u32[]{:S(2)}) collective-permute-start(bf16[40,1024]{1,0:T(8,128)(2,1)S(1)} %fusion.1), channel_id=1, source_target_pairs={{0,1},{1,2},{2,3},{3,4},{4,5},{5,6},{6,7},{7,0},{8,9},{9,10},{10,1... | collective-permute-start | bytes 245768 | tf_op jit(solution)/shard_map/ppermute | solution.py:293
  33.8 28.8 %collective-permute-start.4 = (bf16[40,1024]{1,0:T(8,128)(2,1)S(1)}, bf16[40,1024]{1,0:T(8,128)(2,1)S(1)}, u32[]{:S(2)}, u32[]{:S(2)}) collective-permute-start(bf16[40,1024]{1,0:T(8,128)(2,1)S(1)} %fusion.1), channel_id=1, source_target_pairs={{0,2},{1,3},{2,4},{3,5},{4,6},{5,7},{6,0},{7,1},{8,10},{9,11},{10,... | collective-permute-start | bytes 245768 | tf_op jit(solution)/shard_map/ppermute | solution.py:293
  35.9 31.1 %collective-permute-start.5 = (bf16[40,1024]{1,0:T(8,128)(2,1)S(1)}, bf16[40,1024]{1,0:T(8,128)(2,1)S(1)}, u32[]{:S(2)}, u32[]{:S(2)}) collective-permute-start(bf16[40,1024]{1,0:T(8,128)(2,1)S(1)} %fusion.1), channel_id=1, source_target_pairs={{0,3},{1,4},{2,5},{3,6},{4,7},{5,0},{6,1},{7,2},{8,11},{9,12},{10,... | collective-permute-start | bytes 245768 | tf_op jit(solution)/shard_map/ppermute | solution.py:293
  38.3 35.3 %collective-permute-start.6 = (bf16[40,1024]{1,0:T(8,128)(2,1)S(1)}, bf16[40,1024]{1,0:T(8,128)(2,1)S(1)}, u32[]{:S(2)}, u32[]{:S(2)}) collective-permute-start(bf16[40,1024]{1,0:T(8,128)(2,1)S(1)} %fusion.1), channel_id=1, source_target_pairs={{0,4},{1,5},{2,6},{3,7},{4,0},{5,1},{6,2},{7,3},{8,12},{9,13},{10,... | collective-permute-start | bytes 245768 | tf_op jit(solution)/shard_map/ppermute | solution.py:293
  40.4 33.2 %collective-permute-start.7 = (bf16[40,1024]{1,0:T(8,128)(2,1)S(1)}, bf16[40,1024]{1,0:T(8,128)(2,1)S(1)}, u32[]{:S(2)}, u32[]{:S(2)}) collective-permute-start(bf16[40,1024]{1,0:T(8,128)(2,1)S(1)} %fusion.1), channel_id=1, source_target_pairs={{0,5},{1,6},{2,7},{3,0},{4,1},{5,2},{6,3},{7,4},{8,13},{9,14},{10,... | collective-permute-start | bytes 245768 | tf_op jit(solution)/shard_map/ppermute | solution.py:293
  53.5 20.0 %collective-permute-start.8 = (bf16[40,1024]{1,0:T(8,128)(2,1)S(1)}, bf16[40,1024]{1,0:T(8,128)(2,1)S(1)}, u32[]{:S(2)}, u32[]{:S(2)}) collective-permute-start(bf16[40,1024]{1,0:T(8,128)(2,1)S(1)} %fusion.1), channel_id=1, source_target_pairs={{0,6},{1,7},{2,0},{3,1},{4,2},{5,3},{6,4},{7,5},{8,14},{9,15},{10,... | collective-permute-start | bytes 245768 | tf_op jit(solution)/shard_map/ppermute | solution.py:293
  62.6 10.9 %collective-permute-start.9 = (bf16[40,1024]{1,0:T(8,128)(2,1)S(1)}, bf16[40,1024]{1,0:T(8,128)(2,1)S(1)}, u32[]{:S(2)}, u32[]{:S(2)}) collective-permute-start(bf16[40,1024]{1,0:T(8,128)(2,1)S(1)} %fusion.1), channel_id=1, source_target_pairs={{0,7},{1,0},{2,1},{3,2},{4,3},{5,4},{6,5},{7,6},{8,15},{9,8},{10,9... | collective-permute-start | bytes 245768 | tf_op jit(solution)/shard_map/ppermute | solution.py:293
  64.2 1.6 copy-start.2
  67.0 33.3 %copy-start = (bf16[1024,1024]{1,0:T(8,128)(2,1)}, bf16[1024,1024]{1,0:T(8,128)(2,1)S(1)}, u32[]{:S(2)}) copy-start(bf16[1024,1024]{1,0:T(8,128)(2,1)S(1)} %norm.1.rows_ref) | copy-start | bytes 6291460
  73.6 127.7 %all-gather.6.cloned.1.call-start = ((), (), s32[]{:S(2)}) async-start(), calls=%async_computation.4 | async-start | bytes 8650752 | tf_op jit(solution)/shard_map/all_gather | solution.py:310
  74.4 10.7 %copy-start.7 = (bf16[8,40,1024]{2,1,0:T(8,128)(2,1)}, bf16[8,40,1024]{2,1,0:T(8,128)(2,1)S(1)}, u32[]{:S(2)}) copy-start(bf16[8,40,1024]{2,1,0:T(8,128)(2,1)S(1)} %gather_fusion) | copy-start | bytes 1966084
  75.2 8.3 %collective-permute-start.12 = (bf16[128,1024]{1,0:T(8,128)(2,1)S(1)}, bf16[128,1024]{1,0:T(8,128)(2,1)S(1)}, u32[]{:S(2)}, u32[]{:S(2)}) collective-permute-start(bf16[128,1024]{1,0:T(8,128)(2,1)S(1)} %bitcast.35), channel_id=1, source_target_pairs={{0,24},{8,0},{16,8},{24,16},{1,25},{9,1},{17,9},{25,17},{2,26},{10... | collective-permute-start | bytes 786440 | tf_op jit(solution)/shard_map/ppermute | solution.py:301
  78.0 7.1 %collective-permute-start.11 = (bf16[128,1024]{1,0:T(8,128)(2,1)S(1)}, bf16[128,1024]{1,0:T(8,128)(2,1)S(1)}, u32[]{:S(2)}, u32[]{:S(2)}) collective-permute-start(bf16[128,1024]{1,0:T(8,128)(2,1)S(1)} %bitcast.36), channel_id=1, source_target_pairs={{0,16},{8,24},{16,0},{24,8},{1,17},{9,25},{17,1},{25,9},{2,18},{10... | collective-permute-start | bytes 786440 | tf_op jit(solution)/shard_map/ppermute | solution.py:301
  78.3 18.3 %collective-permute-start.10 = (bf16[128,1024]{1,0:T(8,128)(2,1)S(1)}, bf16[128,1024]{1,0:T(8,128)(2,1)S(1)}, u32[]{:S(2)}, u32[]{:S(2)}) collective-permute-start(bf16[128,1024]{1,0:T(8,128)(2,1)S(1)} %bitcast.37), channel_id=1, source_target_pairs={{0,8},{8,16},{16,24},{24,0},{1,9},{9,17},{17,25},{25,1},{2,10},{10... | collective-permute-start | bytes 786440 | tf_op jit(solution)/shard_map/ppermute | solution.py:301
  96.7 3.5 %collective-permute-start.13 = (bf16[512,1024]{1,0:T(8,128)(2,1)S(1)}, bf16[512,1024]{1,0:T(8,128)(2,1)}, u32[]{:S(2)}, u32[]{:S(2)}) collective-permute-start(bf16[512,1024]{1,0:T(8,128)(2,1)S(1)} %pad_maximum_fusion.mine_ref), channel_id=1, source_target_pairs={{0,32},{32,0},{1,33},{33,1},{2,34},{34,2},{3,35},{35,3},{4,36},{36... | collective-permute-start | bytes 3145736 | tf_op jit(solution)/shard_map/ppermute | solution.py:303
  104.4 1.3 copy-start.1
  105.7 51.9 %all-to-all-start.1 = ((bf16[8,1024,128]{2,1,0:T(8,128)(2,1)}), bf16[8,1024,128]{2,1,0:T(8,128)(2,1)S(1)}, u32[]{:S(2)}, u32[]{:S(2)}) async-start(bf16[8,1024,128]{2,1,0:T(8,128)(2,1)} %copy-done.1), calls=%async_computation.1 | async-start | bytes 4194304 | tf_op jit(solution)/shard_map/all_to_all | solution.py:262
  157.6 2.8 %copy-start.3 = (bf16[32,768,128]{2,1,0:T(8,128)(2,1)S(1)}, bf16[32,768,128]{2,1,0:T(8,128)(2,1)}, u32[]{:S(2)}) copy-start(bf16[32,768,128]{2,1,0:T(8,128)(2,1)} %all-gather.4.cloned.1.call-done.cache_ref) | copy-start | bytes 18874372
  167.9 56.5 %all-to-all-start.2 = ((bf16[8,1024,128]{2,1,0:T(8,128)(2,1)}), bf16[8,1024,128]{2,1,0:T(8,128)(2,1)S(1)}, u32[]{:S(2)}, u32[]{:S(2)}) async-start(bf16[8,1024,128]{2,1,0:T(8,128)(2,1)} %attend.1), calls=%async_computation.2 | async-start | bytes 4194304 | tf_op jit(solution)/shard_map/all_to_all | solution.py:262
  224.4 1.3 copy-start.6
Sparse Core Ops, SparseCore 0:
  73.7 70.5 all-gather.3
  146.8 54.4 all-gather.5

commit v4 on v3

--- a/solution.py
+++ b/solution.py
@@ -13,7 +13,7 @@
 BLK = 128
 HIST = 384
 TILE = 64
-META = 8
+META = 16
 PIECE = 512
 NX, NC, NY, NZ = 4, 2, 4, 8
 BF = jnp.bfloat16
@@ -34,7 +34,7 @@
     return [(i, (i + step) % size) for i in range(size)]
 
 
-def prep_kernel(len_ref, mask_ref, hist_ref, out_ref):
+def prep_kernel(len_ref, mask_ref, hist_ref, meta_ref, out_ref):
     place = lax.broadcasted_iota(jnp.int32, (HIST, HEAD), 0)
     kept = jnp.where(
         place < BLK, mask_ref[0, 0], jnp.where(place < 2 * BLK, mask_ref[0, 1], mask_ref[0, 2])
@@ -47,20 +47,21 @@
             turned = hist_ref[b : b + BLK, cut].astype(F32).T
             out_ref[h, b : b + BLK, :] = turned.astype(BF)
         values = hist_ref[:, width + h * HEAD : width + (h + 1) * HEAD].astype(F32)
-        out_ref[h, HIST:, :] = jnp.where(live, values, 0.0).astype(BF)
-
-
-def prep(hist, hist_len, block_mask):
+        out_ref[h, HIST : 2 * HIST, :] = jnp.where(live, values, 0.0).astype(BF)
+        out_ref[h, 2 * HIST :, :] = meta_ref[...]
+
+
+def prep(hist, hist_len, block_mask, meta):
     smem = pl.BlockSpec(memory_space=pltpu.SMEM)
     vmem = pl.BlockSpec(memory_space=pltpu.VMEM)
     return pl.pallas_call(
         prep_kernel,
-        in_specs=[smem, smem, vmem],
+        in_specs=[smem, smem, vmem, vmem],
         out_specs=vmem,
-        out_shape=jax.ShapeDtypeStruct((HEADS, 2 * HIST, HEAD), BF),
+        out_shape=jax.ShapeDtypeStruct((HEADS, 2 * HIST + META, HEAD), BF),
         compiler_params=params(),
         name="prep",
-    )(hist_len, block_mask, hist)
+    )(hist_len, block_mask, hist, meta)
 
 
 def norm_kernel(rows_ref, out_ref):
@@ -126,11 +127,11 @@
             weights.append(half_silu(score * (0.5 * scale)).astype(BF))
         for s, u in enumerate(users):
             out_ref[s, here, :] = jnp.dot(
-                weights[s], cache_ref[u, HIST:, :], preferred_element_type=F32
+                weights[s], cache_ref[u, HIST : 2 * HIST, :], preferred_element_type=F32
             ).astype(BF)
         return carry
 
-    lax.fori_loop(0, rows // TILE, step, 0, unroll=2)
+    lax.fori_loop(0, rows // TILE, step, 0, unroll=4)
 
 
 def attend(users, queries, caches, scale):
@@ -282,20 +283,20 @@
     columns = weight_in.T
     share, out_share = columns.shape[0], weight_out.shape[0]
     normed = norm(candidates)
-    caches = swap_z(prep(hist_kv[0], hist_len, block_mask))
+    meta = jnp.zeros((META, HEAD), BF).at[0, :tiles].set(tile_user[:, 0].astype(BF))
+    caches = swap_z(prep(hist_kv[0], hist_len, block_mask, meta))
     both = jnp.concatenate([columns, weight_out], axis=0)
     sent = [lax.ppermute(both, "x", [(0, k), (k, 0)]) for k in range(1, NX)]
     query_part = jnp.where(at_x == 0, columns, sent[0][:share] + sent[1][:share] + sent[2][:share])
     out_part = jnp.concatenate([weight_out] + [piece[share:] for piece in sent], axis=0)
     rest_part = jnp.where(at_x == 0, out_part, columns)
-    meta = jnp.zeros((META, width), BF).at[0, :tiles].set(tile_user[:, 0].astype(BF))
-    packed = jnp.concatenate([query_part, rest_part, meta], axis=0)
+    packed = jnp.concatenate([query_part, rest_part], axis=0)
     spread = [packed] + [lax.ppermute(packed, "z", ring(NZ, k)) for k in range(1, NZ)]
     spread, caches, normed = lax.optimization_barrier((spread, caches, normed))
+    users = caches[:, 2 * HIST, :tiles].astype(jnp.int32)
     caches = lax.all_gather(caches, "y", axis=0, tiled=True)
     spread = jnp.stack(spread)[(at_z - jnp.arange(NZ, dtype=jnp.int32)) % NZ]
     query_z = spread[:, :share].reshape(NZ * share, width)
-    users = spread[:, 2 * share, :tiles].astype(jnp.int32)
     rest = spread[:, share : 2 * share].reshape(NZ * share, width)
 
     parts = [query_z] + [lax.ppermute(query_z, "y", ring(NY, k)) for k in range(1, NY)]

time: 241 us -> 240 us (level)
    ppermute x7, waiting for transfers between devices: 21.2 us -> 18.7 us  [shards(): lax.ppermute(packed, 'z', ring(NZ, k))]
    unnamed x29 -> x25, local copies, waits for them, and re-layouts: 9.14 us -> 9.14 us
where the time goes in v4:
time: 240 us; the launch traced here: 239 us
  waiting for transfers between devices  126 us (52%)
  starting transfers between devices  48.7 us (20%)
  Pallas kernels  38.4 us (16%)
  between operations  14.3 us (6%)
  local copies, waits for them, and re-layouts  10.5 us (4%)
    all_to_all x3, waiting for transfers between devices, swap_z(): return lax.all_to_all(values, 'z', split_axis=0, concat_axis=0, tiled=True)  53.6 us
    all_gather x1, waiting for transfers between devices, shards(): gathered = lax.all_gather(rest, ('x', 'core', 'y'))  29.4 us
    ppermute x7, waiting for transfers between devices, shards(): lax.ppermute(packed, 'z', ring(NZ, k))  18.7 us
    ppermute x3, waiting for transfers between devices, shards(): lax.ppermute(query_z, 'y', ring(NY, k))  18.3 us
    ppermute x7, starting transfers between devices, shards(): lax.ppermute(packed, 'z', ring(NZ, k))  18.2 us
    all_to_all x3, starting transfers between devices, swap_z(): return lax.all_to_all(values, 'z', split_axis=0, concat_axis=0, tiled=True)  17.6 us
    pallas_call x1, Pallas kernels, own(): pl.pallas_call(functools.partial(own_kernel, scale), grid=(steps,), in_sp...  12.5 us
    unnamed x25, local copies, waits for them, and re-layouts  9.14 us
  transfers between devices with their start and end apart: 19, of which 12 were waited for; matrix products, arithmetic and copies ran while one was open for 1% of the time, Pallas kernels for 12%

profile of v4, /device:TPU:1, one launch (start us, length us, event | category | flops | bytes accessed | tf_op | source)
XLA Modules:
  0.0 239.1 jit_solution(11182462976286213957)
XLA Ops:
  9.9 2.2 prep.1
  12.1 9.1 %all-to-all-start = ((bf16[8,784,128]{2,1,0:T(8,128)(2,1)}), bf16[8,784,128]{2,1,0:T(8,128)(2,1)}, u32[]{:S(2)}, u32[]{:S(2)}) async-start(bf16[8,784,128]{2,1,0:T(8,128)(2,1)} %prep.1), calls=%async_computation | async-start | bytes 3211264 | tf_op jit(solution)/shard_map/all_to_all | solution.py:263
  21.4 4.4 %collective-permute-start.2 = (bf16[20,1024]{1,0:T(8,128)(2,1)S(1)}, bf16[20,1024]{1,0:T(8,128)(2,1)S(1)}, u32[]{:S(2)}, u32[]{:S(2)}) collective-permute-start(bf16[20,1024]{1,0:T(8,128)(2,1)S(1)} %pad_maximum_fusion.2), channel_id=1, source_target_pairs={{0,192},{192,0},{1,193},{193,1},{2,194},{194,2},{3,195},{195,3},{4... | collective-permute-start | bytes 122888 | tf_op jit(solution)/shard_map/ppermute | solution.py:289
  25.8 1.9 collective-permute-start.1
  27.7 1.9 collective-permute-start
  29.6 2.8 %collective-permute-done.1 = bf16[20,1024]{1,0:T(8,128)(2,1)S(1)} collective-permute-done((bf16[20,1024]{1,0:T(8,128)(2,1)S(1)}, bf16[20,1024]{1,0:T(8,128)(2,1)S(1)}, u32[]{:S(2)}, u32[]{:S(2)}) %collective-permute-start.1) | collective-permute-done | bytes 40992 | tf_op jit(solution)/shard_map/ppermute | solution.py:289
  34.5 2.1 collective-permute-start.4
  36.6 2.4 %collective-permute-start.5 = (bf16[32,1024]{1,0:T(8,128)(2,1)S(1)}, bf16[32,1024]{1,0:T(8,128)(2,1)S(1)}, u32[]{:S(2)}, u32[]{:S(2)}) collective-permute-start(bf16[32,1024]{1,0:T(8,128)(2,1)S(1)} %pad_maximum_fusion.1), channel_id=1, source_target_pairs={{0,3},{1,4},{2,5},{3,6},{4,7},{5,0},{6,1},{7,2},{8,11},{9,12},{10,... | collective-permute-start | bytes 196616 | tf_op jit(solution)/shard_map/ppermute | solution.py:294
  39.0 2.1 collective-permute-start.6
  41.0 2.4 %collective-permute-start.7 = (bf16[32,1024]{1,0:T(8,128)(2,1)S(1)}, bf16[32,1024]{1,0:T(8,128)(2,1)S(1)}, u32[]{:S(2)}, u32[]{:S(2)}) collective-permute-start(bf16[32,1024]{1,0:T(8,128)(2,1)S(1)} %pad_maximum_fusion.1), channel_id=1, source_target_pairs={{0,5},{1,6},{2,7},{3,0},{4,1},{5,2},{6,3},{7,4},{8,13},{9,14},{10,... | collective-permute-start | bytes 196616 | tf_op jit(solution)/shard_map/ppermute | solution.py:294
  43.4 11.1 %collective-permute-done.3 = bf16[32,1024]{1,0:T(8,128)(2,1)S(1)} collective-permute-done((bf16[32,1024]{1,0:T(8,128)(2,1)S(1)}, bf16[32,1024]{1,0:T(8,128)(2,1)S(1)}, u32[]{:S(2)}, u32[]{:S(2)}) %collective-permute-start.3) | collective-permute-done | bytes 65568 | tf_op jit(solution)/shard_map/ppermute | solution.py:294
  54.6 5.2 %collective-permute-start.8 = (bf16[32,1024]{1,0:T(8,128)(2,1)S(1)}, bf16[32,1024]{1,0:T(8,128)(2,1)S(1)}, u32[]{:S(2)}, u32[]{:S(2)}) collective-permute-start(bf16[32,1024]{1,0:T(8,128)(2,1)S(1)} %pad_maximum_fusion.1), channel_id=1, source_target_pairs={{0,6},{1,7},{2,0},{3,1},{4,2},{5,3},{6,4},{7,5},{8,14},{9,15},{10,... | collective-permute-start | bytes 196616 | tf_op jit(solution)/shard_map/ppermute | solution.py:294
  59.7 3.2 %collective-permute-done.4 = bf16[32,1024]{1,0:T(8,128)(2,1)S(1)} collective-permute-done((bf16[32,1024]{1,0:T(8,128)(2,1)S(1)}, bf16[32,1024]{1,0:T(8,128)(2,1)S(1)}, u32[]{:S(2)}, u32[]{:S(2)}) %collective-permute-start.4) | collective-permute-done | bytes 65568 | tf_op jit(solution)/shard_map/ppermute | solution.py:294
  63.0 2.5 %collective-permute-start.9 = (bf16[32,1024]{1,0:T(8,128)(2,1)S(1)}, bf16[32,1024]{1,0:T(8,128)(2,1)S(1)}, u32[]{:S(2)}, u32[]{:S(2)}) collective-permute-start(bf16[32,1024]{1,0:T(8,128)(2,1)S(1)} %pad_maximum_fusion.1), channel_id=1, source_target_pairs={{0,7},{1,0},{2,1},{3,2},{4,3},{5,4},{6,5},{7,6},{8,15},{9,8},{10,9... | collective-permute-start | bytes 196616 | tf_op jit(solution)/shard_map/ppermute | solution.py:294
  65.5 1.6 copy-done.2
  68.3 4.4 %collective-permute-done.6 = bf16[32,1024]{1,0:T(8,128)(2,1)S(1)} collective-permute-done((bf16[32,1024]{1,0:T(8,128)(2,1)S(1)}, bf16[32,1024]{1,0:T(8,128)(2,1)S(1)}, u32[]{:S(2)}, u32[]{:S(2)}) %collective-permute-start.6) | collective-permute-done | bytes 65568 | tf_op jit(solution)/shard_map/ppermute | solution.py:294
  74.3 2.7 %collective-permute-start.12 = (bf16[128,1024]{1,0:T(8,128)(2,1)S(1)}, bf16[128,1024]{1,0:T(8,128)(2,1)S(1)}, u32[]{:S(2)}, u32[]{:S(2)}) collective-permute-start(bf16[128,1024]{1,0:T(8,128)(2,1)S(1)} %bitcast.35), channel_id=1, source_target_pairs={{0,24},{8,0},{16,8},{24,16},{1,25},{9,1},{17,9},{25,17},{2,26},{10... | collective-permute-start | bytes 786440 | tf_op jit(solution)/shard_map/ppermute | solution.py:302
  78.1 4.1 %collective-permute-done.12 = bf16[128,1024]{1,0:T(8,128)(2,1)S(1)} collective-permute-done((bf16[128,1024]{1,0:T(8,128)(2,1)S(1)}, bf16[128,1024]{1,0:T(8,128)(2,1)S(1)}, u32[]{:S(2)}, u32[]{:S(2)}) %collective-permute-start.12) | collective-permute-done | bytes 262176 | tf_op jit(solution)/shard_map/ppermute | solution.py:302
  82.2 2.5 %collective-permute-done.11 = bf16[128,1024]{1,0:T(8,128)(2,1)S(1)} collective-permute-done((bf16[128,1024]{1,0:T(8,128)(2,1)S(1)}, bf16[128,1024]{1,0:T(8,128)(2,1)S(1)}, u32[]{:S(2)}, u32[]{:S(2)}) %collective-permute-start.11) | collective-permute-done | bytes 262176 | tf_op jit(solution)/shard_map/ppermute | solution.py:302
  84.7 11.7 %collective-permute-done.10 = bf16[128,1024]{1,0:T(8,128)(2,1)S(1)} collective-permute-done((bf16[128,1024]{1,0:T(8,128)(2,1)S(1)}, bf16[128,1024]{1,0:T(8,128)(2,1)S(1)}, u32[]{:S(2)}, u32[]{:S(2)}) %collective-permute-start.10) | collective-permute-done | bytes 262176 | tf_op jit(solution)/shard_map/ppermute | solution.py:302
  97.3 2.3 collective-permute-done.13.other_ref
  99.7 4.1 %query.1.query_ref = bf16[8,1024,128]{2,1,0:T(8,128)(2,1)S(1)} custom-call(s32[8]{0:T(128)S(1)} %pad_add_fusion.slot_ref, bf16[1024,1024]{1,0:T(8,128)(2,1)S(1)} %norm.1.rows_ref, bf16[512,1024]{1,0:T(8,128)(2,1)S(1)} %pad_maximum_fusion.mine_ref, bf16[512,1024]{1,0:T(8,128)(2,1)} %collective-permute-done.13.other_ref), custom_call_target="tpu_custom_call" | custom-call | tf_op jit(solution)/shard_map/query/pallas_call | solution.py:105
  105.1 3.6 %all-to-all-start.1 = ((bf16[8,1024,128]{2,1,0:T(8,128)(2,1)}), bf16[8,1024,128]{2,1,0:T(8,128)(2,1)S(1)}, u32[]{:S(2)}, u32[]{:S(2)}) async-start(bf16[8,1024,128]{2,1,0:T(8,128)(2,1)} %copy-done.1), calls=%async_computation.1 | async-start | bytes 4194304 | tf_op jit(solution)/shard_map/all_to_all | solution.py:263
  109.5 47.5 %all-to-all-done.1.query_ref = bf16[8,1024,128]{2,1,0:T(8,128)(2,1)S(1)} async-done(((bf16[8,1024,128]{2,1,0:T(8,128)(2,1)}), bf16[8,1024,128]{2,1,0:T(8,128)(2,1)S(1)}, u32[]{:S(2)}, u32[]{:S(2)}) %all-to-all-start.1) | async-done | bytes 2097184 | tf_op jit(solution)/shard_map/all_to_all | solution.py:263
  157.0 2.8 %copy-done.3 = bf16[32,784,128]{2,1,0:T(8,128)(2,1)S(1)} copy-done((bf16[32,784,128]{2,1,0:T(8,128)(2,1)S(1)}, bf16[32,784,128]{2,1,0:T(8,128)(2,1)}, u32[]{:S(2)}) %copy-start.3) | copy-done | bytes 6422552
  159.8 7.0 %attend.1 = bf16[8,1024,128]{2,1,0:T(8,128)(2,1)} custom-call(s32[8,16]{1,0:T(8,128)S(1)} %bitcast.29, bf16[8,1024,128]{2,1,0:T(8,128)(2,1)S(1)} %all-to-all-done.1.query_ref, bf16[32,784,128]{2,1,0:T(8,128)(2,1)S(1)} %copy-done.3), custom_call_target="tpu_custom_call" | custom-call | tf_op jit(solution)/shard_map/attend/pallas_call | solution.py:140
  166.8 4.8 %all-to-all-start.2 = ((bf16[8,1024,128]{2,1,0:T(8,128)(2,1)}), bf16[8,1024,128]{2,1,0:T(8,128)(2,1)S(1)}, u32[]{:S(2)}, u32[]{:S(2)}) async-start(bf16[8,1024,128]{2,1,0:T(8,128)(2,1)} %attend.1), calls=%async_computation.2 | async-start | bytes 4194304 | tf_op jit(solution)/shard_map/all_to_all | solution.py:263
  171.6 29.4 %all-gather.6.cloned.1.call-done = bf16[4096,1024]{1,0:T(8,128)(2,1)} async-done(((bf16[128,1024]{1,0:T(8,128)(2,1)}), bf16[4096,1024]{1,0:T(8,128)(2,1)}) %all-gather.6.cloned.1.call-update) | async-done | bytes 8388624 | tf_op jit(solution)/shard_map/all_gather | solution.py:311
  201.0 12.5 %own.1 = (f32[1024,1024]{1,0:T(8,128)}, bf16[1024,1024]{1,0:T(8,128)(2,1)}) custom-call(bf16[1024,1024]{1,0:T(8,128)(2,1)} %copy-done, bf16[8,1024,128]{2,1,0:T(8,128)(2,1)} %copy-done.1, bf16[32,128,1024]{2,1,0:T(8,128)(2,1)} %bitcast.30, bf16[32,128,1024]{2,1,0:T(8,128)(2,1)} %bitcast.31, bf16[32,128,1024]{2,1,0:T(8,128)(2,1)} %bitcast.32), custom_call_target="tpu_custom_call" | custom-call | tf_op jit(solution)/shard_map/own/pallas_call | solution.py:176
  213.5 3.7 %turn.1.out_w = bf16[1024,1024]{1,0:T(8,128)(2,1)} custom-call(bf16[32,128,1024]{2,1,0:T(8,128)(2,1)} %bitcast.33), custom_call_target="tpu_custom_call" | custom-call | tf_op jit(solution)/shard_map/turn/pallas_call | solution.py:213
  217.1 6.1 %all-to-all-done.2.hist_ref = bf16[8,1024,128]{2,1,0:T(8,128)(2,1)S(1)} async-done(((bf16[8,1024,128]{2,1,0:T(8,128)(2,1)}), bf16[8,1024,128]{2,1,0:T(8,128)(2,1)S(1)}, u32[]{:S(2)}, u32[]{:S(2)}) %all-to-all-start.2) | async-done | bytes 2097184 | tf_op jit(solution)/shard_map/all_to_all | solution.py:263
  224.6 7.8 %finish.1 = bf16[1024,1024]{1,0:T(8,128)(2,1)} custom-call(s32[16]{0:T(128)} %count_ref.1, bf16[8,1024,128]{2,1,0:T(8,128)(2,1)} %copy-done.6, f32[1024,1024]{1,0:T(8,128)} %get-tuple-element.43.own_ref, bf16[1024,1024]{1,0:T(8,128)(2,1)} %get-tuple-element.44.gate_ref, bf16[1024,1024]{1,0:T(8,128)(2,1)} %turn.1.out_w, bf16[1024,1024]{1,0:T(8,128)(2,1)} %rows_ref.3), custom_call_target="tpu_custom_call" | custom-call | tf_op jit(solution)/shard_map/finish/pallas_call | solution.py:244
  (57 shorter events, 12.9 us)
Async XLA Ops:
  7.9 1.4 copy-start.4
  9.3 0.7 copy-start.5
  12.1 9.2 %copy-start.7 = (bf16[1024,16]{0,1:T(8,128)(2,1)S(1)}, bf16[1024,16]{0,1:T(8,128)(2,1)}, u32[]{:S(2)}) copy-start(bf16[1024,16]{0,1:T(8,128)(2,1)} %param.16) | copy-start | bytes 98308
  12.1 9.2 %copy-start.8 = (bf16[4,1024]{1,0:T(4,128)(2,1)S(1)}, bf16[4,1024]{1,0:T(4,128)(2,1)}, u32[]{:S(2)}) copy-start(bf16[4,1024]{1,0:T(4,128)(2,1)} %param.17) | copy-start | bytes 24580
  12.1 60.6 %all-to-all-start = ((bf16[8,784,128]{2,1,0:T(8,128)(2,1)}), bf16[8,784,128]{2,1,0:T(8,128)(2,1)}, u32[]{:S(2)}, u32[]{:S(2)}) async-start(bf16[8,784,128]{2,1,0:T(8,128)(2,1)} %prep.1), calls=%async_computation | async-start | bytes 3211264 | tf_op jit(solution)/shard_map/all_to_all | solution.py:263
  21.3 135.7 %all-gather.4.cloned.1.call-start = ((), (), s32[]{:S(2)}) async-start(), calls=%async_computation.3 | async-start | bytes 8028160 | tf_op jit(solution)/shard_map/all_gather | solution.py:297
  21.4 8.3 %collective-permute-start.2 = (bf16[20,1024]{1,0:T(8,128)(2,1)S(1)}, bf16[20,1024]{1,0:T(8,128)(2,1)S(1)}, u32[]{:S(2)}, u32[]{:S(2)}) collective-permute-start(bf16[20,1024]{1,0:T(8,128)(2,1)S(1)} %pad_maximum_fusion.2), channel_id=1, source_target_pairs={{0,192},{192,0},{1,193},{193,1},{2,194},{194,2},{3,195},{195,3},{4... | collective-permute-start | bytes 122888 | tf_op jit(solution)/shard_map/ppermute | solution.py:289
  25.8 6.7 %collective-permute-start.1 = (bf16[20,1024]{1,0:T(8,128)(2,1)S(1)}, bf16[20,1024]{1,0:T(8,128)(2,1)S(1)}, u32[]{:S(2)}, u32[]{:S(2)}) collective-permute-start(bf16[20,1024]{1,0:T(8,128)(2,1)S(1)} %pad_maximum_fusion.2), channel_id=1, source_target_pairs={{0,128},{128,0},{1,129},{129,1},{2,130},{130,2},{3,131},{131,3},{4... | collective-permute-start | bytes 122888 | tf_op jit(solution)/shard_map/ppermute | solution.py:289
  27.7 5.2 %collective-permute-start = (bf16[20,1024]{1,0:T(8,128)(2,1)S(1)}, bf16[20,1024]{1,0:T(8,128)(2,1)S(1)}, u32[]{:S(2)}, u32[]{:S(2)}) collective-permute-start(bf16[20,1024]{1,0:T(8,128)(2,1)S(1)} %pad_maximum_fusion.2), channel_id=1, source_target_pairs={{0,64},{64,0},{1,65},{65,1},{2,66},{66,2},{3,67},{67,3},{4,68},{68... | collective-permute-start | bytes 122888 | tf_op jit(solution)/shard_map/ppermute | solution.py:289
  33.0 21.6 %collective-permute-start.3 = (bf16[32,1024]{1,0:T(8,128)(2,1)S(1)}, bf16[32,1024]{1,0:T(8,128)(2,1)S(1)}, u32[]{:S(2)}, u32[]{:S(2)}) collective-permute-start(bf16[32,1024]{1,0:T(8,128)(2,1)S(1)} %pad_maximum_fusion.1), channel_id=1, source_target_pairs={{0,1},{1,2},{2,3},{3,4},{4,5},{5,6},{6,7},{7,0},{8,9},{9,10},{10,1... | collective-permute-start | bytes 196616 | tf_op jit(solution)/shard_map/ppermute | solution.py:294
  34.5 28.5 %collective-permute-start.4 = (bf16[32,1024]{1,0:T(8,128)(2,1)S(1)}, bf16[32,1024]{1,0:T(8,128)(2,1)S(1)}, u32[]{:S(2)}, u32[]{:S(2)}) collective-permute-start(bf16[32,1024]{1,0:T(8,128)(2,1)S(1)} %pad_maximum_fusion.1), channel_id=1, source_target_pairs={{0,2},{1,3},{2,4},{3,5},{4,6},{5,7},{6,0},{7,1},{8,10},{9,11},{10,... | collective-permute-start | bytes 196616 | tf_op jit(solution)/shard_map/ppermute | solution.py:294
  36.6 31.7 %collective-permute-start.5 = (bf16[32,1024]{1,0:T(8,128)(2,1)S(1)}, bf16[32,1024]{1,0:T(8,128)(2,1)S(1)}, u32[]{:S(2)}, u32[]{:S(2)}) collective-permute-start(bf16[32,1024]{1,0:T(8,128)(2,1)S(1)} %pad_maximum_fusion.1), channel_id=1, source_target_pairs={{0,3},{1,4},{2,5},{3,6},{4,7},{5,0},{6,1},{7,2},{8,11},{9,12},{10,... | collective-permute-start | bytes 196616 | tf_op jit(solution)/shard_map/ppermute | solution.py:294
  39.0 33.7 %collective-permute-start.6 = (bf16[32,1024]{1,0:T(8,128)(2,1)S(1)}, bf16[32,1024]{1,0:T(8,128)(2,1)S(1)}, u32[]{:S(2)}, u32[]{:S(2)}) collective-permute-start(bf16[32,1024]{1,0:T(8,128)(2,1)S(1)} %pad_maximum_fusion.1), channel_id=1, source_target_pairs={{0,4},{1,5},{2,6},{3,7},{4,0},{5,1},{6,2},{7,3},{8,12},{9,13},{10,... | collective-permute-start | bytes 196616 | tf_op jit(solution)/shard_map/ppermute | solution.py:294
  41.0 31.6 %collective-permute-start.7 = (bf16[32,1024]{1,0:T(8,128)(2,1)S(1)}, bf16[32,1024]{1,0:T(8,128)(2,1)S(1)}, u32[]{:S(2)}, u32[]{:S(2)}) collective-permute-start(bf16[32,1024]{1,0:T(8,128)(2,1)S(1)} %pad_maximum_fusion.1), channel_id=1, source_target_pairs={{0,5},{1,6},{2,7},{3,0},{4,1},{5,2},{6,3},{7,4},{8,13},{9,14},{10,... | collective-permute-start | bytes 196616 | tf_op jit(solution)/shard_map/ppermute | solution.py:294
  54.6 18.1 %collective-permute-start.8 = (bf16[32,1024]{1,0:T(8,128)(2,1)S(1)}, bf16[32,1024]{1,0:T(8,128)(2,1)S(1)}, u32[]{:S(2)}, u32[]{:S(2)}) collective-permute-start(bf16[32,1024]{1,0:T(8,128)(2,1)S(1)} %pad_maximum_fusion.1), channel_id=1, source_target_pairs={{0,6},{1,7},{2,0},{3,1},{4,2},{5,3},{6,4},{7,5},{8,14},{9,15},{10,... | collective-permute-start | bytes 196616 | tf_op jit(solution)/shard_map/ppermute | solution.py:294
  63.0 9.7 %collective-permute-start.9 = (bf16[32,1024]{1,0:T(8,128)(2,1)S(1)}, bf16[32,1024]{1,0:T(8,128)(2,1)S(1)}, u32[]{:S(2)}, u32[]{:S(2)}) collective-permute-start(bf16[32,1024]{1,0:T(8,128)(2,1)S(1)} %pad_maximum_fusion.1), channel_id=1, source_target_pairs={{0,7},{1,0},{2,1},{3,2},{4,3},{5,4},{6,5},{7,6},{8,15},{9,8},{10,9... | collective-permute-start | bytes 196616 | tf_op jit(solution)/shard_map/ppermute | solution.py:294
  65.5 1.6 copy-start.2
  68.3 31.4 %copy-start = (bf16[1024,1024]{1,0:T(8,128)(2,1)}, bf16[1024,1024]{1,0:T(8,128)(2,1)S(1)}, u32[]{:S(2)}) copy-start(bf16[1024,1024]{1,0:T(8,128)(2,1)S(1)} %norm.1.rows_ref) | copy-start | bytes 6291460
  72.7 128.3 %all-gather.6.cloned.1.call-start = ((), (), s32[]{:S(2)}) async-start(), calls=%async_computation.4 | async-start | bytes 8650752 | tf_op jit(solution)/shard_map/all_gather | solution.py:311
  74.3 7.9 %collective-permute-start.12 = (bf16[128,1024]{1,0:T(8,128)(2,1)S(1)}, bf16[128,1024]{1,0:T(8,128)(2,1)S(1)}, u32[]{:S(2)}, u32[]{:S(2)}) collective-permute-start(bf16[128,1024]{1,0:T(8,128)(2,1)S(1)} %bitcast.35), channel_id=1, source_target_pairs={{0,24},{8,0},{16,8},{24,16},{1,25},{9,1},{17,9},{25,17},{2,26},{10... | collective-permute-start | bytes 786440 | tf_op jit(solution)/shard_map/ppermute | solution.py:302
  77.0 7.6 %collective-permute-start.11 = (bf16[128,1024]{1,0:T(8,128)(2,1)S(1)}, bf16[128,1024]{1,0:T(8,128)(2,1)S(1)}, u32[]{:S(2)}, u32[]{:S(2)}) collective-permute-start(bf16[128,1024]{1,0:T(8,128)(2,1)S(1)} %bitcast.36), channel_id=1, source_target_pairs={{0,16},{8,24},{16,0},{24,8},{1,17},{9,25},{17,1},{25,9},{2,18},{10... | collective-permute-start | bytes 786440 | tf_op jit(solution)/shard_map/ppermute | solution.py:302
  77.4 18.9 %collective-permute-start.10 = (bf16[128,1024]{1,0:T(8,128)(2,1)S(1)}, bf16[128,1024]{1,0:T(8,128)(2,1)S(1)}, u32[]{:S(2)}, u32[]{:S(2)}) collective-permute-start(bf16[128,1024]{1,0:T(8,128)(2,1)S(1)} %bitcast.37), channel_id=1, source_target_pairs={{0,8},{8,16},{16,24},{24,0},{1,9},{9,17},{17,25},{25,1},{2,10},{10... | collective-permute-start | bytes 786440 | tf_op jit(solution)/shard_map/ppermute | solution.py:302
  96.4 3.3 %collective-permute-start.13 = (bf16[512,1024]{1,0:T(8,128)(2,1)S(1)}, bf16[512,1024]{1,0:T(8,128)(2,1)}, u32[]{:S(2)}, u32[]{:S(2)}) collective-permute-start(bf16[512,1024]{1,0:T(8,128)(2,1)S(1)} %pad_maximum_fusion.mine_ref), channel_id=1, source_target_pairs={{0,32},{32,0},{1,33},{33,1},{2,34},{34,2},{3,35},{35,3},{4,36},{36... | collective-permute-start | bytes 3145736 | tf_op jit(solution)/shard_map/ppermute | solution.py:304
  103.7 1.3 copy-start.1
  105.1 51.9 %all-to-all-start.1 = ((bf16[8,1024,128]{2,1,0:T(8,128)(2,1)}), bf16[8,1024,128]{2,1,0:T(8,128)(2,1)S(1)}, u32[]{:S(2)}, u32[]{:S(2)}) async-start(bf16[8,1024,128]{2,1,0:T(8,128)(2,1)} %copy-done.1), calls=%async_computation.1 | async-start | bytes 4194304 | tf_op jit(solution)/shard_map/all_to_all | solution.py:263
  157.0 2.8 %copy-start.3 = (bf16[32,784,128]{2,1,0:T(8,128)(2,1)S(1)}, bf16[32,784,128]{2,1,0:T(8,128)(2,1)}, u32[]{:S(2)}) copy-start(bf16[32,784,128]{2,1,0:T(8,128)(2,1)} %all-gather.4.cloned.1.call-done.cache_ref) | copy-start | bytes 19267588
  166.8 56.5 %all-to-all-start.2 = ((bf16[8,1024,128]{2,1,0:T(8,128)(2,1)}), bf16[8,1024,128]{2,1,0:T(8,128)(2,1)S(1)}, u32[]{:S(2)}, u32[]{:S(2)}) async-start(bf16[8,1024,128]{2,1,0:T(8,128)(2,1)} %attend.1), calls=%async_computation.2 | async-start | bytes 4194304 | tf_op jit(solution)/shard_map/all_to_all | solution.py:263
  223.3 1.3 copy-start.6
Sparse Core Ops, SparseCore 0:
  72.9 71.4 all-gather.3
  146.9 54.0 all-gather.5

commit v5 on v4

--- a/solution.py
+++ b/solution.py
@@ -195,17 +195,11 @@
 
 def turn_kernel(gathered, out_ref):
     shares, rows, _ = gathered.shape
-    piece = rows // (NX * NZ)
-    to = lax.broadcasted_iota(jnp.int32, (rows, rows), 0)
-    at = lax.broadcasted_iota(jnp.int32, (rows, rows), 1)
-    plane, place, line = to // (NZ * piece), to // piece % NZ, to % piece
-    picked = (at == (place * NX + plane) * piece + line).astype(F32).astype(BF)
     span = rows // NX
     for i in range(shares):
-        turned = jnp.dot(picked, gathered[i], preferred_element_type=F32).astype(BF)
         for k in range(NX):
             first = (k * shares + i) * span
-            out_ref[first : first + span, :] = turned[k * span : (k + 1) * span, :]
+            out_ref[first : first + span, :] = gathered[i, k * span : (k + 1) * span, :]
 
 
 def turn(gathered):
@@ -283,23 +277,26 @@
     columns = weight_in.T
     share, out_share = columns.shape[0], weight_out.shape[0]
     normed = norm(candidates)
+    both = jnp.concatenate([columns, weight_out], axis=0)
     meta = jnp.zeros((META, HEAD), BF).at[0, :tiles].set(tile_user[:, 0].astype(BF))
-    caches = swap_z(prep(hist_kv[0], hist_len, block_mask, meta))
-    both = jnp.concatenate([columns, weight_out], axis=0)
+    caches = prep(hist_kv[0], hist_len, block_mask, meta)
+    spread = [both] + [lax.ppermute(both, "z", ring(NZ, k)) for k in range(1, NZ)]
+    caches, spread = lax.optimization_barrier((caches, spread))
+    caches = swap_z(caches)
+    spread = jnp.stack(spread)[(at_z - jnp.arange(NZ, dtype=jnp.int32)) % NZ]
+    in_rows = spread[:, :share].reshape(NZ * share, width)
+    out_rows = spread[:, share:].reshape(NZ * out_share, width)
+    both = jnp.concatenate([in_rows, out_rows], axis=0)
+    cut = in_rows.shape[0]
     sent = [lax.ppermute(both, "x", [(0, k), (k, 0)]) for k in range(1, NX)]
-    query_part = jnp.where(at_x == 0, columns, sent[0][:share] + sent[1][:share] + sent[2][:share])
-    out_part = jnp.concatenate([weight_out] + [piece[share:] for piece in sent], axis=0)
-    rest_part = jnp.where(at_x == 0, out_part, columns)
-    packed = jnp.concatenate([query_part, rest_part], axis=0)
-    spread = [packed] + [lax.ppermute(packed, "z", ring(NZ, k)) for k in range(1, NZ)]
-    spread, caches, normed = lax.optimization_barrier((spread, caches, normed))
+    query_z = jnp.where(at_x == 0, in_rows, sent[0][:cut] + sent[1][:cut] + sent[2][:cut])
+    out_rows = jnp.concatenate([out_rows] + [piece[cut:] for piece in sent], axis=0)
+    rest = jnp.where(at_x == 0, out_rows, in_rows)
+
+    parts = [query_z] + [lax.ppermute(query_z, "y", ring(NY, k)) for k in range(1, NY)]
+    parts, caches, normed = lax.optimization_barrier((parts, caches, normed))
     users = caches[:, 2 * HIST, :tiles].astype(jnp.int32)
     caches = lax.all_gather(caches, "y", axis=0, tiled=True)
-    spread = jnp.stack(spread)[(at_z - jnp.arange(NZ, dtype=jnp.int32)) % NZ]
-    query_z = spread[:, :share].reshape(NZ * share, width)
-    rest = spread[:, share : 2 * share].reshape(NZ * share, width)
-
-    parts = [query_z] + [lax.ppermute(query_z, "y", ring(NY, k)) for k in range(1, NY)]
     mine = jnp.concatenate(parts, axis=0)
     other = lax.ppermute(mine, "core", ring(NC, 1))
     at = (at_y - jnp.arange(NY, dtype=jnp.int32)) % NY

time: 240 us -> 235 us (0.979)
  waiting for transfers between devices: 126 us -> 120 us
  local copies, waits for them, and re-layouts: 10.5 us -> 13.4 us
  starting transfers between devices: 48.7 us -> 46 us
    ppermute x7, waiting for transfers between devices: 18.7 us -> 0.02 us  [shards(): lax.ppermute(both, 'z', ring(NZ, k))]
    all_gather x1, waiting for transfers between devices: 29.4 us -> 45 us  [shards(): gathered = lax.all_gather(rest, ('x', 'core', 'y'))]
    ppermute x3, waiting for transfers between devices: 18.3 us -> 4.53 us  [shards(): lax.ppermute(query_z, 'y', ring(NY, k))]
    ppermute x3, waiting for transfers between devices: 3.27 us -> 9.42 us  [shards(): sent = [lax.ppermute(both, 'x', [(0, k), (k, 0)]) for k in range(1, NX)]]
    all_to_all x3, starting transfers between devices: 17.6 us -> 14.7 us  [swap_z(): return lax.all_to_all(values, 'z', split_axis=0, concat_axis=0, tiled=True)]
    unnamed x25 -> x28, local copies, waits for them, and re-layouts: 9.14 us -> 11.8 us
    all_to_all x3, waiting for transfers between devices: 53.6 us -> 56.1 us  [swap_z(): return lax.all_to_all(values, 'z', split_axis=0, concat_axis=0, tiled=True)]
  transfers between devices with their start and end apart: 19 -> 19, of which waited for: 12 -> 9; matrix products, arithmetic and copies ran while one was open for 1% -> 3% of each run, Pallas kernels for 12% -> 13%
where the time goes in v5:
time: 235 us; the launch traced here: 234 us
  waiting for transfers between devices  120 us (51%)
  starting transfers between devices  46 us (20%)
  Pallas kernels  37.8 us (16%)
  between operations  14.3 us (6%)
  local copies, waits for them, and re-layouts  13.4 us (6%)
  other arithmetic  3.25 us (1%)
    all_to_all x3, waiting for transfers between devices, swap_z(): return lax.all_to_all(values, 'z', split_axis=0, concat_axis=0, tiled=True)  56.1 us
    all_gather x1, waiting for transfers between devices, shards(): gathered = lax.all_gather(rest, ('x', 'core', 'y'))  45 us
    ppermute x7, starting transfers between devices, shards(): lax.ppermute(both, 'z', ring(NZ, k))  17.3 us
    all_to_all x3, starting transfers between devices, swap_z(): return lax.all_to_all(values, 'z', split_axis=0, concat_axis=0, tiled=True)  14.7 us
    pallas_call x1, Pallas kernels, own(): pl.pallas_call(functools.partial(own_kernel, scale), grid=(steps,), in_sp...  12.5 us
    unnamed x28, local copies, waits for them, and re-layouts  11.8 us
    ppermute x3, waiting for transfers between devices, shards(): sent = [lax.ppermute(both, 'x', [(0, k), (k, 0)]) for k in range(1, NX)]  9.42 us
    ppermute x3, starting transfers between devices, shards(): sent = [lax.ppermute(both, 'x', [(0, k), (k, 0)]) for k in range(1, NX)]  8.23 us
  transfers between devices with their start and end apart: 19, of which 9 were waited for; matrix products, arithmetic and copies ran while one was open for 3% of the time, Pallas kernels for 13%

profile of v5, /device:TPU:1, one launch (start us, length us, event | category | flops | bytes accessed | tf_op | source)
XLA Modules:
  0.0 234.4 jit_solution(6713955090288520519)
XLA Ops:
  7.3 2.5 %collective-permute-start = (bf16[20,1024]{1,0:T(8,128)(2,1)S(1)}, bf16[20,1024]{1,0:T(8,128)(2,1)S(1)}, u32[]{:S(2)}, u32[]{:S(2)}) collective-permute-start(bf16[20,1024]{1,0:T(8,128)(2,1)S(1)} %pad_maximum_fusion.1), channel_id=1, source_target_pairs={{0,1},{1,2},{2,3},{3,4},{4,5},{5,6},{6,7},{7,0},{8,9},{9,10},{10,1... | collective-permute-start | bytes 122888 | tf_op jit(solution)/shard_map/ppermute | solution.py:283
  9.8 3.0 %collective-permute-start.1 = (bf16[20,1024]{1,0:T(8,128)(2,1)S(1)}, bf16[20,1024]{1,0:T(8,128)(2,1)S(1)}, u32[]{:S(2)}, u32[]{:S(2)}) collective-permute-start(bf16[20,1024]{1,0:T(8,128)(2,1)S(1)} %pad_maximum_fusion.1), channel_id=1, source_target_pairs={{0,2},{1,3},{2,4},{3,5},{4,6},{5,7},{6,0},{7,1},{8,10},{9,11},{10,... | collective-permute-start | bytes 122888 | tf_op jit(solution)/shard_map/ppermute | solution.py:283
  12.8 3.8 %collective-permute-start.2 = (bf16[20,1024]{1,0:T(8,128)(2,1)S(1)}, bf16[20,1024]{1,0:T(8,128)(2,1)S(1)}, u32[]{:S(2)}, u32[]{:S(2)}) collective-permute-start(bf16[20,1024]{1,0:T(8,128)(2,1)S(1)} %pad_maximum_fusion.1), channel_id=1, source_target_pairs={{0,3},{1,4},{2,5},{3,6},{4,7},{5,0},{6,1},{7,2},{8,11},{9,12},{10,... | collective-permute-start | bytes 122888 | tf_op jit(solution)/shard_map/ppermute | solution.py:283
  17.0 4.5 %collective-permute-start.4 = (bf16[20,1024]{1,0:T(8,128)(2,1)S(1)}, bf16[20,1024]{1,0:T(8,128)(2,1)S(1)}, u32[]{:S(2)}, u32[]{:S(2)}) collective-permute-start(bf16[20,1024]{1,0:T(8,128)(2,1)S(1)} %pad_maximum_fusion.1), channel_id=1, source_target_pairs={{0,5},{1,6},{2,7},{3,0},{4,1},{5,2},{6,3},{7,4},{8,13},{9,14},{10,... | collective-permute-start | bytes 122888 | tf_op jit(solution)/shard_map/ppermute | solution.py:283
  22.2 2.4 %collective-permute-start.5 = (bf16[20,1024]{1,0:T(8,128)(2,1)S(1)}, bf16[20,1024]{1,0:T(8,128)(2,1)S(1)}, u32[]{:S(2)}, u32[]{:S(2)}) collective-permute-start(bf16[20,1024]{1,0:T(8,128)(2,1)S(1)} %pad_maximum_fusion.1), channel_id=1, source_target_pairs={{0,6},{1,7},{2,0},{3,1},{4,2},{5,3},{6,4},{7,5},{8,14},{9,15},{10,... | collective-permute-start | bytes 122888 | tf_op jit(solution)/shard_map/ppermute | solution.py:283
  26.0 1.4 copy-done.4
  28.0 2.2 prep.1
  30.3 4.3 %all-to-all-start = ((bf16[8,784,128]{2,1,0:T(8,128)(2,1)}), bf16[8,784,128]{2,1,0:T(8,128)(2,1)}, u32[]{:S(2)}, u32[]{:S(2)}) async-start(bf16[8,784,128]{2,1,0:T(8,128)(2,1)} %prep.1), calls=%async_computation | async-start | bytes 3211264 | tf_op jit(solution)/shard_map/all_to_all | solution.py:257
  35.5 4.4 %collective-permute-start.9 = (bf16[160,1024]{1,0:T(8,128)(2,1)S(1)}, bf16[160,1024]{1,0:T(8,128)(2,1)S(1)}, u32[]{:S(2)}, u32[]{:S(2)}) collective-permute-start(bf16[160,1024]{1,0:T(8,128)(2,1)S(1)} %pad_maximum_fusion), channel_id=1, source_target_pairs={{0,192},{192,0},{1,193},{193,1},{2,194},{194,2},{3,195},{195,3},{4... | collective-permute-start | bytes 983048 | tf_op jit(solution)/shard_map/ppermute | solution.py:291
  39.8 1.9 collective-permute-start.8
  41.8 1.9 collective-permute-start.7
  43.7 1.5 collective-permute-done.9
  45.2 4.5 %collective-permute-done.8 = bf16[160,1024]{1,0:T(8,128)(2,1)S(1)} collective-permute-done((bf16[160,1024]{1,0:T(8,128)(2,1)S(1)}, bf16[160,1024]{1,0:T(8,128)(2,1)S(1)}, u32[]{:S(2)}, u32[]{:S(2)}) %collective-permute-start.8) | collective-permute-done | bytes 327712 | tf_op jit(solution)/shard_map/ppermute | solution.py:291
  49.7 3.4 %collective-permute-done.7 = bf16[160,1024]{1,0:T(8,128)(2,1)S(1)} collective-permute-done((bf16[160,1024]{1,0:T(8,128)(2,1)S(1)}, bf16[160,1024]{1,0:T(8,128)(2,1)S(1)}, u32[]{:S(2)}, u32[]{:S(2)}) %collective-permute-start.7) | collective-permute-done | bytes 327712 | tf_op jit(solution)/shard_map/ppermute | solution.py:291
  55.4 2.6 %collective-permute-start.11 = (bf16[128,1024]{1,0:T(8,128)(2,1)S(1)}, bf16[128,1024]{1,0:T(8,128)(2,1)S(1)}, u32[]{:S(2)}, u32[]{:S(2)}) collective-permute-start(bf16[128,1024]{1,0:T(8,128)(2,1)S(1)} %get-tuple-element.47), channel_id=1, source_target_pairs={{0,16},{8,24},{16,0},{24,8},{1,17},{9,25},{17,1},{25,9},{2,18},{10... | collective-permute-start | bytes 786440 | tf_op jit(solution)/shard_map/ppermute | solution.py:296
  59.1 1.6 copy-done.2
  61.9 4.5 %collective-permute-done.11 = bf16[128,1024]{1,0:T(8,128)(2,1)S(1)} collective-permute-done((bf16[128,1024]{1,0:T(8,128)(2,1)S(1)}, bf16[128,1024]{1,0:T(8,128)(2,1)S(1)}, u32[]{:S(2)}, u32[]{:S(2)}) %collective-permute-start.11) | collective-permute-done | bytes 262176 | tf_op jit(solution)/shard_map/ppermute | solution.py:296
  67.1 8.6 %all-to-all-done = bf16[8,784,128]{2,1,0:T(8,128)(2,1)} async-done(((bf16[8,784,128]{2,1,0:T(8,128)(2,1)}), bf16[8,784,128]{2,1,0:T(8,128)(2,1)}, u32[]{:S(2)}, u32[]{:S(2)}) %all-to-all-start) | async-done | bytes 1605664 | tf_op jit(solution)/shard_map/all_to_all | solution.py:257
  79.6 2.3 collective-permute-done.13.other_ref
  81.9 4.1 %query.1.query_ref = bf16[8,1024,128]{2,1,0:T(8,128)(2,1)S(1)} custom-call(s32[8]{0:T(128)S(1)} %pad_add_fusion.slot_ref, bf16[1024,1024]{1,0:T(8,128)(2,1)S(1)} %norm.1.rows_ref, bf16[512,1024]{1,0:T(8,128)(2,1)S(1)} %constant_dynamic-update-slice_fusion.mine_ref, bf16[512,1024]{1,0:T(8,128)(2,1)} %collective-permute-done.13.other_ref), custom_call_target="tpu_custom_call" | custom-call | tf_op jit(solution)/shard_map/query/pallas_call | solution.py:105
  86.0 1.3 copy-done.1
  87.4 3.6 %all-to-all-start.1 = ((bf16[8,1024,128]{2,1,0:T(8,128)(2,1)}), bf16[8,1024,128]{2,1,0:T(8,128)(2,1)S(1)}, u32[]{:S(2)}, u32[]{:S(2)}) async-start(bf16[8,1024,128]{2,1,0:T(8,128)(2,1)} %copy-done.1), calls=%async_computation.1 | async-start | bytes 4194304 | tf_op jit(solution)/shard_map/all_to_all | solution.py:257
  91.7 47.5 %all-to-all-done.1.query_ref = bf16[8,1024,128]{2,1,0:T(8,128)(2,1)S(1)} async-done(((bf16[8,1024,128]{2,1,0:T(8,128)(2,1)}), bf16[8,1024,128]{2,1,0:T(8,128)(2,1)S(1)}, u32[]{:S(2)}, u32[]{:S(2)}) %all-to-all-start.1) | async-done | bytes 2097184 | tf_op jit(solution)/shard_map/all_to_all | solution.py:257
  139.2 2.2 all-gather.4.cloned.1.call-done.cache_ref
  141.4 2.8 %copy-done.3 = bf16[32,784,128]{2,1,0:T(8,128)(2,1)S(1)} copy-done((bf16[32,784,128]{2,1,0:T(8,128)(2,1)S(1)}, bf16[32,784,128]{2,1,0:T(8,128)(2,1)}, u32[]{:S(2)}) %copy-start.3) | copy-done | bytes 6422552
  144.2 7.0 %attend.1 = bf16[8,1024,128]{2,1,0:T(8,128)(2,1)} custom-call(s32[8,16]{1,0:T(8,128)S(1)} %bitcast.28, bf16[8,1024,128]{2,1,0:T(8,128)(2,1)S(1)} %all-to-all-done.1.query_ref, bf16[32,784,128]{2,1,0:T(8,128)(2,1)S(1)} %copy-done.3), custom_call_target="tpu_custom_call" | custom-call | tf_op jit(solution)/shard_map/attend/pallas_call | solution.py:140
  151.2 6.8 %all-to-all-start.2 = ((bf16[8,1024,128]{2,1,0:T(8,128)(2,1)}), bf16[8,1024,128]{2,1,0:T(8,128)(2,1)S(1)}, u32[]{:S(2)}, u32[]{:S(2)}) async-start(bf16[8,1024,128]{2,1,0:T(8,128)(2,1)} %attend.1), calls=%async_computation.2 | async-start | bytes 4194304 | tf_op jit(solution)/shard_map/all_to_all | solution.py:257
  158.0 45.0 %all-gather.6.cloned.1.call-done = bf16[4096,1024]{1,0:T(8,128)(2,1)} async-done(((bf16[128,1024]{1,0:T(8,128)(2,1)}), bf16[4096,1024]{1,0:T(8,128)(2,1)}) %all-gather.6.cloned.1.call-update) | async-done | bytes 8388624 | tf_op jit(solution)/shard_map/all_gather | solution.py:308
  203.0 12.5 %own.1 = (f32[1024,1024]{1,0:T(8,128)}, bf16[1024,1024]{1,0:T(8,128)(2,1)}) custom-call(bf16[1024,1024]{1,0:T(8,128)(2,1)} %copy-done, bf16[8,1024,128]{2,1,0:T(8,128)(2,1)} %copy-done.1, bf16[32,128,1024]{2,1,0:T(8,128)(2,1)} %bitcast.29, bf16[32,128,1024]{2,1,0:T(8,128)(2,1)} %bitcast.30, bf16[32,128,1024]{2,1,0:T(8,128)(2,1)} %bitcast.31), custom_call_target="tpu_custom_call" | custom-call | tf_op jit(solution)/shard_map/own/pallas_call | solution.py:176
  215.5 3.0 %turn.1.out_w = bf16[1024,1024]{1,0:T(8,128)(2,1)} custom-call(bf16[32,128,1024]{2,1,0:T(8,128)(2,1)} %bitcast.32), custom_call_target="tpu_custom_call" | custom-call | tf_op jit(solution)/shard_map/turn/pallas_call | solution.py:207
  218.5 1.3 copy-done.6
  219.9 7.7 %finish.1 = bf16[1024,1024]{1,0:T(8,128)(2,1)} custom-call(s32[16]{0:T(128)} %count_ref.1, bf16[8,1024,128]{2,1,0:T(8,128)(2,1)} %copy-done.6, f32[1024,1024]{1,0:T(8,128)} %get-tuple-element.53.own_ref, bf16[1024,1024]{1,0:T(8,128)(2,1)} %get-tuple-element.54.gate_ref, bf16[1024,1024]{1,0:T(8,128)(2,1)} %turn.1.out_w, bf16[1024,1024]{1,0:T(8,128)(2,1)} %rows_ref.3), custom_call_target="tpu_custom_call" | custom-call | tf_op jit(solution)/shard_map/finish/pallas_call | solution.py:238
  (62 shorter events, 13.9 us)
Async XLA Ops:
  7.3 14.8 %collective-permute-start = (bf16[20,1024]{1,0:T(8,128)(2,1)S(1)}, bf16[20,1024]{1,0:T(8,128)(2,1)S(1)}, u32[]{:S(2)}, u32[]{:S(2)}) collective-permute-start(bf16[20,1024]{1,0:T(8,128)(2,1)S(1)} %pad_maximum_fusion.1), channel_id=1, source_target_pairs={{0,1},{1,2},{2,3},{3,4},{4,5},{5,6},{6,7},{7,0},{8,9},{9,10},{10,1... | collective-permute-start | bytes 122888 | tf_op jit(solution)/shard_map/ppermute | solution.py:283
  9.8 14.7 %collective-permute-start.1 = (bf16[20,1024]{1,0:T(8,128)(2,1)S(1)}, bf16[20,1024]{1,0:T(8,128)(2,1)S(1)}, u32[]{:S(2)}, u32[]{:S(2)}) collective-permute-start(bf16[20,1024]{1,0:T(8,128)(2,1)S(1)} %pad_maximum_fusion.1), channel_id=1, source_target_pairs={{0,2},{1,3},{2,4},{3,5},{4,6},{5,7},{6,0},{7,1},{8,10},{9,11},{10,... | collective-permute-start | bytes 122888 | tf_op jit(solution)/shard_map/ppermute | solution.py:283
  12.8 17.4 %collective-permute-start.2 = (bf16[20,1024]{1,0:T(8,128)(2,1)S(1)}, bf16[20,1024]{1,0:T(8,128)(2,1)S(1)}, u32[]{:S(2)}, u32[]{:S(2)}) collective-permute-start(bf16[20,1024]{1,0:T(8,128)(2,1)S(1)} %pad_maximum_fusion.1), channel_id=1, source_target_pairs={{0,3},{1,4},{2,5},{3,6},{4,7},{5,0},{6,1},{7,2},{8,11},{9,12},{10,... | collective-permute-start | bytes 122888 | tf_op jit(solution)/shard_map/ppermute | solution.py:283
  16.6 13.7 %collective-permute-start.3 = (bf16[20,1024]{1,0:T(8,128)(2,1)S(1)}, bf16[20,1024]{1,0:T(8,128)(2,1)S(1)}, u32[]{:S(2)}, u32[]{:S(2)}) collective-permute-start(bf16[20,1024]{1,0:T(8,128)(2,1)S(1)} %pad_maximum_fusion.1), channel_id=1, source_target_pairs={{0,4},{1,5},{2,6},{3,7},{4,0},{5,1},{6,2},{7,3},{8,12},{9,13},{10,... | collective-permute-start | bytes 122888 | tf_op jit(solution)/shard_map/ppermute | solution.py:283
  17.0 13.2 %collective-permute-start.4 = (bf16[20,1024]{1,0:T(8,128)(2,1)S(1)}, bf16[20,1024]{1,0:T(8,128)(2,1)S(1)}, u32[]{:S(2)}, u32[]{:S(2)}) collective-permute-start(bf16[20,1024]{1,0:T(8,128)(2,1)S(1)} %pad_maximum_fusion.1), channel_id=1, source_target_pairs={{0,5},{1,6},{2,7},{3,0},{4,1},{5,2},{6,3},{7,4},{8,13},{9,14},{10,... | collective-permute-start | bytes 122888 | tf_op jit(solution)/shard_map/ppermute | solution.py:283
  22.2 8.1 %collective-permute-start.5 = (bf16[20,1024]{1,0:T(8,128)(2,1)S(1)}, bf16[20,1024]{1,0:T(8,128)(2,1)S(1)}, u32[]{:S(2)}, u32[]{:S(2)}) collective-permute-start(bf16[20,1024]{1,0:T(8,128)(2,1)S(1)} %pad_maximum_fusion.1), channel_id=1, source_target_pairs={{0,6},{1,7},{2,0},{3,1},{4,2},{5,3},{6,4},{7,5},{8,14},{9,15},{10,... | collective-permute-start | bytes 122888 | tf_op jit(solution)/shard_map/ppermute | solution.py:283
  24.5 5.7 %collective-permute-start.6 = (bf16[20,1024]{1,0:T(8,128)(2,1)S(1)}, bf16[20,1024]{1,0:T(8,128)(2,1)S(1)}, u32[]{:S(2)}, u32[]{:S(2)}) collective-permute-start(bf16[20,1024]{1,0:T(8,128)(2,1)S(1)} %pad_maximum_fusion.1), channel_id=1, source_target_pairs={{0,7},{1,0},{2,1},{3,2},{4,3},{5,4},{6,5},{7,6},{8,15},{9,8},{10,9... | collective-permute-start | bytes 122888 | tf_op jit(solution)/shard_map/ppermute | solution.py:283
  26.0 1.4 copy-start.4
  27.4 0.7 copy-start.5
  30.3 45.4 %all-to-all-start = ((bf16[8,784,128]{2,1,0:T(8,128)(2,1)}), bf16[8,784,128]{2,1,0:T(8,128)(2,1)}, u32[]{:S(2)}, u32[]{:S(2)}) async-start(bf16[8,784,128]{2,1,0:T(8,128)(2,1)} %prep.1), calls=%async_computation | async-start | bytes 3211264 | tf_op jit(solution)/shard_map/all_to_all | solution.py:257
  34.6 106.8 %all-gather.4.cloned.1.call-start = ((), (), s32[]{:S(2)}) async-start(), calls=%async_computation.3 | async-start | bytes 8028160 | tf_op jit(solution)/shard_map/all_gather | solution.py:299
  35.5 9.8 %collective-permute-start.9 = (bf16[160,1024]{1,0:T(8,128)(2,1)S(1)}, bf16[160,1024]{1,0:T(8,128)(2,1)S(1)}, u32[]{:S(2)}, u32[]{:S(2)}) collective-permute-start(bf16[160,1024]{1,0:T(8,128)(2,1)S(1)} %pad_maximum_fusion), channel_id=1, source_target_pairs={{0,192},{192,0},{1,193},{193,1},{2,194},{194,2},{3,195},{195,3},{4... | collective-permute-start | bytes 983048 | tf_op jit(solution)/shard_map/ppermute | solution.py:291
  39.8 9.9 %collective-permute-start.8 = (bf16[160,1024]{1,0:T(8,128)(2,1)S(1)}, bf16[160,1024]{1,0:T(8,128)(2,1)S(1)}, u32[]{:S(2)}, u32[]{:S(2)}) collective-permute-start(bf16[160,1024]{1,0:T(8,128)(2,1)S(1)} %pad_maximum_fusion), channel_id=1, source_target_pairs={{0,128},{128,0},{1,129},{129,1},{2,130},{130,2},{3,131},{131,3},{4... | collective-permute-start | bytes 983048 | tf_op jit(solution)/shard_map/ppermute | solution.py:291
  41.8 11.4 %collective-permute-start.7 = (bf16[160,1024]{1,0:T(8,128)(2,1)S(1)}, bf16[160,1024]{1,0:T(8,128)(2,1)S(1)}, u32[]{:S(2)}, u32[]{:S(2)}) collective-permute-start(bf16[160,1024]{1,0:T(8,128)(2,1)S(1)} %pad_maximum_fusion), channel_id=1, source_target_pairs={{0,64},{64,0},{1,65},{65,1},{2,66},{66,2},{3,67},{67,3},{4,68},{68... | collective-permute-start | bytes 983048 | tf_op jit(solution)/shard_map/ppermute | solution.py:291
  54.1 7.8 %collective-permute-start.10 = (bf16[128,1024]{1,0:T(8,128)(2,1)S(1)}, bf16[128,1024]{1,0:T(8,128)(2,1)S(1)}, u32[]{:S(2)}, u32[]{:S(2)}) collective-permute-start(bf16[128,1024]{1,0:T(8,128)(2,1)S(1)} %get-tuple-element.47), channel_id=1, source_target_pairs={{0,8},{8,16},{16,24},{24,0},{1,9},{9,17},{17,25},{25,1},{2,10},{10... | collective-permute-start | bytes 786440 | tf_op jit(solution)/shard_map/ppermute | solution.py:296
  55.4 11.1 %collective-permute-start.11 = (bf16[128,1024]{1,0:T(8,128)(2,1)S(1)}, bf16[128,1024]{1,0:T(8,128)(2,1)S(1)}, u32[]{:S(2)}, u32[]{:S(2)}) collective-permute-start(bf16[128,1024]{1,0:T(8,128)(2,1)S(1)} %get-tuple-element.47), channel_id=1, source_target_pairs={{0,16},{8,24},{16,0},{24,8},{1,17},{9,25},{17,1},{25,9},{2,18},{10... | collective-permute-start | bytes 786440 | tf_op jit(solution)/shard_map/ppermute | solution.py:296
  58.0 9.1 %collective-permute-start.12 = (bf16[128,1024]{1,0:T(8,128)(2,1)S(1)}, bf16[128,1024]{1,0:T(8,128)(2,1)}, u32[]{:S(2)}, u32[]{:S(2)}) collective-permute-start(bf16[128,1024]{1,0:T(8,128)(2,1)S(1)} %get-tuple-element.47), channel_id=1, source_target_pairs={{0,24},{8,0},{16,8},{24,16},{1,25},{9,1},{17,9},{25,17},{2,26},{10... | collective-permute-start | bytes 786440 | tf_op jit(solution)/shard_map/ppermute | solution.py:296
  59.1 1.6 copy-start.2
  61.9 24.1 %copy-start = (bf16[1024,1024]{1,0:T(8,128)(2,1)}, bf16[1024,1024]{1,0:T(8,128)(2,1)S(1)}, u32[]{:S(2)}) copy-start(bf16[1024,1024]{1,0:T(8,128)(2,1)S(1)} %norm.1.rows_ref) | copy-start | bytes 6291460
  61.9 4.5 %copy-start.7 = (bf16[128,1024]{1,0:T(8,128)(2,1)}, bf16[128,1024]{1,0:T(8,128)(2,1)S(1)}, u32[]{:S(2)}) copy-start(bf16[128,1024]{1,0:T(8,128)(2,1)S(1)} %collective-permute-done.10) | copy-start | bytes 786436
  66.4 0.7 copy-start.8
  75.7 127.3 %all-gather.6.cloned.1.call-start = ((), (), s32[]{:S(2)}) async-start(), calls=%async_computation.4 | async-start | bytes 8650752 | tf_op jit(solution)/shard_map/all_gather | solution.py:308
  78.7 3.2 %collective-permute-start.13 = (bf16[512,1024]{1,0:T(8,128)(2,1)S(1)}, bf16[512,1024]{1,0:T(8,128)(2,1)}, u32[]{:S(2)}, u32[]{:S(2)}) collective-permute-start(bf16[512,1024]{1,0:T(8,128)(2,1)S(1)} %constant_dynamic-update-slice_fusion.mine_ref), channel_id=1, source_target_pairs={{0,32},{32,0},{1,33},{33,1},{2,34},{34,2},{3,35},{35,3},{4,36},{36... | collective-permute-start | bytes 3145736 | tf_op jit(solution)/shard_map/ppermute | solution.py:301
  86.0 1.3 copy-start.1
  87.4 51.9 %all-to-all-start.1 = ((bf16[8,1024,128]{2,1,0:T(8,128)(2,1)}), bf16[8,1024,128]{2,1,0:T(8,128)(2,1)S(1)}, u32[]{:S(2)}, u32[]{:S(2)}) async-start(bf16[8,1024,128]{2,1,0:T(8,128)(2,1)} %copy-done.1), calls=%async_computation.1 | async-start | bytes 4194304 | tf_op jit(solution)/shard_map/all_to_all | solution.py:257
  141.4 2.8 %copy-start.3 = (bf16[32,784,128]{2,1,0:T(8,128)(2,1)S(1)}, bf16[32,784,128]{2,1,0:T(8,128)(2,1)}, u32[]{:S(2)}) copy-start(bf16[32,784,128]{2,1,0:T(8,128)(2,1)} %all-gather.4.cloned.1.call-done.cache_ref) | copy-start | bytes 19267588
  151.2 67.3 %all-to-all-start.2 = ((bf16[8,1024,128]{2,1,0:T(8,128)(2,1)}), bf16[8,1024,128]{2,1,0:T(8,128)(2,1)S(1)}, u32[]{:S(2)}, u32[]{:S(2)}) async-start(bf16[8,1024,128]{2,1,0:T(8,128)(2,1)} %attend.1), calls=%async_computation.2 | async-start | bytes 4194304 | tf_op jit(solution)/shard_map/all_to_all | solution.py:257
  218.5 1.3 copy-start.6
Sparse Core Ops, SparseCore 0:
  75.9 65.4 all-gather.3
  143.9 59.0 all-gather.5
